TPU v7x, 128 devices: a whole 4x4x4 slice. The times are simulated.
128 devices in a mesh: ctx: 16 (over z, x), tp: 8 (over y, core).
Axes of the slice: x: 4, y: 4, z: 4, core: 2. Of those that a mesh axis runs over, the one named last changes fastest.
Arguments:
- qkv: bfloat16 [3, 8192, 4096], P(None, ('ctx', 'tp')), may hold values from -6 to 6
- residues: float32 [4096, 16], P('tp'), may hold values from -2 to 2
- spans: float32 [4096, 16], P('tp'), may hold values from 20 to 40960
- skip: float32 [4096], P('tp'), may hold values from -3 to 3
Outputs:
- gated: bfloat16 [4096, 8192], P('tp', 'ctx')
All inputs are finite; a program needn't handle non-finite values.
Results may differ from a plain program's by a relative error of at most 0.00205.
Values may be sent and summed in bfloat16 or wider, within the bound.
No kernel may reach another device: no remote copies, remote signals or barrier semaphores. Data moves between devices by JAX's collectives and lax.ppermute only.
A program may use at most 192 MiB of HBM per device.

v0:
```python
import math

import jax
import jax.numpy as jnp
from jax import lax
from jax.sharding import PartitionSpec as P

two_pi = 2.0 * math.pi


def swapped(value, axis, stride):
    return lax.ppermute(value, axis, [(i, i ^ 1 << stride) for i in range(lax.axis_size(axis))])


def product(form, left, right):
    return jnp.einsum(
        form, left, right, precision=lax.Precision.HIGHEST, preferred_element_type=jnp.float32
    )


def cmul(left_real, left_imag, right_real, right_imag):
    return (
        left_real * right_real - left_imag * right_imag,
        left_real * right_imag + left_imag * right_real,
    )


def split_factor(count):
    chosen = 1
    for factor in range(1, math.isqrt(count) + 1):
        if count % factor == 0:
            chosen = factor
    return chosen


def dft_tables(count, direction):
    indices = jnp.arange(count, dtype=jnp.int32)
    angles = two_pi / count * (indices[:, None] * indices[None, :] % count).astype(jnp.float32)
    return (jnp.cos(angles), direction * jnp.sin(angles))


def twiddle_table(rows_count, cols_count, modulus, direction):
    rows_index = jnp.arange(rows_count, dtype=jnp.int32)
    cols_index = jnp.arange(cols_count, dtype=jnp.int32)
    angles = (
        two_pi / modulus * (rows_index[:, None] * cols_index[None, :] % modulus).astype(jnp.float32)
    )
    return (jnp.cos(angles), direction * jnp.sin(angles))


def local_forward(real_part, imag_part):
    leading = real_part.shape[:-1]
    count = real_part.shape[-1]
    first = split_factor(count)
    second = count // first
    real_part = real_part.reshape(leading + (first, second))
    imag_part = imag_part.reshape(leading + (first, second))
    cos_first, sin_first = dft_tables(first, -1.0)
    mid_real = product("...xj,xk->...kj", real_part, cos_first) - product(
        "...xj,xk->...kj", imag_part, sin_first
    )
    mid_imag = product("...xj,xk->...kj", real_part, sin_first) + product(
        "...xj,xk->...kj", imag_part, cos_first
    )
    cos_twist, sin_twist = twiddle_table(first, second, count, -1.0)
    mid_real, mid_imag = cmul(mid_real, mid_imag, cos_twist, sin_twist)
    cos_second, sin_second = dft_tables(second, -1.0)
    out_real = product("...kj,jl->...kl", mid_real, cos_second) - product(
        "...kj,jl->...kl", mid_imag, sin_second
    )
    out_imag = product("...kj,jl->...kl", mid_real, sin_second) + product(
        "...kj,jl->...kl", mid_imag, cos_second
    )
    return (out_real.reshape(leading + (count,)), out_imag.reshape(leading + (count,)))


def local_inverse(real_part, imag_part):
    leading = real_part.shape[:-1]
    count = real_part.shape[-1]
    first = split_factor(count)
    second = count // first
    real_part = real_part.reshape(leading + (first, second))
    imag_part = imag_part.reshape(leading + (first, second))
    cos_second, sin_second = dft_tables(second, 1.0)
    mid_real = product("...kl,lj->...kj", real_part, cos_second) - product(
        "...kl,lj->...kj", imag_part, sin_second
    )
    mid_imag = product("...kl,lj->...kj", real_part, sin_second) + product(
        "...kl,lj->...kj", imag_part, cos_second
    )
    cos_twist, sin_twist = twiddle_table(first, second, count, 1.0)
    mid_real, mid_imag = cmul(mid_real, mid_imag, cos_twist, sin_twist)
    cos_first, sin_first = dft_tables(first, 1.0)
    out_real = product("...kj,kx->...xj", mid_real, cos_first) - product(
        "...kj,kx->...xj", mid_imag, sin_first
    )
    out_imag = product("...kj,kx->...xj", mid_real, sin_first) + product(
        "...kj,kx->...xj", mid_imag, cos_first
    )
    scale_factor = 1.0 / count
    return (
        (out_real * scale_factor).reshape(leading + (count,)),
        (out_imag * scale_factor).reshape(leading + (count,)),
    )


def forward_butterfly(signal, my_index, devices):
    bit_count = devices.bit_length() - 1
    shift_angle = -two_pi * my_index.astype(jnp.float32) / (2 * devices)
    real_part = jnp.stack([signal, signal * jnp.cos(shift_angle)], 1)
    imag_part = jnp.stack([jnp.zeros_like(signal), signal * jnp.sin(shift_angle)], 1)
    states = jnp.stack([real_part, imag_part])
    for section_bit in reversed(range(bit_count)):
        half_span = 1 << section_bit
        partner = swapped(states, "ctx", section_bit)
        upper_bit = my_index >> section_bit & 1
        phase_angle = -two_pi * (my_index % half_span).astype(jnp.float32) / (2 * half_span)
        rotated = cmul(
            partner[0] - states[0],
            partner[1] - states[1],
            jnp.cos(phase_angle),
            jnp.sin(phase_angle),
        )
        states = jnp.where(upper_bit == 1, jnp.stack(rotated), states + partner)
    reversal = jnp.zeros((), jnp.int32)
    for section_bit in range(bit_count):
        reversal = reversal + ((my_index >> section_bit & 1) << bit_count - 1 - section_bit)
    return (states[0], states[1], 2 * reversal + jnp.arange(2, dtype=jnp.int32))


def inverse_butterfly(real_part, imag_part, my_index, devices):
    bit_count = devices.bit_length() - 1
    states = jnp.stack([real_part, imag_part])
    for section_bit in range(bit_count):
        half_span = 1 << section_bit
        partner = swapped(states, "ctx", section_bit)
        upper_bit = my_index >> section_bit & 1
        phase_angle = two_pi * (my_index % half_span).astype(jnp.float32) / (2 * half_span)
        cosine_value = jnp.cos(phase_angle)
        sine_value = jnp.sin(phase_angle)
        turned_self = jnp.stack(cmul(states[0], states[1], cosine_value, sine_value))
        turned_partner = jnp.stack(cmul(partner[0], partner[1], cosine_value, sine_value))
        states = jnp.where(upper_bit == 1, partner - turned_self, states + turned_partner)
    shift_angle = two_pi * my_index.astype(jnp.float32) / (2 * devices)
    summed = (
        states[0][:, 0]
        + states[0][:, 1] * jnp.cos(shift_angle)
        - states[1][:, 1] * jnp.sin(shift_angle)
    )
    return summed * (1.0 / (2 * devices))


def per_device(qkv, residues, spans, skip):
    gathered = lax.all_to_all(qkv, "tp", split_axis=2, concat_axis=1, tiled=True)
    queries = gathered[0].astype(jnp.float32).T
    drive = (gathered[1].astype(jnp.float32) * gathered[2].astype(jnp.float32)).T
    channel_count, length = drive.shape
    devices = lax.axis_size("ctx")
    my_index = lax.axis_index("ctx")
    seq_total = devices * length
    period = 2 * seq_total
    positions = jnp.arange(length, dtype=jnp.int32)
    rates = 1.0 / spans
    scaled = residues * jnp.sqrt(rates)
    times_now = (my_index * length + positions).astype(jnp.float32)
    filt = jnp.sum(
        scaled[:, :, None] * jnp.exp(-rates[:, :, None] * times_now[None, None, :]), axis=1
    )
    signal = jnp.concatenate([drive, filt], 0)
    spec_real, spec_imag, coarse_freq = forward_butterfly(signal, my_index, devices)
    twist_angle = (
        two_pi / period * (coarse_freq[:, None] * positions[None, :] % period).astype(jnp.float32)
    )
    twist_cos = jnp.cos(twist_angle)
    twist_sin = jnp.sin(twist_angle)
    spec_real, spec_imag = cmul(spec_real, spec_imag, twist_cos, -twist_sin)
    spec_real, spec_imag = local_forward(spec_real, spec_imag)
    filt_real = spec_real[channel_count:]
    filt_imag = spec_imag[channel_count:]
    prod_real, prod_imag = cmul(
        spec_real[:channel_count], spec_imag[:channel_count], filt_real, filt_imag
    )
    prod_real, prod_imag = local_inverse(prod_real, prod_imag)
    prod_real, prod_imag = cmul(prod_real, prod_imag, twist_cos, twist_sin)
    conv = inverse_butterfly(prod_real, prod_imag, my_index, devices)
    return (queries * (conv + skip[:, None] * drive)).astype(jnp.bfloat16)


def solution(mesh):
    return jax.shard_map(
        per_device,
        mesh=mesh,
        in_specs=(P(None, ("ctx", "tp"), None), P("tp", None), P("tp", None), P("tp")),
        out_specs=P("tp", "ctx"),
        check_vma=False,
    )
```

profile of v0, /device:TPU:0, one launch (start us, length us, event | category | flops | bytes accessed | tf_op | source)
XLA Modules:
  0.0 1369.9 jit_solution(11235483929386822828)
XLA Ops:
  0.0 6.4 copy.115
  6.4 7.3 reshape.334
  18.8 7.7 multiply_reduce_fusion
  26.4 13.4 all-to-all-done
  66.8 180.4 %collective-permute-done = f32[2,1024,2,512]{3,1,2,0:T(8,128)} collective-permute-done((f32[2,1024,2,512]{3,1,2,0:T(8,128)}, f32[2,1024,2,512]{3,1,2,0:T(8,128)}, u32[]{:S(2)}, u32[]{:S(2)}) %collective-permute-start) | collective-permute-done | bytes 8388640 | tf_op jit(solution)/shard_map/ppermute | solution.py:12
  247.2 5.6 subtract_bitcast_fusion.1
  252.9 10.3 maximum_select_fusion
  265.1 180.3 %collective-permute-done.1 = f32[2,1024,2,512]{3,1,2,0:T(8,128)} collective-permute-done((f32[2,1024,2,512]{3,1,2,0:T(8,128)}, f32[2,1024,2,512]{3,1,2,0:T(8,128)}, u32[]{:S(2)}, u32[]{:S(2)}) %collective-permute-start.1) | collective-permute-done | bytes 8388640 | tf_op jit(solution)/shard_map/ppermute | solution.py:12
  445.4 9.4 multiply_subtract_fusion.3
  454.8 18.1 %maximum_select_fusion.1 = f32[2,1024,2,512]{3,1,2,0:T(8,128)} fusion(f32[1,1024,2,512]{3,1,2,0:T(8,128)} %get-tuple-element.13, f32[1,1024,2,512]{3,1,2,0:T(8,128)} %get-tuple-element.12, f32[2,1024,2,512]{3,1,2,0:T(8,128)} %collective-permute-done.1, pred[]{:T(512)S(6)} %eq.37, f32[2,1024,2,512]{3,1,2,0:T(8,128)} %collective-permute-done, ...), kind=kLoop, calls=%fused_computation.3 | loop fusion | flops 14680064 | bytes 50331648 | tf_op jit(solution)/shard_map/jit(_where)/select_n | solution.py:124
  476.1 179.1 %collective-permute-done.2 = f32[2,1024,2,512]{3,1,2,0:T(8,128)} collective-permute-done((f32[2,1024,2,512]{3,1,2,0:T(8,128)}, f32[2,1024,2,512]{3,1,2,0:T(8,128)}, u32[]{:S(2)}, u32[]{:S(2)}) %collective-permute-start.2) | collective-permute-done | bytes 8388640 | tf_op jit(solution)/shard_map/ppermute | solution.py:12
  655.2 7.1 multiply_subtract_fusion.2
  663.4 7.4 maximum_select_fusion.2
  672.9 177.8 %collective-permute-done.3 = f32[2,1024,2,512]{3,1,2,0:T(8,128)} collective-permute-done((f32[2,1024,2,512]{3,1,2,0:T(8,128)}, f32[2,1024,2,512]{3,1,2,0:T(8,128)}, u32[]{:S(2)}, u32[]{:S(2)}) %collective-permute-start.3) | collective-permute-done | bytes 8388640 | tf_op jit(solution)/shard_map/ppermute | solution.py:12
  850.7 6.9 multiply_subtract_fusion.1
  857.6 7.5 maximum_select_fusion.3
  869.3 5.4 copy.123
  874.8 5.4 copy.124
  884.4 5.8 fusion.13
  890.1 5.8 fusion.15
  895.9 6.0 fusion.22
  902.0 7.3 subtract_bitcast_fusion
  909.2 8.0 fusion.5
  917.3 8.3 fusion.7
  925.6 8.2 fusion.28
  933.7 8.4 fusion.31
  981.4 86.8 %collective-permute-done.4 = f32[2,512,2,512]{3,1,2,0:T(8,128)S(1)} collective-permute-done((f32[2,512,2,512]{3,1,2,0:T(8,128)S(1)}, f32[2,512,2,512]{3,1,2,0:T(8,128)S(1)}, u32[]{:S(2)}, u32[]{:S(2)}) %collective-permute-start.4) | collective-permute-done | bytes 4194336 | tf_op jit(solution)/shard_map/ppermute | solution.py:12
  1080.1 83.5 %collective-permute-done.5 = f32[2,512,2,512]{3,1,2,0:T(8,128)} collective-permute-done((f32[2,512,2,512]{3,1,2,0:T(8,128)}, f32[2,512,2,512]{3,1,2,0:T(8,128)}, u32[]{:S(2)}, u32[]{:S(2)}) %collective-permute-start.5) | collective-permute-done | bytes 4194336 | tf_op jit(solution)/shard_map/ppermute | solution.py:12
  1168.7 7.2 fusion.2
  1179.1 84.2 %collective-permute-done.6 = f32[2,512,2,512]{3,1,2,0:T(8,128)} collective-permute-done((f32[2,512,2,512]{3,1,2,0:T(8,128)}, f32[2,512,2,512]{3,1,2,0:T(8,128)}, u32[]{:S(2)}, u32[]{:S(2)}) %collective-permute-start.6) | collective-permute-done | bytes 4194336 | tf_op jit(solution)/shard_map/ppermute | solution.py:12
  1266.2 5.8 fusion.3
  1278.6 81.2 %collective-permute-done.7 = f32[2,512,2,512]{3,1,2,0:T(8,128)} collective-permute-done((f32[2,512,2,512]{3,1,2,0:T(8,128)}, f32[2,512,2,512]{3,1,2,0:T(8,128)}, u32[]{:S(2)}, u32[]{:S(2)}) %collective-permute-start.7) | collective-permute-done | bytes 4194336 | tf_op jit(solution)/shard_map/ppermute | solution.py:12
  (120 shorter events, 125.7 us)
Async XLA Ops:
  6.4 12.0 copy-start.26
  6.4 12.0 copy-start.27
  13.7 26.1 %all-to-all-start = ((bf16[8,2,49152]{2,1,0:T(2,128)(2,1)}), bf16[8,2,49152]{2,1,0:T(2,128)(2,1)S(1)}, u32[]{:S(2)}, u32[]{:S(2)}) async-start(bf16[8,2,49152]{2,1,0:T(2,128)(2,1)} %reshape.334), calls=%async_computation | async-start | bytes 3145728 | tf_op jit(solution)/shard_map/all_to_all | solution.py:154
  49.0 3.4 copy-start.24
  52.3 2.5 copy-start.22
  56.8 4.7 copy-start.1
  56.8 6.0 copy-start.4
  62.8 184.4 %collective-permute-start = (f32[2,1024,2,512]{3,1,2,0:T(8,128)}, f32[2,1024,2,512]{3,1,2,0:T(8,128)}, u32[]{:S(2)}, u32[]{:S(2)}) collective-permute-start(f32[2,1024,2,512]{3,1,2,0:T(8,128)} %pad_maximum_fusion), channel_id=1, source_target_pairs={{0,64},{8,72},{16,80},{24,88},{32,96},{40,104},{48,112},{56,120},{... | collective-permute-start | bytes 25165832 | tf_op jit(solution)/shard_map/ppermute | solution.py:12
  66.8 186.0 %copy-start.2 = (f32[1,1024,2,512]{3,1,2,0:T(8,128)S(1)}, f32[1,1024,2,512]{3,1,2,0:T(8,128)}, u32[]{:S(2)}) copy-start(f32[1,1024,2,512]{3,1,2,0:T(8,128)} %copy-done.1) | copy-start | bytes 12582916
  66.8 186.0 %copy-start.5 = (f32[1,1024,2,512]{3,1,2,0:T(8,128)S(1)}, f32[1,1024,2,512]{3,1,2,0:T(8,128)}, u32[]{:S(2)}) copy-start(f32[1,1024,2,512]{3,1,2,0:T(8,128)} %copy-done.4) | copy-start | bytes 12582916
  252.8 10.4 copy-start.10
  252.8 10.4 copy-start.11
  263.2 182.2 %collective-permute-start.1 = (f32[2,1024,2,512]{3,1,2,0:T(8,128)}, f32[2,1024,2,512]{3,1,2,0:T(8,128)}, u32[]{:S(2)}, u32[]{:S(2)}) collective-permute-start(f32[2,1024,2,512]{3,1,2,0:T(8,128)} %maximum_select_fusion), channel_id=1, source_target_pairs={{0,32},{8,40},{16,48},{24,56},{32,0},{40,8},{48,16},{56,24},{64,96... | collective-permute-start | bytes 25165832 | tf_op jit(solution)/shard_map/ppermute | solution.py:12
  265.1 189.7 %copy-start.3 = (f32[1,1024,2,512]{3,1,2,0:T(8,128)S(1)}, f32[1,1024,2,512]{3,1,2,0:T(8,128)}, u32[]{:S(2)}) copy-start(f32[1,1024,2,512]{3,1,2,0:T(8,128)} %copy-done.1) | copy-start | bytes 12582916
  472.9 182.3 %collective-permute-start.2 = (f32[2,1024,2,512]{3,1,2,0:T(8,128)}, f32[2,1024,2,512]{3,1,2,0:T(8,128)}, u32[]{:S(2)}, u32[]{:S(2)}) collective-permute-start(f32[2,1024,2,512]{3,1,2,0:T(8,128)} %maximum_select_fusion.1), channel_id=1, source_target_pairs={{0,16},{8,24},{16,0},{24,8},{32,48},{40,56},{48,32},{56,40},{64,80... | collective-permute-start | bytes 25165832 | tf_op jit(solution)/shard_map/ppermute | solution.py:12
  655.2 8.2 copy-start
  670.8 179.9 %collective-permute-start.3 = (f32[2,1024,2,512]{3,1,2,0:T(8,128)}, f32[2,1024,2,512]{3,1,2,0:T(8,128)}, u32[]{:S(2)}, u32[]{:S(2)}) collective-permute-start(f32[2,1024,2,512]{3,1,2,0:T(8,128)} %maximum_select_fusion.2), channel_id=1, source_target_pairs={{0,8},{8,0},{16,24},{24,16},{32,40},{40,32},{48,56},{56,48},{64,72... | collective-permute-start | bytes 25165832 | tf_op jit(solution)/shard_map/ppermute | solution.py:12
  978.8 90.2 %copy-start.6 = (f32[1,512,2,512]{3,1,2,0:T(8,128)}, f32[1,512,2,512]{3,1,2,0:T(8,128)S(1)}, u32[]{:S(2)}) copy-start(f32[1,512,2,512]{3,1,2,0:T(8,128)S(1)} %get-tuple-element.7) | copy-start | bytes 6291460
  978.8 90.2 %copy-start.16 = (f32[1,512,2,512]{3,1,2,0:T(8,128)}, f32[1,512,2,512]{3,1,2,0:T(8,128)S(1)}, u32[]{:S(2)}) copy-start(f32[1,512,2,512]{3,1,2,0:T(8,128)S(1)} %get-tuple-element.5) | copy-start | bytes 6291460
  979.3 88.9 %collective-permute-start.4 = (f32[2,512,2,512]{3,1,2,0:T(8,128)S(1)}, f32[2,512,2,512]{3,1,2,0:T(8,128)S(1)}, u32[]{:S(2)}, u32[]{:S(2)}) collective-permute-start(f32[2,512,2,512]{3,1,2,0:T(8,128)S(1)} %pad_maximum_fusion.2), channel_id=1, source_target_pairs={{0,8},{8,0},{16,24},{24,16},{32,40},{40,32},{48,56},{56,48},{64,72... | collective-permute-start | bytes 12582920 | tf_op jit(solution)/shard_map/ppermute | solution.py:12
  981.4 87.6 %copy-start.12 = (f32[1,512,2,512]{3,1,2,0:T(8,128)}, f32[1,512,2,512]{3,1,2,0:T(8,128)S(1)}, u32[]{:S(2)}) copy-start(f32[1,512,2,512]{3,1,2,0:T(8,128)S(1)} %multiply_add_fusion.11) | copy-start | bytes 6291460
  1069.0 4.9 copy-start.18
  1069.0 4.9 copy-start.20
  1073.9 89.7 %collective-permute-start.5 = (f32[2,512,2,512]{3,1,2,0:T(8,128)}, f32[2,512,2,512]{3,1,2,0:T(8,128)}, u32[]{:S(2)}, u32[]{:S(2)}) collective-permute-start(f32[2,512,2,512]{3,1,2,0:T(8,128)} %fusion.1), channel_id=1, source_target_pairs={{0,16},{8,24},{16,0},{24,8},{32,48},{40,56},{48,32},{56,40},{64,80... | collective-permute-start | bytes 12582920 | tf_op jit(solution)/shard_map/ppermute | solution.py:12
  1077.1 91.6 %copy-start.17 = (f32[1,512,2,512]{3,1,2,0:T(8,128)S(1)}, f32[1,512,2,512]{3,1,2,0:T(8,128)}, u32[]{:S(2)}) copy-start(f32[1,512,2,512]{3,1,2,0:T(8,128)} %copy-done.16) | copy-start | bytes 6291460
  1077.1 91.6 %copy-start.19 = (f32[1,512,2,512]{3,1,2,0:T(8,128)S(1)}, f32[1,512,2,512]{3,1,2,0:T(8,128)}, u32[]{:S(2)}) copy-start(f32[1,512,2,512]{3,1,2,0:T(8,128)} %copy-done.18) | copy-start | bytes 6291460
  1077.1 91.6 %copy-start.21 = (f32[1,512,2,512]{3,1,2,0:T(8,128)S(1)}, f32[1,512,2,512]{3,1,2,0:T(8,128)}, u32[]{:S(2)}) copy-start(f32[1,512,2,512]{3,1,2,0:T(8,128)} %copy-done.20) | copy-start | bytes 6291460
  1080.1 88.6 %copy-start.7 = (f32[1,512,2,512]{3,1,2,0:T(8,128)S(1)}, f32[1,512,2,512]{3,1,2,0:T(8,128)}, u32[]{:S(2)}) copy-start(f32[1,512,2,512]{3,1,2,0:T(8,128)} %copy-done.6) | copy-start | bytes 6291460
  1080.1 88.6 %copy-start.9 = (f32[2,512,2,512]{3,1,2,0:T(8,128)S(1)}, f32[2,512,2,512]{3,1,2,0:T(8,128)}, u32[]{:S(2)}) copy-start(f32[2,512,2,512]{3,1,2,0:T(8,128)} %copy-done.8) | copy-start | bytes 12582916
  1080.1 88.6 %copy-start.13 = (f32[1,512,2,512]{3,1,2,0:T(8,128)S(1)}, f32[1,512,2,512]{3,1,2,0:T(8,128)}, u32[]{:S(2)}) copy-start(f32[1,512,2,512]{3,1,2,0:T(8,128)} %copy-done.12) | copy-start | bytes 6291460
  1175.9 87.4 %collective-permute-start.6 = (f32[2,512,2,512]{3,1,2,0:T(8,128)}, f32[2,512,2,512]{3,1,2,0:T(8,128)}, u32[]{:S(2)}, u32[]{:S(2)}) collective-permute-start(f32[2,512,2,512]{3,1,2,0:T(8,128)} %fusion.2), channel_id=1, source_target_pairs={{0,32},{8,40},{16,48},{24,56},{32,0},{40,8},{48,16},{56,24},{64,96... | collective-permute-start | bytes 12582920 | tf_op jit(solution)/shard_map/ppermute | solution.py:12
  1272.0 87.8 %collective-permute-start.7 = (f32[2,512,2,512]{3,1,2,0:T(8,128)}, f32[2,512,2,512]{3,1,2,0:T(8,128)}, u32[]{:S(2)}, u32[]{:S(2)}) collective-permute-start(f32[2,512,2,512]{3,1,2,0:T(8,128)} %fusion.3), channel_id=1, source_target_pairs={{0,64},{8,72},{16,80},{24,88},{32,96},{40,104},{48,112},{56,120},{... | collective-permute-start | bytes 12582920 | tf_op jit(solution)/shard_map/ppermute | solution.py:12
  (6 other events, 10.1 us)
where the time goes:
time: 1380 us; the launch traced here: 1370 us
  waiting for transfers between devices  1070 us (78%)
  other arithmetic  141 us (10%)
  matrix products  79.5 us (6%)
  local copies, waits for them, and re-layouts  59.5 us (4%)
  starting transfers between devices  20.8 us (2%)
    ppermute x8, waiting for transfers between devices, swapped(): lax.ppermute(value, axis, [(i, i ^ 1 << stride) for i in range(lax.axis_s...  1050 us
    dot_general x16, matrix products, product(): jnp.einsum(form, left, right, precision=lax.Precision.HIGHEST, preferred_...  79.5 us
    sub x12, other arithmetic, cmul(): left_real * right_real - left_imag * right_imag  50.6 us
    select_n x4, other arithmetic, forward_butterfly(): states = jnp.where(upper_bit == 1, jnp.stack(rotated), states + partner)  43.2 us
  transfers between devices with their start and end apart: 9, of which 9 were waited for; matrix products, arithmetic and copies ran while one was open for 1% of the time, Pallas kernels for 0%

commit v1 on v0

v1 whole, which is shorter than its diff:
```python
import functools

import jax
import jax.numpy as jnp
from jax import lax
from jax.experimental import pallas as pl
from jax.experimental.pallas import tpu as pltpu
from jax.sharding import PartitionSpec as P

F32 = jnp.float32
BF16 = jnp.bfloat16
SUBS = 8
LANES = 128


def encode(drive):
    scaled = drive * 1024.0
    size = jnp.abs(scaled)
    square = scaled * scaled
    fourth = square * square
    code = jnp.where(size >= 1.0, fourth * fourth, size)
    return jnp.where(scaled < 0.0, -code, code).astype(BF16)


def decode(code):
    code = code.astype(F32)
    size = jnp.abs(code)
    half = lax.rsqrt(jnp.maximum(size, 1.0))
    quarter = lax.rsqrt(half)
    root = quarter * lax.rsqrt(quarter)
    drive = jnp.where(size >= 1.0, root, size) * (1.0 / 1024.0)
    return jnp.where(code < 0.0, -drive, drive)


def encode_kernel(qkv_ref, code_ref, query_ref):
    drive = qkv_ref[1].astype(F32) * qkv_ref[2].astype(F32)
    code_ref[0] = encode(drive)
    query_ref[0] = qkv_ref[0]


def wide(ref, mode, lanes):
    return jnp.broadcast_to(ref[mode : mode + 1, lanes], (SUBS, LANES))


def state_kernel(modes, code_ref, decay_ref, tail_ref, drive_ref, sub_ref, block_ref):
    subs, steps, channels = code_ref.shape
    for sub in range(subs):
        rows = pl.ds(sub * steps, steps)
        for group in range(channels // LANES):
            lanes = pl.ds(group * LANES, LANES)
            drive_ref[group, rows, :] = decode(code_ref[sub, :, lanes])
    for group in range(channels // LANES):
        lanes = pl.ds(group * LANES, LANES)
        decay = [wide(decay_ref, mode, lanes) for mode in range(modes)]

        def step(i, states):
            x = drive_ref[group, pl.ds(i, SUBS, stride=steps), :]
            return [states[m] * decay[m] + x for m in range(modes)]

        zero = jnp.zeros((SUBS, LANES), F32)
        states = lax.fori_loop(0, steps, step, [zero] * modes, unroll=8)
        for mode in range(modes):
            sub_ref[mode, :, lanes] = states[mode]
            block_ref[mode : mode + 1, lanes] = jnp.sum(
                states[mode] * tail_ref[mode, :, lanes], axis=0, keepdims=True
            )


def local_kernel(modes, drive_ref, sub_ref, decay_ref, step_decay_ref, weight_ref, skip_ref, out_ref):
    groups, tokens, _ = drive_ref.shape
    steps = tokens // SUBS
    for group in range(groups):
        lanes = pl.ds(group * LANES, LANES)
        decay = [wide(decay_ref, mode, lanes) for mode in range(modes)]
        weight = [wide(weight_ref, mode, lanes) for mode in range(modes)]
        row = lax.broadcasted_iota(jnp.int32, (SUBS, LANES), 0)
        first = []
        for mode in range(modes):
            held = sub_ref[mode, :, lanes]
            factor = wide(step_decay_ref, mode, lanes)
            shift = 1
            while shift < SUBS:
                moved = jnp.where(row >= shift, pltpu.roll(held, shift, 0), 0.0)
                held = held + factor * moved
                factor = factor * factor
                shift *= 2
            first.append(jnp.where(row >= 1, pltpu.roll(held, 1, 0), 0.0))
        skip = jnp.broadcast_to(skip_ref[0:1, lanes], (SUBS, LANES))

        def step(i, states):
            at = pl.ds(i, SUBS, stride=steps)
            x = drive_ref[group, at, :]
            states = [states[m] * decay[m] + x for m in range(modes)]
            parts = [states[m] * weight[m] for m in range(modes)] + [skip * x]
            while len(parts) > 1:
                parts = [parts[j] + parts[j + 1] if j + 1 < len(parts) else parts[j] for j in range(0, len(parts), 2)]
            out_ref[group, at, :] = parts[0]
            return states

        lax.fori_loop(0, steps, step, first, unroll=4)


def final_kernel(modes, local_ref, query_ref, carry_ref, start_ref, decay_ref, out_ref, sum_ref):
    groups, tokens, _ = local_ref.shape
    steps = tokens // SUBS
    for group in range(groups):
        lanes = pl.ds(group * LANES, LANES)
        decay = [wide(decay_ref, mode, lanes) for mode in range(modes)]
        first = [start_ref[mode, :, lanes] * wide(carry_ref, mode, lanes) for mode in range(modes)]

        def step(i, states):
            at = pl.ds(i, SUBS, stride=steps)
            parts = [local_ref[group, at, :]] + states
            while len(parts) > 1:
                parts = [parts[j] + parts[j + 1] if j + 1 < len(parts) else parts[j] for j in range(0, len(parts), 2)]
            sum_ref[group, at, :] = parts[0]
            return [states[m] * decay[m] for m in range(modes)]

        lax.fori_loop(0, steps, step, first, unroll=8)
        for tile in range(tokens // LANES):
            rows = pl.ds(tile * LANES, LANES)
            gated = sum_ref[group, rows, :] * query_ref[rows, lanes].astype(F32)
            out_ref[pl.ds(group * LANES, LANES), rows] = gated.T.astype(BF16)


def per_device(qkv, residues, spans, skip):
    _, span_tokens, all_channels = qkv.shape
    devices = lax.axis_size("tp")
    channels, modes = residues.shape
    tokens = devices * span_tokens
    steps = tokens // SUBS
    groups = channels // LANES
    vmem = pl.BlockSpec(memory_space=pltpu.VMEM)
    params = pltpu.CompilerParams(vmem_limit_bytes=32 * 1024 * 1024)

    code, query = pl.pallas_call(
        encode_kernel,
        grid=(devices,),
        in_specs=[pl.BlockSpec((3, span_tokens, channels), lambda j: (0, 0, j))],
        out_specs=[pl.BlockSpec((1, span_tokens, channels), lambda j: (j, 0, 0))] * 2,
        out_shape=[jax.ShapeDtypeStruct((devices, span_tokens, channels), BF16)] * 2,
    )(qkv)
    code = lax.all_to_all(code, "tp", 0, 0)
    query = lax.all_to_all(query, "tp", 0, 0).reshape(tokens, channels)

    rates = 1.0 / spans.T
    weight = residues.T * jnp.sqrt(rates)
    decay = jnp.exp(-rates)
    sub_index = jnp.arange(SUBS, dtype=F32)[None, :, None]
    tail = jnp.exp(-rates[:, None, :] * (steps * (SUBS - 1 - sub_index)))
    start = weight[:, None, :] * jnp.exp(-rates[:, None, :] * (steps * sub_index + 1.0))
    step_decay = jnp.exp(-rates * steps)

    drive, subs, block = pl.pallas_call(
        functools.partial(state_kernel, modes),
        in_specs=[vmem] * 3,
        out_specs=[vmem] * 3,
        out_shape=[
            jax.ShapeDtypeStruct((groups, tokens, LANES), F32),
            jax.ShapeDtypeStruct((modes, SUBS, channels), F32),
            jax.ShapeDtypeStruct((modes, channels), F32),
        ],
        compiler_params=params,
        cost_estimate=pl.CostEstimate(flops=40_000_000, bytes_accessed=2_000_000, transcendentals=0),
    )(code, decay, tail)

    local = pl.pallas_call(
        functools.partial(local_kernel, modes),
        in_specs=[vmem] * 6,
        out_specs=vmem,
        out_shape=jax.ShapeDtypeStruct((groups, tokens, LANES), F32),
        compiler_params=params,
        cost_estimate=pl.CostEstimate(flops=80_000_000, bytes_accessed=2_000_000, transcendentals=0),
    )(drive, subs, decay, step_decay, weight, skip.reshape(1, channels))

    blocks = lax.axis_size("ctx")
    cols = 4
    place = lax.axis_index("ctx")
    col = place % cols
    row = place // cols

    def swapped(value, bits):
        return lax.ppermute(value, "ctx", [(i, i ^ bits) for i in range(blocks)])

    def power(count):
        count = jnp.asarray(count)
        factor = jnp.exp(-rates * jnp.maximum(count, 0).astype(F32))
        return jnp.where(count >= 0, factor, 0.0)

    before = jnp.zeros_like(block)
    total = power(tokens * (cols - 1 - col)) * block
    for k in range(1, cols):
        other = swapped(block, k)
        before = before + power(tokens * (col - 1 - (col ^ k))) * other
        total = total + power(tokens * (cols - 1 - (col ^ k))) * other
    carry = jnp.zeros_like(block)
    for k in range(1, blocks // cols):
        other = swapped(total, k * cols)
        carry = carry + power(tokens * cols * (row - 1 - (row ^ k))) * other
    carry = before + power(tokens * col) * carry

    return pl.pallas_call(
        functools.partial(final_kernel, modes),
        in_specs=[vmem] * 5,
        out_specs=vmem,
        out_shape=jax.ShapeDtypeStruct((channels, tokens), BF16),
        scratch_shapes=[pltpu.VMEM((groups, tokens, LANES), F32)],
        compiler_params=params,
        cost_estimate=pl.CostEstimate(flops=40_000_000, bytes_accessed=2_000_000, transcendentals=0),
    )(local, query, carry, start, decay)


def solution(mesh):
    return jax.shard_map(
        per_device,
        mesh=mesh,
        in_specs=(P(None, ("ctx", "tp"), None), P("tp", None), P("tp", None), P("tp")),
        out_specs=P("tp", "ctx"),
        check_vma=False,
    )
```

time: 1380 us -> 46 us (0.03)
  waiting for transfers between devices: 1070 us -> 12.6 us
  other arithmetic: 141 us -> 0.3 us
  matrix products: 79.5 us -> 0 us
  local copies, waits for them, and re-layouts: 59.5 us -> 0.01 us
  Pallas kernels: 0 us -> 14.2 us
    ppermute x8 -> x6, waiting for transfers between devices: 1050 us -> 2.44 us  [swapped(): return lax.ppermute(value, 'ctx', [(i, i ^ bits) for i in range(blocks)])]
    dot_general x16 -> x0, matrix products: 79.5 us -> none  [product(): jnp.einsum(form, left, right, precision=lax.Precision.HIGHEST, preferred_...]
    select_n x8 -> x0, other arithmetic: 64.3 us -> none  [the longest x4 43.2 us: forward_butterfly(): states = jnp.where(upper_bit == 1, jnp.stack(rotated), states + partner)]
    sub x12 -> x0, other arithmetic: 50.6 us -> none  [cmul(): left_real * right_real - left_imag * right_imag]
    unnamed x61 -> x6, local copies, waits for them, and re-layouts: 24.1 us -> 0.01 us
    slice x3 -> x0, local copies, waits for them, and re-layouts: 15 us -> none  [forward_butterfly(): return (states[0], states[1], 2 * reversal + jnp.arange(2, dtype=jnp.int32))]
    pallas_call x0 -> x4, Pallas kernels: none -> 14.2 us  [the longest x1 5.4 us: per_device(): pl.pallas_call(encode_kernel, grid=(devices,), in_specs=[pl.BlockSpec((3,...]
  transfers between devices with their start and end apart: 9 -> 8, of which waited for: 9 -> 3; matrix products, arithmetic and copies ran while one was open for 1% -> 1% of each run, Pallas kernels for 0% -> 8%
where the time goes in v1:
time: 46 us; the launch traced here: 45.6 us
  starting transfers between devices  18.4 us (40%)
  Pallas kernels  14.2 us (31%)
  waiting for transfers between devices  12.6 us (27%)
    ppermute x6, starting transfers between devices, swapped(): return lax.ppermute(value, 'ctx', [(i, i ^ bits) for i in range(blocks)])  10.4 us
    all_to_all x1, waiting for transfers between devices, per_device(): code = lax.all_to_all(code, 'tp', 0, 0)  10.1 us
    pallas_call x1, Pallas kernels, per_device(): pl.pallas_call(encode_kernel, grid=(devices,), in_specs=[pl.BlockSpec((3,...  5.4 us
    all_to_all x1, starting transfers between devices, per_device(): code = lax.all_to_all(code, 'tp', 0, 0)  4.57 us
    pallas_call x1, Pallas kernels, per_device(): pl.pallas_call(functools.partial(local_kernel, modes), in_specs=[vmem] *...  3.75 us
    all_to_all x1, starting transfers between devices, per_device(): query = lax.all_to_all(query, 'tp', 0, 0).reshape(tokens, channels)  3.49 us
    pallas_call x1, Pallas kernels, per_device(): pl.pallas_call(functools.partial(final_kernel, modes), in_specs=[vmem] *...  2.91 us
    ppermute x6, waiting for transfers between devices, swapped(): return lax.ppermute(value, 'ctx', [(i, i ^ bits) for i in range(blocks)])  2.44 us
  transfers between devices with their start and end apart: 8, of which 3 were waited for; matrix products, arithmetic and copies ran while one was open for 1% of the time, Pallas kernels for 8%

profile of v1, /device:TPU:0, one launch (start us, length us, event | category | flops | bytes accessed | tf_op | source)
XLA Modules:
  0.0 45.6 jit_solution(17069712566919746233)
XLA Ops:
  0.0 0.0 copy-start.2
  0.0 0.0 copy-start.1
  0.0 5.4 %shard_map.46 = (bf16[8,64,512]{2,1,0:T(8,128)(2,1)}, bf16[8,64,512]{2,1,0:T(8,128)(2,1)}) custom-call(bf16[3,64,4096]{2,1,0:T(8,128)(2,1)} %qkv_ref.1), custom_call_target="tpu_custom_call" | custom-call | tf_op jit(solution)/shard_map/pallas_call | solution.py:136
  5.4 4.6 %all-to-all-start = ((bf16[8,64,512]{2,1,0:T(8,128)(2,1)}), bf16[8,64,512]{2,1,0:T(8,128)(2,1)S(1)}, u32[]{:S(2)}, u32[]{:S(2)}) async-start(bf16[8,64,512]{2,1,0:T(8,128)(2,1)} %get-tuple-element.10), calls=%async_computation | async-start | bytes 1048576 | tf_op jit(solution)/shard_map/all_to_all | solution.py:143
  10.0 0.0 copy-start
  10.0 0.0 copy-done.2
  10.0 0.0 copy-done.1
  10.1 0.1 exponential_multiply_fusion
  10.2 10.1 %all-to-all-done.code_ref = bf16[8,64,512]{2,1,0:T(8,128)(2,1)S(1)} async-done(((bf16[8,64,512]{2,1,0:T(8,128)(2,1)}), bf16[8,64,512]{2,1,0:T(8,128)(2,1)S(1)}, u32[]{:S(2)}, u32[]{:S(2)}) %all-to-all-start) | async-done | bytes 524320 | tf_op jit(solution)/shard_map/all_to_all | solution.py:143
  20.3 2.1 %shard_map.47 = (f32[4,512,128]{2,1,0:T(8,128)S(1)}, f32[16,8,512]{2,1,0:T(8,128)S(1)}, f32[16,512]{1,0:T(8,128)S(1)}) custom-call(bf16[8,64,512]{2,1,0:T(8,128)(2,1)S(1)} %all-to-all-done.code_ref, f32[16,512]{1,0:T(8,128)S(1)} %fusion.decay_ref, f32[16,8,512]{2,1,0:T(8,128)S(1)} %get-tuple-element.16.tail_ref), custom_call_target="tpu_custom_call" | custom-call | flops 40000000 | bytes 2000000 | tf_op jit(solution)/shard_map/pallas_call | solution.py:154
  22.4 1.6 %collective-permute-start = (f32[16,512]{1,0:T(8,128)S(1)}, f32[16,512]{1,0:T(8,128)S(1)}, u32[]{:S(2)}, u32[]{:S(2)}) collective-permute-start(f32[16,512]{1,0:T(8,128)S(1)} %get-tuple-element.14), channel_id=1, source_target_pairs={{0,8},{8,0},{16,24},{24,16},{32,40},{40,32},{48,56},{56,48},{64,72... | collective-permute-start | bytes 98312 | tf_op jit(solution)/shard_map/ppermute | solution.py:183
  24.0 2.7 %collective-permute-start.1 = (f32[16,512]{1,0:T(8,128)S(1)}, f32[16,512]{1,0:T(8,128)S(1)}, u32[]{:S(2)}, u32[]{:S(2)}) collective-permute-start(f32[16,512]{1,0:T(8,128)S(1)} %get-tuple-element.14), channel_id=1, source_target_pairs={{0,16},{8,24},{16,0},{24,8},{32,48},{40,56},{48,32},{56,40},{64,80... | collective-permute-start | bytes 98312 | tf_op jit(solution)/shard_map/ppermute | solution.py:183
  26.8 0.5 %collective-permute-start.2 = (f32[16,512]{1,0:T(8,128)S(1)}, f32[16,512]{1,0:T(8,128)S(1)}, u32[]{:S(2)}, u32[]{:S(2)}) collective-permute-start(f32[16,512]{1,0:T(8,128)S(1)} %get-tuple-element.14), channel_id=1, source_target_pairs={{0,24},{8,16},{16,8},{24,0},{32,56},{40,48},{48,40},{56,32},{64,88... | collective-permute-start | bytes 98312 | tf_op jit(solution)/shard_map/ppermute | solution.py:183
  27.2 3.5 %all-to-all-start.1 = ((bf16[8,64,512]{2,1,0:T(8,128)(2,1)}), bf16[8,64,512]{2,1,0:T(8,128)(2,1)S(1)}, u32[]{:S(2)}, u32[]{:S(2)}) async-start(bf16[8,64,512]{2,1,0:T(8,128)(2,1)} %get-tuple-element.13), calls=%async_computation.1 | async-start | bytes 1048576 | tf_op jit(solution)/shard_map/all_to_all | solution.py:144
  30.8 0.0 collective-permute-done
  30.8 0.0 collective-permute-done.1
  30.8 1.1 %collective-permute-done.2 = f32[16,512]{1,0:T(8,128)S(1)} collective-permute-done((f32[16,512]{1,0:T(8,128)S(1)}, f32[16,512]{1,0:T(8,128)S(1)}, u32[]{:S(2)}, u32[]{:S(2)}) %collective-permute-start.2) | collective-permute-done | bytes 32800 | tf_op jit(solution)/shard_map/ppermute | solution.py:183
  31.9 2.0 %collective-permute-start.3 = (f32[16,512]{1,0:T(8,128)S(1)}, f32[16,512]{1,0:T(8,128)S(1)}, u32[]{:S(2)}, u32[]{:S(2)}) collective-permute-start(f32[16,512]{1,0:T(8,128)S(1)} %get-tuple-element.17), channel_id=1, source_target_pairs={{0,32},{8,40},{16,48},{24,56},{32,0},{40,8},{48,16},{56,24},{64,96... | collective-permute-start | bytes 98312 | tf_op jit(solution)/shard_map/ppermute | solution.py:183
  33.9 3.6 %collective-permute-start.4 = (f32[16,512]{1,0:T(8,128)S(1)}, f32[16,512]{1,0:T(8,128)S(1)}, u32[]{:S(2)}, u32[]{:S(2)}) collective-permute-start(f32[16,512]{1,0:T(8,128)S(1)} %get-tuple-element.17), channel_id=1, source_target_pairs={{0,64},{8,72},{16,80},{24,88},{32,96},{40,104},{48,112},{56,120},{... | collective-permute-start | bytes 98312 | tf_op jit(solution)/shard_map/ppermute | solution.py:183
  37.5 0.0 collective-permute-start.5
  37.5 0.0 copy-done
  37.5 3.8 %shard_map.48.local_ref = f32[4,512,128]{2,1,0:T(8,128)S(1)} custom-call(f32[4,512,128]{2,1,0:T(8,128)S(1)} %get-tuple-element.11.drive_ref, f32[16,8,512]{2,1,0:T(8,128)S(1)} %get-tuple-element.12.sub_ref, f32[16,512]{1,0:T(8,128)S(1)} %fusion.decay_ref, f32[16,512]{1,0:T(8,128)S(1)} %get-tuple-element.18.step_decay_ref, ...), custom_call_target="tpu_custom_call" | custom-call | flops 80000000 | bytes 2000000 | tf_op jit(solution)/shard_map/pallas_call | solution.py:167
  41.3 0.0 collective-permute-done.3
  41.3 0.0 collective-permute-done.4
  41.3 1.3 %collective-permute-done.5 = f32[16,512]{1,0:T(8,128)S(1)} collective-permute-done((f32[16,512]{1,0:T(8,128)S(1)}, f32[16,512]{1,0:T(8,128)S(1)}, u32[]{:S(2)}, u32[]{:S(2)}) %collective-permute-start.5) | collective-permute-done | bytes 32800 | tf_op jit(solution)/shard_map/ppermute | solution.py:183
  42.6 0.1 multiply_add_fusion.carry_ref
  42.7 0.0 all-to-all-done.1
  42.7 2.9 %shard_map.49 = bf16[512,512]{1,0:T(8,128)(2,1)} custom-call(f32[4,512,128]{2,1,0:T(8,128)S(1)} %shard_map.48.local_ref, bf16[512,512]{1,0:T(8,128)(2,1)S(1)} %bitcast.14, f32[16,512]{1,0:T(8,128)S(1)} %multiply_add_fusion.carry_ref, f32[16,8,512]{2,1,0:T(8,128)S(1)} %get-tuple-element.15.start_ref, f32[16,512]{1,0:T(8,128)S(1)} %fusion.decay_ref), custom_call_target="tpu_custom_call" | custom-call | flops 40000000 | bytes 2000000 | tf_op jit(solution)/shard_map/pallas_call | solution.py:202
  (4 shorter events, 0.1 us)
Async XLA Ops:
  0.0 10.0 %copy-start.2 = (f32[512,16]{0,1:T(8,128)S(1)}, f32[512,16]{0,1:T(8,128)}, u32[]{:S(2)}) copy-start(f32[512,16]{0,1:T(8,128)} %param.5) | copy-start | bytes 98308
  0.0 10.0 %copy-start.1 = (f32[512,16]{0,1:T(8,128)S(1)}, f32[512,16]{0,1:T(8,128)}, u32[]{:S(2)}) copy-start(f32[512,16]{0,1:T(8,128)} %param.6) | copy-start | bytes 98308
  5.4 14.9 %all-to-all-start = ((bf16[8,64,512]{2,1,0:T(8,128)(2,1)}), bf16[8,64,512]{2,1,0:T(8,128)(2,1)S(1)}, u32[]{:S(2)}, u32[]{:S(2)}) async-start(bf16[8,64,512]{2,1,0:T(8,128)(2,1)} %get-tuple-element.10), calls=%async_computation | async-start | bytes 1048576 | tf_op jit(solution)/shard_map/all_to_all | solution.py:143
  10.0 27.5 %copy-start = (f32[512]{0:T(512)S(1)}, f32[512]{0:T(512)}, u32[]{:S(2)}) copy-start(f32[512]{0:T(512)} %param.7) | copy-start | bytes 6148
  22.4 8.3 %collective-permute-start = (f32[16,512]{1,0:T(8,128)S(1)}, f32[16,512]{1,0:T(8,128)S(1)}, u32[]{:S(2)}, u32[]{:S(2)}) collective-permute-start(f32[16,512]{1,0:T(8,128)S(1)} %get-tuple-element.14), channel_id=1, source_target_pairs={{0,8},{8,0},{16,24},{24,16},{32,40},{40,32},{48,56},{56,48},{64,72... | collective-permute-start | bytes 98312 | tf_op jit(solution)/shard_map/ppermute | solution.py:183
  24.0 6.8 %collective-permute-start.1 = (f32[16,512]{1,0:T(8,128)S(1)}, f32[16,512]{1,0:T(8,128)S(1)}, u32[]{:S(2)}, u32[]{:S(2)}) collective-permute-start(f32[16,512]{1,0:T(8,128)S(1)} %get-tuple-element.14), channel_id=1, source_target_pairs={{0,16},{8,24},{16,0},{24,8},{32,48},{40,56},{48,32},{56,40},{64,80... | collective-permute-start | bytes 98312 | tf_op jit(solution)/shard_map/ppermute | solution.py:183
  26.8 5.1 %collective-permute-start.2 = (f32[16,512]{1,0:T(8,128)S(1)}, f32[16,512]{1,0:T(8,128)S(1)}, u32[]{:S(2)}, u32[]{:S(2)}) collective-permute-start(f32[16,512]{1,0:T(8,128)S(1)} %get-tuple-element.14), channel_id=1, source_target_pairs={{0,24},{8,16},{16,8},{24,0},{32,56},{40,48},{48,40},{56,32},{64,88... | collective-permute-start | bytes 98312 | tf_op jit(solution)/shard_map/ppermute | solution.py:183
  27.2 15.5 %all-to-all-start.1 = ((bf16[8,64,512]{2,1,0:T(8,128)(2,1)}), bf16[8,64,512]{2,1,0:T(8,128)(2,1)S(1)}, u32[]{:S(2)}, u32[]{:S(2)}) async-start(bf16[8,64,512]{2,1,0:T(8,128)(2,1)} %get-tuple-element.13), calls=%async_computation.1 | async-start | bytes 1048576 | tf_op jit(solution)/shard_map/all_to_all | solution.py:144
  31.9 9.3 %collective-permute-start.3 = (f32[16,512]{1,0:T(8,128)S(1)}, f32[16,512]{1,0:T(8,128)S(1)}, u32[]{:S(2)}, u32[]{:S(2)}) collective-permute-start(f32[16,512]{1,0:T(8,128)S(1)} %get-tuple-element.17), channel_id=1, source_target_pairs={{0,32},{8,40},{16,48},{24,56},{32,0},{40,8},{48,16},{56,24},{64,96... | collective-permute-start | bytes 98312 | tf_op jit(solution)/shard_map/ppermute | solution.py:183
  33.9 7.4 %collective-permute-start.4 = (f32[16,512]{1,0:T(8,128)S(1)}, f32[16,512]{1,0:T(8,128)S(1)}, u32[]{:S(2)}, u32[]{:S(2)}) collective-permute-start(f32[16,512]{1,0:T(8,128)S(1)} %get-tuple-element.17), channel_id=1, source_target_pairs={{0,64},{8,72},{16,80},{24,88},{32,96},{40,104},{48,112},{56,120},{... | collective-permute-start | bytes 98312 | tf_op jit(solution)/shard_map/ppermute | solution.py:183
  37.5 5.1 %collective-permute-start.5 = (f32[16,512]{1,0:T(8,128)S(1)}, f32[16,512]{1,0:T(8,128)S(1)}, u32[]{:S(2)}, u32[]{:S(2)}) collective-permute-start(f32[16,512]{1,0:T(8,128)S(1)} %get-tuple-element.17), channel_id=1, source_target_pairs={{0,96},{8,104},{16,112},{24,120},{32,64},{40,72},{48,80},{56,88},{... | collective-permute-start | bytes 98312 | tf_op jit(solution)/shard_map/ppermute | solution.py:183

commit v2 on v1

v2 whole, which is shorter than its diff:
```python
import functools

import jax
import jax.numpy as jnp
from jax import lax
from jax.experimental import pallas as pl
from jax.experimental.pallas import tpu as pltpu
from jax.sharding import PartitionSpec as P

F32 = jnp.float32
BF16 = jnp.bfloat16
SUBS = 8
LANES = 128
SCALE = 1024.0


def encode(scaled):
    size = jnp.maximum(jnp.abs(scaled), 1.0)
    square = size * size
    return (scaled * (square * square * square * size)).astype(BF16)


def decode(code):
    code = code.astype(F32)
    half = lax.rsqrt(jnp.maximum(jnp.abs(code), 1.0))
    eighth = lax.rsqrt(lax.rsqrt(half))
    return code * (half * eighth * eighth * eighth)


def open_kernel(qkv_ref, own_ref, other_ref, query_own_ref, query_other_ref, held_ref, held_sem, query_sem):
    chips, tokens, width = own_ref.shape
    place = lax.axis_index("tp")
    chip, core = place // 2, place % 2

    def fetch(k):
        lanes = pl.ds(pl.multiple_of((chip ^ k) * 2 * width, 2 * width), 2 * width)
        return pltpu.make_async_copy(qkv_ref.at[pl.ds(1, 2), :, lanes], held_ref.at[k], held_sem.at[k])

    def pass_on(k, flip):
        lanes = pl.ds(pl.multiple_of((place ^ (2 * k + flip)) * width, width), width)
        out_ref = (query_own_ref, query_other_ref)[flip]
        return pltpu.make_async_copy(qkv_ref.at[0, :, lanes], out_ref.at[k], query_sem.at[2 * k + flip])

    for k in range(chips):
        fetch(k).start()
    for k in range(chips):
        for flip in range(2):
            pass_on(k, flip).start()
    for k in range(chips):
        fetch(k).wait()
        for flip, out_ref in ((0, own_ref), (1, other_ref)):
            half = pl.ds(pl.multiple_of((core ^ flip) * width, width), width)
            scaled = held_ref[k, 0, :, half].astype(F32) * held_ref[k, 1, :, half].astype(F32) * SCALE
            out_ref[k] = encode(scaled)
    for k in range(chips):
        for flip in range(2):
            pass_on(k, flip).wait()


def across_core(value):
    return lax.ppermute(value, "tp", [(i, i ^ 1) for i in range(lax.axis_size("tp"))])


def across_chips(value, k):
    return lax.ppermute(value, "tp", [(i, i ^ 2 * k) for i in range(lax.axis_size("tp"))])


def wide(ref, mode, lanes):
    return jnp.broadcast_to(ref[mode : mode + 1, lanes], (SUBS, LANES))


def state_kernel(modes, code_ref, decay_ref, tail_ref, drive_ref, sub_ref, block_ref):
    chips, _, steps, channels = code_ref.shape
    place = lax.axis_index("tp")
    for sub in range(2 * chips):
        k, flip = (place // 2) ^ (sub // 2), (place % 2) ^ (sub % 2)
        rows = pl.ds(sub * steps, steps)
        for group in range(channels // LANES):
            lanes = pl.ds(group * LANES, LANES)
            drive_ref[group, rows, :] = decode(code_ref[k, flip, :, lanes])
    for group in range(channels // LANES):
        lanes = pl.ds(group * LANES, LANES)
        decay = [wide(decay_ref, mode, lanes) for mode in range(modes)]

        def step(i, states):
            x = drive_ref[group, pl.ds(i, SUBS, stride=steps), :]
            return [states[m] * decay[m] + x for m in range(modes)]

        zero = jnp.zeros((SUBS, LANES), F32)
        states = lax.fori_loop(0, steps, step, [zero] * modes, unroll=8)
        for mode in range(modes):
            sub_ref[mode, :, lanes] = states[mode]
            block_ref[mode : mode + 1, lanes] = jnp.sum(
                states[mode] * tail_ref[mode, :, lanes], axis=0, keepdims=True
            )


def local_kernel(modes, begin, drive_ref, sub_ref, decay_ref, step_decay_ref, weight_ref, skip_ref, out_ref):
    groups, tokens, _ = out_ref.shape
    steps = tokens // SUBS
    for group in range(groups):
        lanes = pl.ds((begin + group) * LANES, LANES)
        decay = [wide(decay_ref, mode, lanes) for mode in range(modes)]
        weight = [wide(weight_ref, mode, lanes) for mode in range(modes)]
        row = lax.broadcasted_iota(jnp.int32, (SUBS, LANES), 0)
        first = []
        for mode in range(modes):
            held = sub_ref[mode, :, lanes]
            factor = wide(step_decay_ref, mode, lanes)
            shift = 1
            while shift < SUBS:
                moved = jnp.where(row >= shift, pltpu.roll(held, shift, 0), 0.0)
                held = held + factor * moved
                factor = factor * factor
                shift *= 2
            first.append(jnp.where(row >= 1, pltpu.roll(held, 1, 0), 0.0))
        skip = jnp.broadcast_to(skip_ref[0:1, lanes], (SUBS, LANES))

        def step(i, states):
            at = pl.ds(i, SUBS, stride=steps)
            x = drive_ref[begin + group, at, :]
            states = [states[m] * decay[m] + x for m in range(modes)]
            parts = [states[m] * weight[m] for m in range(modes)] + [skip * x]
            while len(parts) > 1:
                parts = [parts[j] + parts[j + 1] if j + 1 < len(parts) else parts[j] for j in range(0, len(parts), 2)]
            out_ref[group, at, :] = parts[0]
            return states

        lax.fori_loop(0, steps, step, first, unroll=4)


def final_kernel(modes, low_ref, high_ref, part_ref, carry_ref, start_ref, decay_ref, out_ref, sum_ref, query_ref):
    groups, tokens, _ = sum_ref.shape
    steps = tokens // SUBS
    place = lax.axis_index("tp")
    for sub in range(SUBS):
        query_ref[pl.ds(sub * steps, steps), :] = part_ref[(place // 2) ^ (sub // 2), (place % 2) ^ (sub % 2)]
    for group in range(groups):
        lanes = pl.ds(group * LANES, LANES)
        decay = [wide(decay_ref, mode, lanes) for mode in range(modes)]
        local_ref = (low_ref, high_ref)[group // (groups // 2)]
        first = [start_ref[mode, :, lanes] * wide(carry_ref, mode, lanes) for mode in range(modes)]

        def step(i, states):
            at = pl.ds(i, SUBS, stride=steps)
            parts = [local_ref[group % (groups // 2), at, :]] + states
            while len(parts) > 1:
                parts = [parts[j] + parts[j + 1] if j + 1 < len(parts) else parts[j] for j in range(0, len(parts), 2)]
            sum_ref[group, at, :] = parts[0]
            return [states[m] * decay[m] for m in range(modes)]

        lax.fori_loop(0, steps, step, first, unroll=8)
        for tile in range(tokens // LANES):
            rows = pl.ds(tile * LANES, LANES)
            gated = sum_ref[group, rows, :] * query_ref[rows, lanes].astype(F32)
            out_ref[pl.ds(group * LANES, LANES), rows] = gated.T.astype(BF16)


def per_device(qkv, residues, spans, skip):
    _, span_tokens, all_channels = qkv.shape
    devices = lax.axis_size("tp")
    channels, modes = residues.shape
    tokens = devices * span_tokens
    steps = tokens // SUBS
    groups = channels // LANES
    vmem = pl.BlockSpec(memory_space=pltpu.VMEM)
    params = pltpu.CompilerParams(vmem_limit_bytes=32 * 1024 * 1024)

    chips = devices // 2
    own, other, query_own, query_other = pl.pallas_call(
        open_kernel,
        in_specs=[pl.BlockSpec(memory_space=pl.ANY)],
        out_specs=[vmem] * 4,
        out_shape=[jax.ShapeDtypeStruct((n, span_tokens, channels), BF16) for n in [chips] * 4],
        scratch_shapes=[
            pltpu.VMEM((chips, 2, span_tokens, 2 * channels), BF16),
            pltpu.SemaphoreType.DMA((chips,)),
            pltpu.SemaphoreType.DMA((devices,)),
        ],
        compiler_params=params,
    )(qkv)
    code = jnp.stack([own, across_core(other)], 1)
    code = jnp.stack([code[0]] + [across_chips(code[k], k) for k in range(1, chips)])
    query = jnp.stack([query_own, across_core(query_other)], 1)
    code, query = lax.optimization_barrier((code, query))

    rates = 1.0 / spans.T
    weight = residues.T * jnp.sqrt(rates) * (1.0 / SCALE)
    decay = jnp.exp(-rates)
    sub_index = jnp.arange(SUBS, dtype=F32)[None, :, None]
    tail = jnp.exp(-rates[:, None, :] * (steps * (SUBS - 1 - sub_index)))
    start = weight[:, None, :] * jnp.exp(-rates[:, None, :] * (steps * sub_index + 1.0))
    step_decay = jnp.exp(-rates * steps)

    drive, subs, block = pl.pallas_call(
        functools.partial(state_kernel, modes),
        in_specs=[vmem] * 3,
        out_specs=[vmem] * 3,
        out_shape=[
            jax.ShapeDtypeStruct((groups, tokens, LANES), F32),
            jax.ShapeDtypeStruct((modes, SUBS, channels), F32),
            jax.ShapeDtypeStruct((modes, channels), F32),
        ],
        compiler_params=params,
        cost_estimate=pl.CostEstimate(flops=40_000_000, bytes_accessed=2_000_000, transcendentals=0),
    )(code, decay, tail)

    local = [
        pl.pallas_call(
            functools.partial(local_kernel, modes, begin),
            in_specs=[vmem] * 6,
            out_specs=vmem,
            out_shape=jax.ShapeDtypeStruct((groups // 2, tokens, LANES), F32),
            compiler_params=params,
            cost_estimate=pl.CostEstimate(flops=40_000_000, bytes_accessed=4_000_000, transcendentals=0),
        )(drive, subs, decay, step_decay, weight, skip.reshape(1, channels) * (1.0 / SCALE))
        for begin in (0, groups // 2)
    ]

    query = lax.optimization_barrier((query, block))[0]
    query = [query[0]] + [across_chips(query[k], k) for k in range(1, chips)]

    index = lax.axis_index("ctx")
    col, row = index % 4, index // 4

    def swapped(value, bits):
        return lax.ppermute(value, "ctx", [(i, i ^ bits) for i in range(lax.axis_size("ctx"))])

    def power(count):
        return jnp.exp(-rates * jnp.asarray(count).astype(F32))

    def join(before, total, upper, offset, span, bits, along=()):
        other, *along = lax.optimization_barrier((swapped(total, bits), *along))
        before = before + jnp.where(upper, power(offset), 0.0) * other
        whole = power(span)
        total = jnp.where(upper, whole * other + total, whole * total + other)
        return before, total, along

    before, total, along = join(jnp.zeros_like(block), block, col % 2 == 1, 0, tokens, 1, local[:1])
    local[:1] = along
    before, total, _ = join(before, total, col >= 2, tokens * (col % 2), 2 * tokens, 3)
    before, total, along = join(before, total, row % 2 == 1, tokens * col, 4 * tokens, 4, [query[1], query[3]])
    query[1], query[3] = along
    along = [query[2], local[1]]
    carry, _, along = join(before, total, row >= 2, tokens * (col + 4 * (row % 2)), 8 * tokens, 12, along)
    query[2], local[1] = along
    query = jnp.stack(query)

    return pl.pallas_call(
        functools.partial(final_kernel, modes),
        in_specs=[vmem] * 6,
        out_specs=vmem,
        out_shape=jax.ShapeDtypeStruct((channels, tokens), BF16),
        scratch_shapes=[pltpu.VMEM((groups, tokens, LANES), F32), pltpu.VMEM((tokens, channels), BF16)],
        compiler_params=params,
        cost_estimate=pl.CostEstimate(flops=40_000_000, bytes_accessed=2_000_000, transcendentals=0),
    )(*local, query, carry, start, decay)


def solution(mesh):
    return jax.shard_map(
        per_device,
        mesh=mesh,
        in_specs=(P(None, ("ctx", "tp"), None), P("tp", None), P("tp", None), P("tp")),
        out_specs=P("tp", "ctx"),
        check_vma=False,
    )
```

time: 46 us -> 40.4 us (0.88)
  Pallas kernels: 14.2 us -> 9.5 us
  waiting for transfers between devices: 12.6 us -> 8.56 us
  starting transfers between devices: 18.4 us -> 20 us
  local copies, waits for them, and re-layouts: 0.01 us -> 1.46 us
    all_to_all x2 -> x0, waiting for transfers between devices: 10.1 us -> none  [the longest x1 10.1 us: per_device(): code = lax.all_to_all(code, 'tp', 0, 0)]
    ppermute x6 -> x12, starting transfers between devices: 10.4 us -> 20 us  [the longest x4 10.1 us: swapped(): lax.ppermute(value, 'ctx', [(i, i ^ bits) for i in range(lax.axis_size('c...]
    all_to_all x2 -> x0, starting transfers between devices: 8.06 us -> none  [the longest x1 4.57 us: per_device(): code = lax.all_to_all(code, 'tp', 0, 0)]
    ppermute x6 -> x12, waiting for transfers between devices: 2.44 us -> 8.56 us  [the longest x6 7.13 us: across_chips(): lax.ppermute(value, 'tp', [(i, i ^ 2 * k) for i in range(lax.axis_size('t...]
    pallas_call x2 -> x3, Pallas kernels: 9.15 us -> 4.49 us  [the longest x2 3.77 us: per_device(): pl.pallas_call(functools.partial(local_kernel, modes, begin), in_specs=[v...]
    unnamed x6 -> x8, local copies, waits for them, and re-layouts: 0.01 us -> 1.42 us
  transfers between devices with their start and end apart: 8 -> 12, of which waited for: 3 -> 7; matrix products, arithmetic and copies ran while one was open for 1% -> 1% of each run, Pallas kernels for 8% -> 9%
where the time goes in v2:
time: 40.4 us; the launch traced here: 40.2 us
  starting transfers between devices  20 us (50%)
  Pallas kernels  9.5 us (24%)
  waiting for transfers between devices  8.56 us (21%)
  local copies, waits for them, and re-layouts  1.46 us (4%)
  other arithmetic  0.54 us (1%)
    ppermute x4, starting transfers between devices, swapped(): lax.ppermute(value, 'ctx', [(i, i ^ bits) for i in range(lax.axis_size('c...  10.1 us
    ppermute x6, starting transfers between devices, across_chips(): lax.ppermute(value, 'tp', [(i, i ^ 2 * k) for i in range(lax.axis_size('t...  9.36 us
    ppermute x6, waiting for transfers between devices, across_chips(): lax.ppermute(value, 'tp', [(i, i ^ 2 * k) for i in range(lax.axis_size('t...  7.13 us
    pallas_call x2, Pallas kernels, per_device(): pl.pallas_call(functools.partial(local_kernel, modes, begin), in_specs=[v...  3.77 us
    pallas_call x1, Pallas kernels, per_device(): pl.pallas_call(functools.partial(final_kernel, modes), in_specs=[vmem] *...  2.93 us
    pallas_call x1, Pallas kernels, per_device(): pl.pallas_call(functools.partial(state_kernel, modes), in_specs=[vmem] *...  2.08 us
    unnamed x8, local copies, waits for them, and re-layouts  1.42 us
    ppermute x2, waiting for transfers between devices, across_core(): lax.ppermute(value, 'tp', [(i, i ^ 1) for i in range(lax.axis_size('tp'))])  0.83 us
  transfers between devices with their start and end apart: 12, of which 7 were waited for; matrix products, arithmetic and copies ran while one was open for 1% of the time, Pallas kernels for 9%

profile of v2, /device:TPU:0, one launch (start us, length us, event | category | flops | bytes accessed | tf_op | source)
XLA Modules:
  0.0 40.2 jit_solution(18199552975668682341)
XLA Ops:
  0.0 1.4 %copy-done = bf16[3,64,4096]{2,1,0:T(8,128)(2,1)S(1)} copy-done((bf16[3,64,4096]{2,1,0:T(8,128)(2,1)S(1)}, bf16[3,64,4096]{2,1,0:T(8,128)(2,1)}, u32[]{:S(2)}) %copy-start) | copy-done | bytes 1572888
  1.4 0.7 %shard_map.46 = (bf16[4,64,512]{2,1,0:T(8,128)(2,1)S(1)}, bf16[4,64,512]{2,1,0:T(8,128)(2,1)S(1)}, bf16[4,64,512]{2,1,0:T(8,128)(2,1)S(1)}, bf16[4,64,512]{2,1,0:T(8,128)(2,1)S(1)}) custom-call(bf16[3,64,4096]{2,1,0:T(8,128)(2,1)S(1)} %copy-done), custom_call_target="tpu_custom_call" | custom-call | tf_op jit(solution)/shard_map/pallas_call | solution.py:170
  2.1 0.1 collective-permute-start
  2.2 0.5 %collective-permute-start.4 = (bf16[4,64,512]{2,1,0:T(8,128)(2,1)S(1)}, bf16[4,64,512]{2,1,0:T(8,128)(2,1)S(1)}, u32[]{:S(2)}, u32[]{:S(2)}) collective-permute-start(bf16[4,64,512]{2,1,0:T(8,128)(2,1)S(1)} %get-tuple-element.26), channel_id=1, source_target_pairs={{0,1},{1,0},{2,3},{3,2},{4,5},{5,4},{6,7},{7,6},{8,9},{9,8},{10,11... | collective-permute-start | bytes 786440 | tf_op jit(solution)/shard_map/ppermute | solution.py:61
  2.8 0.1 exponential_multiply_fusion
  2.9 0.8 %collective-permute-done = bf16[4,64,512]{2,1,0:T(8,128)(2,1)S(1)} collective-permute-done((bf16[4,64,512]{2,1,0:T(8,128)(2,1)S(1)}, bf16[4,64,512]{2,1,0:T(8,128)(2,1)S(1)}, u32[]{:S(2)}, u32[]{:S(2)}) %collective-permute-start) | collective-permute-done | bytes 262176 | tf_op jit(solution)/shard_map/ppermute | solution.py:61
  3.8 0.0 copy-start.3
  3.8 1.7 %collective-permute-start.1 = (bf16[2,64,512]{2,1,0:T(8,128)(2,1)S(1)}, bf16[2,64,512]{2,1,0:T(8,128)(2,1)S(1)}, u32[]{:S(2)}, u32[]{:S(2)}) collective-permute-start(bf16[2,64,512]{2,1,0:T(8,128)(2,1)S(1)} %get-tuple-element.46), channel_id=1, source_target_pairs={{0,2},{1,3},{2,0},{3,1},{4,6},{5,7},{6,4},{7,5},{8,10},{9,11},{10,... | collective-permute-start | bytes 393224 | tf_op jit(solution)/shard_map/ppermute | solution.py:65
  5.6 2.2 %collective-permute-start.3 = (bf16[2,64,512]{2,1,0:T(8,128)(2,1)S(1)}, bf16[2,64,512]{2,1,0:T(8,128)(2,1)S(1)}, u32[]{:S(2)}, u32[]{:S(2)}) collective-permute-start(bf16[2,64,512]{2,1,0:T(8,128)(2,1)S(1)} %get-tuple-element.47), channel_id=1, source_target_pairs={{0,6},{1,7},{2,4},{3,5},{4,2},{5,3},{6,0},{7,1},{8,14},{9,15},{10,... | collective-permute-start | bytes 393224 | tf_op jit(solution)/shard_map/ppermute | solution.py:65
  7.7 0.7 %collective-permute-start.2 = (bf16[2,64,512]{2,1,0:T(8,128)(2,1)S(1)}, bf16[2,64,512]{2,1,0:T(8,128)(2,1)S(1)}, u32[]{:S(2)}, u32[]{:S(2)}) collective-permute-start(bf16[2,64,512]{2,1,0:T(8,128)(2,1)S(1)} %get-tuple-element.48), channel_id=1, source_target_pairs={{0,4},{1,5},{2,6},{3,7},{4,0},{5,1},{6,2},{7,3},{8,12},{9,13},{10,... | collective-permute-start | bytes 393224 | tf_op jit(solution)/shard_map/ppermute | solution.py:65
  8.5 0.0 collective-permute-done.4
  8.5 0.1 pad_maximum_fusion.1
  8.6 0.9 %collective-permute-done.1 = bf16[2,64,512]{2,1,0:T(8,128)(2,1)S(1)} collective-permute-done((bf16[2,64,512]{2,1,0:T(8,128)(2,1)S(1)}, bf16[2,64,512]{2,1,0:T(8,128)(2,1)S(1)}, u32[]{:S(2)}, u32[]{:S(2)}) %collective-permute-start.1) | collective-permute-done | bytes 131104 | tf_op jit(solution)/shard_map/ppermute | solution.py:65
  9.4 3.9 %collective-permute-done.3 = bf16[2,64,512]{2,1,0:T(8,128)(2,1)S(1)} collective-permute-done((bf16[2,64,512]{2,1,0:T(8,128)(2,1)S(1)}, bf16[2,64,512]{2,1,0:T(8,128)(2,1)S(1)}, u32[]{:S(2)}, u32[]{:S(2)}) %collective-permute-start.3) | collective-permute-done | bytes 131104 | tf_op jit(solution)/shard_map/ppermute | solution.py:65
  13.3 1.5 %collective-permute-done.2 = bf16[2,64,512]{2,1,0:T(8,128)(2,1)S(1)} collective-permute-done((bf16[2,64,512]{2,1,0:T(8,128)(2,1)S(1)}, bf16[2,64,512]{2,1,0:T(8,128)(2,1)S(1)}, u32[]{:S(2)}, u32[]{:S(2)}) %collective-permute-start.2) | collective-permute-done | bytes 131104 | tf_op jit(solution)/shard_map/ppermute | solution.py:65
  14.8 0.1 pad_maximum_fusion.code_ref
  14.9 2.1 %shard_map.47 = (f32[4,512,128]{2,1,0:T(8,128)S(1)}, f32[16,8,512]{2,1,0:T(8,128)S(1)}, f32[16,512]{1,0:T(8,128)S(1)}) custom-call(bf16[4,2,64,512]{3,2,1,0:T(8,128)(2,1)S(1)} %pad_maximum_fusion.code_ref, f32[16,512]{1,0:T(8,128)S(1)} %get-tuple-element.54.decay_ref, f32[16,8,512]{2,1,0:T(8,128)S(1)} %get-tuple-element.50.tail_ref), custom_call_target="tpu_custom_call" | custom-call | flops 40000000 | bytes 2000000 | tf_op jit(solution)/shard_map/pallas_call | solution.py:195
  17.0 1.6 %collective-permute-start.5 = (f32[16,512]{1,0:T(8,128)S(1)}, f32[16,512]{1,0:T(8,128)S(1)}, u32[]{:S(2)}, u32[]{:S(2)}) collective-permute-start(f32[16,512]{1,0:T(8,128)S(1)} %get-tuple-element.28), channel_id=1, source_target_pairs={{0,8},{8,0},{16,24},{24,16},{32,40},{40,32},{48,56},{56,48},{64,72... | collective-permute-start | bytes 98312 | tf_op jit(solution)/shard_map/ppermute | solution.py:227
  18.6 1.9 %shard_map.48.low_ref = f32[2,512,128]{2,1,0:T(8,128)S(1)} custom-call(f32[4,512,128]{2,1,0:T(8,128)S(1)} %get-tuple-element.29.drive_ref, f32[16,8,512]{2,1,0:T(8,128)S(1)} %get-tuple-element.30.sub_ref, f32[16,512]{1,0:T(8,128)S(1)} %get-tuple-element.54.decay_ref, f32[16,512]{1,0:T(8,128)S(1)} %get-tuple-element.53.step_decay_ref, ...), custom_call_target="tpu_custom_call" | custom-call | flops 40000000 | bytes 4000000 | tf_op jit(solution)/shard_map/pallas_call | solution.py:209
  20.5 0.5 %collective-permute-done.5 = f32[16,512]{1,0:T(8,128)S(1)} collective-permute-done((f32[16,512]{1,0:T(8,128)S(1)}, f32[16,512]{1,0:T(8,128)S(1)}, u32[]{:S(2)}, u32[]{:S(2)}) %collective-permute-start.5) | collective-permute-done | bytes 32800 | tf_op jit(solution)/shard_map/ppermute | solution.py:227
  21.0 2.8 %collective-permute-start.6 = (f32[16,512]{1,0:T(8,128)S(1)}, f32[16,512]{1,0:T(8,128)S(1)}, u32[]{:S(2)}, u32[]{:S(2)}) collective-permute-start(f32[16,512]{1,0:T(8,128)S(1)} %add_select_fusion.2), channel_id=1, source_target_pairs={{0,24},{8,16},{16,8},{24,0},{32,56},{40,48},{48,40},{56,32},{64,88... | collective-permute-start | bytes 98312 | tf_op jit(solution)/shard_map/ppermute | solution.py:227
  23.9 2.3 %collective-permute-start.9 = (bf16[2,64,512]{2,1,0:T(8,128)(2,1)S(1)}, bf16[2,64,512]{2,1,0:T(8,128)(2,1)S(1)}, u32[]{:S(2)}, u32[]{:S(2)}) collective-permute-start(bf16[2,64,512]{2,1,0:T(8,128)(2,1)S(1)} %get-tuple-element.43), channel_id=1, source_target_pairs={{0,6},{1,7},{2,4},{3,5},{4,2},{5,3},{6,0},{7,1},{8,14},{9,15},{10,... | collective-permute-start | bytes 393224 | tf_op jit(solution)/shard_map/ppermute | solution.py:65
  26.2 0.0 collective-permute-start.8
  26.2 0.1 collective-permute-done.6
  26.3 2.0 %collective-permute-start.7 = (f32[16,512]{1,0:T(8,128)S(1)}, f32[16,512]{1,0:T(8,128)S(1)}, u32[]{:S(2)}, u32[]{:S(2)}) collective-permute-start(f32[16,512]{1,0:T(8,128)S(1)} %add_select_fusion.1), channel_id=1, source_target_pairs={{0,32},{8,40},{16,48},{24,56},{32,0},{40,8},{48,16},{56,24},{64,96... | collective-permute-start | bytes 98312 | tf_op jit(solution)/shard_map/ppermute | solution.py:227
  28.3 2.5 %collective-permute-start.11 = (bf16[2,64,512]{2,1,0:T(8,128)(2,1)S(1)}, bf16[2,64,512]{2,1,0:T(8,128)(2,1)S(1)}, u32[]{:S(2)}, u32[]{:S(2)}) collective-permute-start(bf16[2,64,512]{2,1,0:T(8,128)(2,1)S(1)} %get-tuple-element.42), channel_id=1, source_target_pairs={{0,4},{1,5},{2,6},{3,7},{4,0},{5,1},{6,2},{7,3},{8,12},{9,13},{10,... | collective-permute-start | bytes 393224 | tf_op jit(solution)/shard_map/ppermute | solution.py:65
  30.7 0.9 %collective-permute-done.9 = bf16[2,64,512]{2,1,0:T(8,128)(2,1)S(1)} collective-permute-done((bf16[2,64,512]{2,1,0:T(8,128)(2,1)S(1)}, bf16[2,64,512]{2,1,0:T(8,128)(2,1)S(1)}, u32[]{:S(2)}, u32[]{:S(2)}) %collective-permute-start.9) | collective-permute-done | bytes 131104 | tf_op jit(solution)/shard_map/ppermute | solution.py:65
  31.6 3.7 %collective-permute-start.10 = (f32[16,512]{1,0:T(8,128)S(1)}, f32[16,512]{1,0:T(8,128)S(1)}, u32[]{:S(2)}, u32[]{:S(2)}) collective-permute-start(f32[16,512]{1,0:T(8,128)S(1)} %add_select_fusion), channel_id=1, source_target_pairs={{0,96},{8,104},{16,112},{24,120},{32,64},{40,72},{48,80},{56,88},{... | collective-permute-start | bytes 98312 | tf_op jit(solution)/shard_map/ppermute | solution.py:227
  35.3 1.9 %shard_map.49.high_ref = f32[2,512,128]{2,1,0:T(8,128)S(1)} custom-call(f32[4,512,128]{2,1,0:T(8,128)S(1)} %get-tuple-element.29.drive_ref, f32[16,8,512]{2,1,0:T(8,128)S(1)} %get-tuple-element.30.sub_ref, f32[16,512]{1,0:T(8,128)S(1)} %get-tuple-element.54.decay_ref, f32[16,512]{1,0:T(8,128)S(1)} %get-tuple-element.53.step_decay_ref, ...), custom_call_target="tpu_custom_call" | custom-call | flops 40000000 | bytes 4000000 | tf_op jit(solution)/shard_map/pallas_call | solution.py:209
  37.2 0.0 collective-permute-done.10
  37.2 0.1 pad_maximum_fusion.2.part_ref
  37.3 2.9 %shard_map.50 = bf16[512,512]{1,0:T(8,128)(2,1)} custom-call(f32[2,512,128]{2,1,0:T(8,128)S(1)} %shard_map.48.low_ref, f32[2,512,128]{2,1,0:T(8,128)S(1)} %shard_map.49.high_ref, bf16[4,2,64,512]{3,2,1,0:T(8,128)(2,1)S(1)} %pad_maximum_fusion.2.part_ref, f32[16,512]{1,0:T(8,128)S(1)} %multiply_add_fusion.carry_ref, ...), custom_call_target="tpu_custom_call" | custom-call | flops 40000000 | bytes 2000000 | tf_op jit(solution)/shard_map/pallas_call | solution.py:249
  (19 shorter events, 0.3 us)
Async XLA Ops:
  0.0 1.4 %copy-start = (bf16[3,64,4096]{2,1,0:T(8,128)(2,1)S(1)}, bf16[3,64,4096]{2,1,0:T(8,128)(2,1)}, u32[]{:S(2)}) copy-start(bf16[3,64,4096]{2,1,0:T(8,128)(2,1)} %qkv_ref.1) | copy-start | bytes 4718596
  1.4 1.3 %copy-start.1 = (f32[512,16]{0,1:T(8,128)S(1)}, f32[512,16]{0,1:T(8,128)}, u32[]{:S(2)}) copy-start(f32[512,16]{0,1:T(8,128)} %param.6) | copy-start | bytes 98308
  1.4 1.3 %copy-start.2 = (f32[512,16]{0,1:T(8,128)S(1)}, f32[512,16]{0,1:T(8,128)}, u32[]{:S(2)}) copy-start(f32[512,16]{0,1:T(8,128)} %param.5) | copy-start | bytes 98308
  2.1 1.6 %collective-permute-start = (bf16[4,64,512]{2,1,0:T(8,128)(2,1)S(1)}, bf16[4,64,512]{2,1,0:T(8,128)(2,1)S(1)}, u32[]{:S(2)}, u32[]{:S(2)}) collective-permute-start(bf16[4,64,512]{2,1,0:T(8,128)(2,1)S(1)} %get-tuple-element.24), channel_id=1, source_target_pairs={{0,1},{1,0},{2,3},{3,2},{4,5},{5,4},{6,7},{7,6},{8,9},{9,8},{10,11... | collective-permute-start | bytes 786440 | tf_op jit(solution)/shard_map/ppermute | solution.py:61
  2.2 6.3 %collective-permute-start.4 = (bf16[4,64,512]{2,1,0:T(8,128)(2,1)S(1)}, bf16[4,64,512]{2,1,0:T(8,128)(2,1)S(1)}, u32[]{:S(2)}, u32[]{:S(2)}) collective-permute-start(bf16[4,64,512]{2,1,0:T(8,128)(2,1)S(1)} %get-tuple-element.26), channel_id=1, source_target_pairs={{0,1},{1,0},{2,3},{3,2},{4,5},{5,4},{6,7},{7,6},{8,9},{9,8},{10,11... | collective-permute-start | bytes 786440 | tf_op jit(solution)/shard_map/ppermute | solution.py:61
  3.8 14.8 %copy-start.3 = (f32[512]{0:T(512)S(1)}, f32[512]{0:T(512)}, u32[]{:S(2)}) copy-start(f32[512]{0:T(512)} %param.7) | copy-start | bytes 6148
  3.8 5.6 %collective-permute-start.1 = (bf16[2,64,512]{2,1,0:T(8,128)(2,1)S(1)}, bf16[2,64,512]{2,1,0:T(8,128)(2,1)S(1)}, u32[]{:S(2)}, u32[]{:S(2)}) collective-permute-start(bf16[2,64,512]{2,1,0:T(8,128)(2,1)S(1)} %get-tuple-element.46), channel_id=1, source_target_pairs={{0,2},{1,3},{2,0},{3,1},{4,6},{5,7},{6,4},{7,5},{8,10},{9,11},{10,... | collective-permute-start | bytes 393224 | tf_op jit(solution)/shard_map/ppermute | solution.py:65
  5.6 7.8 %collective-permute-start.3 = (bf16[2,64,512]{2,1,0:T(8,128)(2,1)S(1)}, bf16[2,64,512]{2,1,0:T(8,128)(2,1)S(1)}, u32[]{:S(2)}, u32[]{:S(2)}) collective-permute-start(bf16[2,64,512]{2,1,0:T(8,128)(2,1)S(1)} %get-tuple-element.47), channel_id=1, source_target_pairs={{0,6},{1,7},{2,4},{3,5},{4,2},{5,3},{6,0},{7,1},{8,14},{9,15},{10,... | collective-permute-start | bytes 393224 | tf_op jit(solution)/shard_map/ppermute | solution.py:65
  7.7 7.1 %collective-permute-start.2 = (bf16[2,64,512]{2,1,0:T(8,128)(2,1)S(1)}, bf16[2,64,512]{2,1,0:T(8,128)(2,1)S(1)}, u32[]{:S(2)}, u32[]{:S(2)}) collective-permute-start(bf16[2,64,512]{2,1,0:T(8,128)(2,1)S(1)} %get-tuple-element.48), channel_id=1, source_target_pairs={{0,4},{1,5},{2,6},{3,7},{4,0},{5,1},{6,2},{7,3},{8,12},{9,13},{10,... | collective-permute-start | bytes 393224 | tf_op jit(solution)/shard_map/ppermute | solution.py:65
  17.0 4.0 %collective-permute-start.5 = (f32[16,512]{1,0:T(8,128)S(1)}, f32[16,512]{1,0:T(8,128)S(1)}, u32[]{:S(2)}, u32[]{:S(2)}) collective-permute-start(f32[16,512]{1,0:T(8,128)S(1)} %get-tuple-element.28), channel_id=1, source_target_pairs={{0,8},{8,0},{16,24},{24,16},{32,40},{40,32},{48,56},{56,48},{64,72... | collective-permute-start | bytes 98312 | tf_op jit(solution)/shard_map/ppermute | solution.py:227
  21.0 5.2 %collective-permute-start.6 = (f32[16,512]{1,0:T(8,128)S(1)}, f32[16,512]{1,0:T(8,128)S(1)}, u32[]{:S(2)}, u32[]{:S(2)}) collective-permute-start(f32[16,512]{1,0:T(8,128)S(1)} %add_select_fusion.2), channel_id=1, source_target_pairs={{0,24},{8,16},{16,8},{24,0},{32,56},{40,48},{48,40},{56,32},{64,88... | collective-permute-start | bytes 98312 | tf_op jit(solution)/shard_map/ppermute | solution.py:227
  23.9 7.7 %collective-permute-start.9 = (bf16[2,64,512]{2,1,0:T(8,128)(2,1)S(1)}, bf16[2,64,512]{2,1,0:T(8,128)(2,1)S(1)}, u32[]{:S(2)}, u32[]{:S(2)}) collective-permute-start(bf16[2,64,512]{2,1,0:T(8,128)(2,1)S(1)} %get-tuple-element.43), channel_id=1, source_target_pairs={{0,6},{1,7},{2,4},{3,5},{4,2},{5,3},{6,0},{7,1},{8,14},{9,15},{10,... | collective-permute-start | bytes 393224 | tf_op jit(solution)/shard_map/ppermute | solution.py:65
  26.2 5.4 %collective-permute-start.8 = (bf16[2,64,512]{2,1,0:T(8,128)(2,1)S(1)}, bf16[2,64,512]{2,1,0:T(8,128)(2,1)S(1)}, u32[]{:S(2)}, u32[]{:S(2)}) collective-permute-start(bf16[2,64,512]{2,1,0:T(8,128)(2,1)S(1)} %get-tuple-element.44), channel_id=1, source_target_pairs={{0,2},{1,3},{2,0},{3,1},{4,6},{5,7},{6,4},{7,5},{8,10},{9,11},{10,... | collective-permute-start | bytes 393224 | tf_op jit(solution)/shard_map/ppermute | solution.py:65
  26.3 4.5 %collective-permute-start.7 = (f32[16,512]{1,0:T(8,128)S(1)}, f32[16,512]{1,0:T(8,128)S(1)}, u32[]{:S(2)}, u32[]{:S(2)}) collective-permute-start(f32[16,512]{1,0:T(8,128)S(1)} %add_select_fusion.1), channel_id=1, source_target_pairs={{0,32},{8,40},{16,48},{24,56},{32,0},{40,8},{48,16},{56,24},{64,96... | collective-permute-start | bytes 98312 | tf_op jit(solution)/shard_map/ppermute | solution.py:227
  28.3 8.9 %collective-permute-start.11 = (bf16[2,64,512]{2,1,0:T(8,128)(2,1)S(1)}, bf16[2,64,512]{2,1,0:T(8,128)(2,1)S(1)}, u32[]{:S(2)}, u32[]{:S(2)}) collective-permute-start(bf16[2,64,512]{2,1,0:T(8,128)(2,1)S(1)} %get-tuple-element.42), channel_id=1, source_target_pairs={{0,4},{1,5},{2,6},{3,7},{4,0},{5,1},{6,2},{7,3},{8,12},{9,13},{10,... | collective-permute-start | bytes 393224 | tf_op jit(solution)/shard_map/ppermute | solution.py:65
  31.6 5.6 %collective-permute-start.10 = (f32[16,512]{1,0:T(8,128)S(1)}, f32[16,512]{1,0:T(8,128)S(1)}, u32[]{:S(2)}, u32[]{:S(2)}) collective-permute-start(f32[16,512]{1,0:T(8,128)S(1)} %add_select_fusion), channel_id=1, source_target_pairs={{0,96},{8,104},{16,112},{24,120},{32,64},{40,72},{48,80},{56,88},{... | collective-permute-start | bytes 98312 | tf_op jit(solution)/shard_map/ppermute | solution.py:227

commit v3 on v2

v3 whole, which is shorter than its diff:
```python
import functools

import jax
import jax.numpy as jnp
from jax import lax
from jax.experimental import pallas as pl
from jax.experimental.pallas import tpu as pltpu
from jax.sharding import PartitionSpec as P

F32 = jnp.float32
BF16 = jnp.bfloat16
SUBS = 8
LANES = 128
SCALE = 1024.0
VMEM = pl.BlockSpec(memory_space=pltpu.VMEM)
PARAMS = pltpu.CompilerParams(vmem_limit_bytes=32 * 1024 * 1024)


def encode(scaled):
    size = jnp.maximum(jnp.abs(scaled), 1.0)
    square = size * size
    return (scaled * (square * square * square * size)).astype(BF16)


def decode(code):
    code = code.astype(F32)
    half = lax.rsqrt(jnp.maximum(jnp.abs(code), 1.0))
    eighth = lax.rsqrt(lax.rsqrt(half))
    return code * (half * eighth * eighth * eighth)


def open_kernel(qkv_ref, *refs):
    *code_refs, low_ref, high_ref = refs
    _, _, width = code_refs[0].shape
    place = lax.axis_index("tp")
    chips = len(code_refs)
    for k, code_ref in enumerate(code_refs):
        for flip in range(2):
            lanes = pl.ds(pl.multiple_of((place ^ (2 * k + flip)) * width, width), width)
            code_ref[flip] = encode(qkv_ref[1, :, lanes].astype(F32) * qkv_ref[2, :, lanes].astype(F32) * SCALE)
    for half, out_ref in enumerate((low_ref, high_ref)):
        for part in range(chips):
            out_ref[part] = qkv_ref[0, :, pl.ds((half * chips + part) * width, width)]


def across_core(value):
    return lax.ppermute(value, "tp", [(i, i ^ 1) for i in range(lax.axis_size("tp"))])


def across_chips(value, k):
    return lax.ppermute(value, "tp", [(i, i ^ 2 * k) for i in range(lax.axis_size("tp"))])


def across_blocks(value, bits):
    return lax.ppermute(value, "ctx", [(i, i ^ bits) for i in range(lax.axis_size("ctx"))])


def wide(ref, mode, lanes):
    return jnp.broadcast_to(ref[mode : mode + 1, lanes], (SUBS, LANES))


def total_of(parts):
    while len(parts) > 1:
        parts = [parts[j] + parts[j + 1] if j + 1 < len(parts) else parts[j] for j in range(0, len(parts), 2)]
    return parts[0]


def state_kernel(modes, code_ref, decay_ref, tail_ref, earlier_ref, drive_ref, sub_ref, block_ref):
    chips, tokens, channels = code_ref.shape
    steps = chips * tokens // SUBS
    chip = lax.axis_index("tp") // 2
    for source in range(chips):
        for group in range(channels // LANES):
            lanes = pl.ds(group * LANES, LANES)
            drive_ref[group, pl.ds(source * tokens, tokens), :] = decode(code_ref[chip ^ source, :, lanes])
    for group in range(channels // LANES):
        lanes = pl.ds(group * LANES, LANES)
        decay = [wide(decay_ref, mode, lanes) for mode in range(modes)]

        def step(i, states):
            x = drive_ref[group, pl.ds(i, SUBS, stride=steps), :]
            return [states[m] * decay[m] + x for m in range(modes)]

        zero = jnp.zeros((SUBS, LANES), F32)
        states = lax.fori_loop(0, steps, step, [zero] * modes, unroll=8)
        for mode in range(modes):
            sub_ref[mode, :, lanes] = states[mode]
            block_ref[mode : mode + 1, lanes] = earlier_ref[mode : mode + 1, lanes] + jnp.sum(
                states[mode] * tail_ref[mode, :, lanes], axis=0, keepdims=True
            )


def first_states(near, far, decay_32, core):
    row = lax.broadcasted_iota(jnp.int32, (SUBS, LANES), 0)
    odd = row % 2 == 1
    decay_64 = decay_32 * decay_32
    decay_128 = decay_64 * decay_64
    first = jnp.where(core == 0, near, far)
    second = jnp.where(core == 0, far, near)
    first_before, second_before = pltpu.roll(first, 1, 0), pltpu.roll(second, 1, 0)
    first_whole = first + decay_32 * first_before
    held = second + decay_32 * second_before + decay_64 * first_whole
    held = held + decay_128 * jnp.where(row >= 2, pltpu.roll(held, 2, 0), 0.0)
    held = held + decay_128 * decay_128 * jnp.where(row >= 4, pltpu.roll(held, 4, 0), 0.0)
    into = jnp.where(odd, pltpu.roll(held, 2, 0), pltpu.roll(held, 1, 0))
    into = jnp.where(row >= 2, into, 0.0)
    middle = decay_64 * into + jnp.where(odd, first_whole, pltpu.roll(first_whole, SUBS - 1, 0))
    first = jnp.where(odd, decay_32 * into + first_before, into)
    second = jnp.where(odd, decay_32 * middle + second_before, middle)
    return jnp.where(core == 0, first, second), jnp.where(core == 0, second, first)


def local_kernel(modes, begin, *refs):
    drive_refs, (near_ref, far_ref, decay_ref, step_decay_ref, weight_ref, skip_ref), out_refs = refs[:2], refs[2:8], refs[8:]
    groups, tokens, _ = out_refs[0].shape
    steps = tokens // SUBS
    core = lax.axis_index("tp") % 2
    for group in range(groups):
        lanes = pl.ds((begin + group) * LANES, LANES)
        decay = [wide(decay_ref, mode, lanes) for mode in range(modes)]
        weight = [wide(weight_ref, mode, lanes) for mode in range(modes)]
        skip = jnp.broadcast_to(skip_ref[0:1, lanes], (SUBS, LANES))
        starts = [
            first_states(near_ref[m, :, lanes], far_ref[m, :, lanes], wide(step_decay_ref, m, lanes), core)
            for m in range(modes)
        ]
        for part, (drive_ref, out_ref) in enumerate(zip(drive_refs, out_refs)):

            def step(i, states):
                at = pl.ds(i, SUBS, stride=steps)
                x = drive_ref[begin + group, at, :]
                states = [states[m] * decay[m] + x for m in range(modes)]
                out_ref[group, at, :] = total_of([states[m] * weight[m] for m in range(modes)] + [skip * x])
                return states

            lax.fori_loop(0, steps, step, [start[part] for start in starts], unroll=4)


def final_kernel(modes, *refs):
    low_refs, high_refs = refs[0:2], refs[2:4]
    query_ref, carry_ref, near_ref, far_ref, decay_ref, out_ref, sum_ref, held_ref, out_sem = refs[4:]
    _, groups, tokens, _ = sum_ref.shape
    steps = tokens // SUBS
    core = lax.axis_index("tp") % 2

    def copy_out(group):
        return pltpu.make_async_copy(held_ref.at[group], out_ref.at[pl.ds(group * LANES, LANES)], out_sem.at[group])

    for group in range(groups):
        lanes = pl.ds(group * LANES, LANES)
        decay = [wide(decay_ref, mode, lanes) for mode in range(modes)]
        local_refs = low_refs if group < groups // 2 else high_refs
        for part, start_ref in enumerate((near_ref, far_ref)):
            local_ref = local_refs[part]
            first = [start_ref[mode, :, lanes] * wide(carry_ref, mode, lanes) for mode in range(modes)]

            def step(i, states):
                at = pl.ds(i, SUBS, stride=steps)
                sum_ref[core ^ part, group, at, :] = total_of([local_ref[group % (groups // 2), at, :]] + states)
                return [states[m] * decay[m] for m in range(modes)]

            lax.fori_loop(0, steps, step, first, unroll=8)
        for tile in range(2 * tokens // LANES):
            rows = pl.ds(tile * LANES, LANES)
            mixed = jnp.concatenate([sum_ref[part, group, pl.ds(tile * LANES // 2, LANES // 2), :] for part in range(2)])
            gated = mixed * query_ref[rows, lanes].astype(F32)
            held_ref[group, :, rows] = gated.T.astype(BF16)
        copy_out(group).start()
    for group in range(groups):
        copy_out(group).wait()


def per_device(qkv, residues, spans, skip):
    _, span_tokens, _ = qkv.shape
    devices = lax.axis_size("tp")
    chips = devices // 2
    channels, modes = residues.shape
    tokens = devices * span_tokens
    half = tokens // 2
    groups = channels // LANES
    steps = half // SUBS
    core = lax.axis_index("tp") % 2

    outs = pl.pallas_call(
        open_kernel,
        in_specs=[VMEM],
        out_specs=[VMEM] * (chips + 2),
        out_shape=[jax.ShapeDtypeStruct((2, span_tokens, channels), BF16)] * chips
        + [jax.ShapeDtypeStruct((chips, span_tokens, channels), BF16)] * 2,
        compiler_params=PARAMS,
    )(qkv)
    code, (low, high) = list(outs[:chips]), outs[chips:]
    for k in (1, 3, 2):
        code[k] = across_chips(code[k], k)
    query = jnp.concatenate([low, high])
    query = lax.all_to_all(query, "tp", 0, 0).reshape(tokens, channels)
    near_code = jnp.stack([piece[0] for piece in code])
    far_code = across_core(jnp.stack([piece[1] for piece in code]))

    rates = 1.0 / spans.T
    weight = residues.T * jnp.sqrt(rates) * (1.0 / SCALE)
    decay = jnp.exp(-rates)
    step_decay = jnp.exp(-rates * steps)
    sub_index = jnp.arange(SUBS, dtype=jnp.int32)

    def first_token(side):
        return (2 * span_tokens * (sub_index // 2) + steps * (sub_index % 2) + span_tokens * side).astype(F32)[None, :, None]

    def tail(side):
        return jnp.exp(-rates[:, None, :] * (tokens - steps - first_token(side)))

    def start(side):
        return weight[:, None, :] * jnp.exp(-rates[:, None, :] * (first_token(side) + 1.0))

    def states(code, tail, earlier):
        return pl.pallas_call(
            functools.partial(state_kernel, modes),
            in_specs=[VMEM] * 4,
            out_specs=[VMEM] * 3,
            out_shape=[
                jax.ShapeDtypeStruct((groups, half, LANES), F32),
                jax.ShapeDtypeStruct((modes, SUBS, channels), F32),
                jax.ShapeDtypeStruct((modes, channels), F32),
            ],
            compiler_params=PARAMS,
            cost_estimate=pl.CostEstimate(flops=1000, bytes_accessed=1000, transcendentals=0),
        )(code, decay, tail, earlier)

    near_drive, near_subs, block = states(near_code, tail(core), jnp.zeros((modes, channels), F32))
    far_drive, far_subs, block = states(far_code, tail(1 - core), block)

    local = [
        pl.pallas_call(
            functools.partial(local_kernel, modes, begin),
            in_specs=[VMEM] * 8,
            out_specs=[VMEM] * 2,
            out_shape=[jax.ShapeDtypeStruct((groups // 2, half, LANES), F32)] * 2,
            compiler_params=PARAMS,
            cost_estimate=pl.CostEstimate(flops=40_000_000, bytes_accessed=4_000_000, transcendentals=0),
        )(
            near_drive, far_drive, near_subs, far_subs, decay, step_decay, weight,
            skip.reshape(1, channels) * (1.0 / SCALE),
        )
        for begin in (0, groups // 2)
    ]

    index = lax.axis_index("ctx")
    col, row = index % 4, index // 4

    def power(count):
        count = jnp.asarray(count)
        return jnp.where(count >= 0, jnp.exp(-rates * jnp.maximum(count, 0).astype(F32)), 0.0)

    others = [across_blocks(block, k) for k in (2, 1, 3)]
    others, query, local[0] = lax.optimization_barrier((others, query, local[0]))
    before = jnp.zeros_like(block)
    total = power(tokens * (3 - col)) * block
    for k, other in zip((2, 1, 3), others):
        before = before + power(tokens * (col - 1 - (col ^ k))) * other
        total = total + power(tokens * (3 - (col ^ k))) * other
    others = [across_blocks(total, 4 * k) for k in (2, 1, 3)]
    others, local[1] = lax.optimization_barrier((others, local[1]))
    carry = jnp.zeros_like(block)
    for k, other in zip((2, 1, 3), others):
        carry = carry + power(4 * tokens * (row - 1 - (row ^ k))) * other
    carry = before + power(tokens * col) * carry

    return pl.pallas_call(
        functools.partial(final_kernel, modes),
        in_specs=[VMEM] * 9,
        out_specs=pl.BlockSpec(memory_space=pl.ANY),
        out_shape=jax.ShapeDtypeStruct((channels, tokens), BF16),
        scratch_shapes=[
            pltpu.VMEM((2, groups, half, LANES), F32),
            pltpu.VMEM((groups, LANES, tokens), BF16),
            pltpu.SemaphoreType.DMA((groups,)),
        ],
        compiler_params=PARAMS,
        cost_estimate=pl.CostEstimate(flops=40_000_000, bytes_accessed=2_000_000, transcendentals=0),
    )(*local[0], *local[1], query, carry, start(core), start(1 - core), decay)


def solution(mesh):
    return jax.shard_map(
        per_device,
        mesh=mesh,
        in_specs=(P(None, ("ctx", "tp"), None), P("tp", None), P("tp", None), P("tp")),
        out_specs=P("tp", "ctx"),
        check_vma=False,
    )
```

time: 40.4 us -> 39.5 us (0.978)
  starting transfers between devices: 20 us -> 18.5 us
  other arithmetic: 0.54 us -> 1.32 us
    ppermute x4 -> x6, waiting for transfers between devices: 0.59 us -> 5.62 us  [across_blocks(): lax.ppermute(value, 'ctx', [(i, i ^ bits) for i in range(lax.axis_size('c...]
    ppermute x6 -> x3, waiting for transfers between devices: 7.13 us -> 2.44 us  [across_chips(): lax.ppermute(value, 'tp', [(i, i ^ 2 * k) for i in range(lax.axis_size('t...]
    ppermute x6 -> x3, starting transfers between devices: 9.36 us -> 4.78 us  [across_chips(): lax.ppermute(value, 'tp', [(i, i ^ 2 * k) for i in range(lax.axis_size('t...]
    all_to_all x0 -> x1, starting transfers between devices: none -> 4.37 us  [per_device(): query = lax.all_to_all(query, 'tp', 0, 0).reshape(tokens, channels)]
    ppermute x4 -> x6, starting transfers between devices: 10.1 us -> 9.22 us  [across_blocks(): lax.ppermute(value, 'ctx', [(i, i ^ bits) for i in range(lax.axis_size('c...]
    concatenate x0 -> x1, other arithmetic: none -> 0.84 us  [per_device(): query = jnp.concatenate([low, high])]
    ppermute x2 -> x1, waiting for transfers between devices: 0.83 us -> 0.32 us  [across_core(): lax.ppermute(value, 'tp', [(i, i ^ 1) for i in range(lax.axis_size('tp'))])]
    ppermute x2 -> x1, starting transfers between devices: 0.58 us -> 0.09 us  [across_core(): lax.ppermute(value, 'tp', [(i, i ^ 1) for i in range(lax.axis_size('tp'))])]
  transfers between devices with their start and end apart: 12 -> 11, of which waited for: 7 -> 7; matrix products, arithmetic and copies ran while one was open for 1% -> 3% of each run, Pallas kernels for 9% -> 16%
where the time goes in v3:
time: 39.5 us; the launch traced here: 39.3 us
  starting transfers between devices  18.5 us (47%)
  Pallas kernels  9.46 us (24%)
  waiting for transfers between devices  8.38 us (21%)
  local copies, waits for them, and re-layouts  1.47 us (4%)
  other arithmetic  1.32 us (3%)
    ppermute x6, starting transfers between devices, across_blocks(): lax.ppermute(value, 'ctx', [(i, i ^ bits) for i in range(lax.axis_size('c...  9.22 us
    ppermute x6, waiting for transfers between devices, across_blocks(): lax.ppermute(value, 'ctx', [(i, i ^ bits) for i in range(lax.axis_size('c...  5.62 us
    ppermute x3, starting transfers between devices, across_chips(): lax.ppermute(value, 'tp', [(i, i ^ 2 * k) for i in range(lax.axis_size('t...  4.78 us
    all_to_all x1, starting transfers between devices, per_device(): query = lax.all_to_all(query, 'tp', 0, 0).reshape(tokens, channels)  4.37 us
    pallas_call x2, Pallas kernels, per_device(): pl.pallas_call(functools.partial(local_kernel, modes, begin), in_specs=[V...  4.04 us
    pallas_call x1, Pallas kernels, per_device(): pl.pallas_call(functools.partial(final_kernel, modes), in_specs=[VMEM] *...  2.81 us
    ppermute x3, waiting for transfers between devices, across_chips(): lax.ppermute(value, 'tp', [(i, i ^ 2 * k) for i in range(lax.axis_size('t...  2.44 us
    pallas_call x2, Pallas kernels, states(): pl.pallas_call(functools.partial(state_kernel, modes), in_specs=[VMEM] *...  2.2 us
  transfers between devices with their start and end apart: 11, of which 7 were waited for; matrix products, arithmetic and copies ran while one was open for 3% of the time, Pallas kernels for 16%

profile of v3, /device:TPU:0, one launch (start us, length us, event | category | flops | bytes accessed | tf_op | source)
XLA Modules:
  0.0 39.3 jit_solution(13080438837682973008)
XLA Ops:
  0.0 1.4 %copy-done = bf16[3,64,4096]{2,1,0:T(8,128)(2,1)S(1)} copy-done((bf16[3,64,4096]{2,1,0:T(8,128)(2,1)S(1)}, bf16[3,64,4096]{2,1,0:T(8,128)(2,1)}, u32[]{:S(2)}) %copy-start) | copy-done | bytes 1572888
  1.4 0.4 %shard_map.46 = (bf16[2,64,512]{2,1,0:T(8,128)(2,1)S(1)}, bf16[2,64,512]{2,1,0:T(8,128)(2,1)S(1)}, bf16[2,64,512]{2,1,0:T(8,128)(2,1)S(1)}, bf16[2,64,512]{2,1,0...) custom-call(bf16[3,64,4096]{2,1,0:T(8,128)(2,1)S(1)} %copy-done), custom_call_target="tpu_custom_call" | custom-call | tf_op jit(solution)/shard_map/pallas_call | solution.py:184
  1.8 1.7 %collective-permute-start = (bf16[2,64,512]{2,1,0:T(8,128)(2,1)S(1)}, bf16[2,64,512]{2,1,0:T(8,128)(2,1)S(1)}, u32[]{:S(2)}, u32[]{:S(2)}) collective-permute-start(bf16[2,64,512]{2,1,0:T(8,128)(2,1)S(1)} %get-tuple-element.33), channel_id=1, source_target_pairs={{0,2},{1,3},{2,0},{3,1},{4,6},{5,7},{6,4},{7,5},{8,10},{9,11},{10,... | collective-permute-start | bytes 393224 | tf_op jit(solution)/shard_map/ppermute | solution.py:51
  3.6 2.9 %collective-permute-start.1 = (bf16[2,64,512]{2,1,0:T(8,128)(2,1)S(1)}, bf16[2,64,512]{2,1,0:T(8,128)(2,1)S(1)}, u32[]{:S(2)}, u32[]{:S(2)}) collective-permute-start(bf16[2,64,512]{2,1,0:T(8,128)(2,1)S(1)} %get-tuple-element.34), channel_id=1, source_target_pairs={{0,4},{1,5},{2,6},{3,7},{4,0},{5,1},{6,2},{7,3},{8,12},{9,13},{10,... | collective-permute-start | bytes 393224 | tf_op jit(solution)/shard_map/ppermute | solution.py:51
  6.5 0.1 collective-permute-start.2
  6.6 0.8 %pad_maximum_fusion = bf16[8,64,512]{2,1,0:T(8,128)(2,1)} fusion(bf16[4,64,512]{2,1,0:T(8,128)(2,1)S(1)} %get-tuple-element.39, bf16[4,64,512]{2,1,0:T(8,128)(2,1)S(1)} %get-tuple-element.38), kind=kLoop, calls=%fused_computation | loop fusion | flops 262144 | bytes 1048576 | tf_op jit(solution)/shard_map/concatenate | solution.py:195
  7.4 4.4 %all-to-all-start = ((bf16[8,64,512]{2,1,0:T(8,128)(2,1)}), bf16[8,64,512]{2,1,0:T(8,128)(2,1)S(1)}, u32[]{:S(2)}, u32[]{:S(2)}) async-start(bf16[8,64,512]{2,1,0:T(8,128)(2,1)} %pad_maximum_fusion), calls=%async_computation | async-start | bytes 1048576 | tf_op jit(solution)/shard_map/all_to_all | solution.py:196
  11.9 0.2 exponential_multiply_fusion
  12.1 0.0 copy-start.3
  12.2 0.0 collective-permute-done
  12.2 0.4 collective-permute-done.1
  12.6 2.0 %collective-permute-done.2 = bf16[2,64,512]{2,1,0:T(8,128)(2,1)S(1)} collective-permute-done((bf16[2,64,512]{2,1,0:T(8,128)(2,1)S(1)}, bf16[2,64,512]{2,1,0:T(8,128)(2,1)S(1)}, u32[]{:S(2)}, u32[]{:S(2)}) %collective-permute-start.2) | collective-permute-done | bytes 131104 | tf_op jit(solution)/shard_map/ppermute | solution.py:51
  14.7 0.1 collective-permute-start.3
  14.9 1.1 %shard_map.47 = (f32[4,256,128]{2,1,0:T(8,128)S(1)}, f32[16,8,512]{2,1,0:T(8,128)S(1)}, f32[16,512]{1,0:T(8,128)S(1)}) custom-call(bf16[4,64,512]{2,1,0:T(8,128)(2,1)S(1)} %pad_maximum_fusion.2.code_ref, f32[16,512]{1,0:T(8,128)S(1)} %get-tuple-element.74.decay_ref.refs_4_.refs_8_, f32[16,8,512]{2,1,0:T(8,128)S(1)} %get-tuple-element.69.tail_ref, ...), custom_call_target="tpu_custom_call" | custom-call | flops 1000 | bytes 1000 | tf_op jit(solution)/shard_map/pallas_call | solution.py:216
  16.0 0.3 collective-permute-done.3.code_ref
  16.3 1.1 %shard_map.48 = (f32[4,256,128]{2,1,0:T(8,128)S(1)}, f32[16,8,512]{2,1,0:T(8,128)S(1)}, f32[16,512]{1,0:T(8,128)S(1)}) custom-call(bf16[4,64,512]{2,1,0:T(8,128)(2,1)S(1)} %collective-permute-done.3.code_ref, f32[16,512]{1,0:T(8,128)S(1)} %get-tuple-element.74.decay_ref.refs_4_.refs_8_, f32[16,8,512]{2,1,0:T(8,128)S(1)} %get-tuple-element.70.tail_ref, ...), custom_call_target="tpu_custom_call" | custom-call | flops 1000 | bytes 1000 | tf_op jit(solution)/shard_map/pallas_call | solution.py:216
  17.4 3.1 %collective-permute-start.4 = (f32[16,512]{1,0:T(8,128)S(1)}, f32[16,512]{1,0:T(8,128)S(1)}, u32[]{:S(2)}, u32[]{:S(2)}) collective-permute-start(f32[16,512]{1,0:T(8,128)S(1)} %get-tuple-element.37), channel_id=1, source_target_pairs={{0,16},{8,24},{16,0},{24,8},{32,48},{40,56},{48,32},{56,40},{64,80... | collective-permute-start | bytes 98312 | tf_op jit(solution)/shard_map/ppermute | solution.py:55
  20.5 0.6 %collective-permute-start.5 = (f32[16,512]{1,0:T(8,128)S(1)}, f32[16,512]{1,0:T(8,128)S(1)}, u32[]{:S(2)}, u32[]{:S(2)}) collective-permute-start(f32[16,512]{1,0:T(8,128)S(1)} %get-tuple-element.37), channel_id=1, source_target_pairs={{0,8},{8,0},{16,24},{24,16},{32,40},{40,32},{48,56},{56,48},{64,72... | collective-permute-start | bytes 98312 | tf_op jit(solution)/shard_map/ppermute | solution.py:55
  21.1 0.6 %collective-permute-start.6 = (f32[16,512]{1,0:T(8,128)S(1)}, f32[16,512]{1,0:T(8,128)S(1)}, u32[]{:S(2)}, u32[]{:S(2)}) collective-permute-start(f32[16,512]{1,0:T(8,128)S(1)} %get-tuple-element.37), channel_id=1, source_target_pairs={{0,24},{8,16},{16,8},{24,0},{32,56},{40,48},{48,40},{56,32},{64,88... | collective-permute-start | bytes 98312 | tf_op jit(solution)/shard_map/ppermute | solution.py:55
  21.7 2.0 %shard_map.49 = (f32[2,256,128]{2,1,0:T(8,128)S(1)}, f32[2,256,128]{2,1,0:T(8,128)S(1)}) custom-call(f32[4,256,128]{2,1,0:T(8,128)S(1)} %get-tuple-element.40.refs_0_, f32[4,256,128]{2,1,0:T(8,128)S(1)} %get-tuple-element.41.refs_1_, f32[16,8,512]{2,1,0:T(8,128)S(1)} %get-tuple-element.42.refs_2_, f32[16,8,512]{2,1,0:T(8,128)S(1)} %get-tuple-element.43.refs_3_, ...), custom_call_target="tpu_custom_call" | custom-call | flops 40000000 | bytes 4000000 | tf_op jit(solution)/shard_map/pallas_call | solution.py:233
  23.7 0.0 collective-permute-done.4
  23.7 0.7 %collective-permute-done.5 = f32[16,512]{1,0:T(8,128)S(1)} collective-permute-done((f32[16,512]{1,0:T(8,128)S(1)}, f32[16,512]{1,0:T(8,128)S(1)}, u32[]{:S(2)}, u32[]{:S(2)}) %collective-permute-start.5) | collective-permute-done | bytes 32800 | tf_op jit(solution)/shard_map/ppermute | solution.py:55
  24.4 1.8 %collective-permute-done.6 = f32[16,512]{1,0:T(8,128)S(1)} collective-permute-done((f32[16,512]{1,0:T(8,128)S(1)}, f32[16,512]{1,0:T(8,128)S(1)}, u32[]{:S(2)}, u32[]{:S(2)}) %collective-permute-start.6) | collective-permute-done | bytes 32800 | tf_op jit(solution)/shard_map/ppermute | solution.py:55
  26.2 0.0 all-to-all-done
  26.3 4.0 %collective-permute-start.7 = (f32[16,512]{1,0:T(8,128)S(1)}, f32[16,512]{1,0:T(8,128)S(1)}, u32[]{:S(2)}, u32[]{:S(2)}) collective-permute-start(f32[16,512]{1,0:T(8,128)S(1)} %multiply_add_fusion.1), channel_id=1, source_target_pairs={{0,64},{8,72},{16,80},{24,88},{32,96},{40,104},{48,112},{56,120},{... | collective-permute-start | bytes 98312 | tf_op jit(solution)/shard_map/ppermute | solution.py:55
  30.2 1.0 %collective-permute-start.8 = (f32[16,512]{1,0:T(8,128)S(1)}, f32[16,512]{1,0:T(8,128)S(1)}, u32[]{:S(2)}, u32[]{:S(2)}) collective-permute-start(f32[16,512]{1,0:T(8,128)S(1)} %multiply_add_fusion.1), channel_id=1, source_target_pairs={{0,32},{8,40},{16,48},{24,56},{32,0},{40,8},{48,16},{56,24},{64,96... | collective-permute-start | bytes 98312 | tf_op jit(solution)/shard_map/ppermute | solution.py:55
  31.3 0.0 collective-permute-start.9
  31.3 2.0 %shard_map.50 = (f32[2,256,128]{2,1,0:T(8,128)S(1)}, f32[2,256,128]{2,1,0:T(8,128)S(1)}) custom-call(f32[4,256,128]{2,1,0:T(8,128)S(1)} %get-tuple-element.40.refs_0_, f32[4,256,128]{2,1,0:T(8,128)S(1)} %get-tuple-element.41.refs_1_, f32[16,8,512]{2,1,0:T(8,128)S(1)} %get-tuple-element.42.refs_2_, f32[16,8,512]{2,1,0:T(8,128)S(1)} %get-tuple-element.43.refs_3_, ...), custom_call_target="tpu_custom_call" | custom-call | flops 40000000 | bytes 4000000 | tf_op jit(solution)/shard_map/pallas_call | solution.py:233
  33.3 0.9 %collective-permute-done.8 = f32[16,512]{1,0:T(8,128)S(1)} collective-permute-done((f32[16,512]{1,0:T(8,128)S(1)}, f32[16,512]{1,0:T(8,128)S(1)}, u32[]{:S(2)}, u32[]{:S(2)}) %collective-permute-start.8) | collective-permute-done | bytes 32800 | tf_op jit(solution)/shard_map/ppermute | solution.py:55
  34.2 2.2 %collective-permute-done.9 = f32[16,512]{1,0:T(8,128)S(1)} collective-permute-done((f32[16,512]{1,0:T(8,128)S(1)}, f32[16,512]{1,0:T(8,128)S(1)}, u32[]{:S(2)}, u32[]{:S(2)}) %collective-permute-start.9) | collective-permute-done | bytes 32800 | tf_op jit(solution)/shard_map/ppermute | solution.py:55
  36.4 0.1 multiply_add_fusion.refs_5_
  36.4 2.8 %shard_map.51 = bf16[512,512]{1,0:T(8,128)(2,1)} custom-call(f32[2,256,128]{2,1,0:T(8,128)S(1)} %get-tuple-element.46.refs_0_, f32[2,256,128]{2,1,0:T(8,128)S(1)} %get-tuple-element.47.refs_1_, f32[2,256,128]{2,1,0:T(8,128)S(1)} %get-tuple-element.53.refs_2_, f32[2,256,128]{2,1,0:T(8,128)S(1)} %get-tuple-element.54.refs_3_, bf16[512,512]{1,0:T(8,128)(2,1)S(1)} %bitcast.14, ...), custom_call_target="tpu_custom_call" | custom-call | flops 40000000 | bytes 2000000 | tf_op jit(solution)/shard_map/pallas_call | solution.py:268
  (20 shorter events, 0.2 us)
Async XLA Ops:
  0.0 1.4 %copy-start = (bf16[3,64,4096]{2,1,0:T(8,128)(2,1)S(1)}, bf16[3,64,4096]{2,1,0:T(8,128)(2,1)}, u32[]{:S(2)}) copy-start(bf16[3,64,4096]{2,1,0:T(8,128)(2,1)} %qkv_ref.1) | copy-start | bytes 4718596
  1.4 10.4 %copy-start.1 = (f32[512,16]{0,1:T(8,128)S(1)}, f32[512,16]{0,1:T(8,128)}, u32[]{:S(2)}) copy-start(f32[512,16]{0,1:T(8,128)} %param.6) | copy-start | bytes 98308
  1.4 10.4 %copy-start.2 = (f32[512,16]{0,1:T(8,128)S(1)}, f32[512,16]{0,1:T(8,128)}, u32[]{:S(2)}) copy-start(f32[512,16]{0,1:T(8,128)} %param.5) | copy-start | bytes 98308
  1.8 10.3 %collective-permute-start = (bf16[2,64,512]{2,1,0:T(8,128)(2,1)S(1)}, bf16[2,64,512]{2,1,0:T(8,128)(2,1)S(1)}, u32[]{:S(2)}, u32[]{:S(2)}) collective-permute-start(bf16[2,64,512]{2,1,0:T(8,128)(2,1)S(1)} %get-tuple-element.33), channel_id=1, source_target_pairs={{0,2},{1,3},{2,0},{3,1},{4,6},{5,7},{6,4},{7,5},{8,10},{9,11},{10,... | collective-permute-start | bytes 393224 | tf_op jit(solution)/shard_map/ppermute | solution.py:51
  3.6 9.0 %collective-permute-start.1 = (bf16[2,64,512]{2,1,0:T(8,128)(2,1)S(1)}, bf16[2,64,512]{2,1,0:T(8,128)(2,1)S(1)}, u32[]{:S(2)}, u32[]{:S(2)}) collective-permute-start(bf16[2,64,512]{2,1,0:T(8,128)(2,1)S(1)} %get-tuple-element.34), channel_id=1, source_target_pairs={{0,4},{1,5},{2,6},{3,7},{4,0},{5,1},{6,2},{7,3},{8,12},{9,13},{10,... | collective-permute-start | bytes 393224 | tf_op jit(solution)/shard_map/ppermute | solution.py:51
  6.5 8.2 %collective-permute-start.2 = (bf16[2,64,512]{2,1,0:T(8,128)(2,1)S(1)}, bf16[2,64,512]{2,1,0:T(8,128)(2,1)S(1)}, u32[]{:S(2)}, u32[]{:S(2)}) collective-permute-start(bf16[2,64,512]{2,1,0:T(8,128)(2,1)S(1)} %get-tuple-element.35), channel_id=1, source_target_pairs={{0,6},{1,7},{2,4},{3,5},{4,2},{5,3},{6,0},{7,1},{8,14},{9,15},{10,... | collective-permute-start | bytes 393224 | tf_op jit(solution)/shard_map/ppermute | solution.py:51
  7.4 18.8 %all-to-all-start = ((bf16[8,64,512]{2,1,0:T(8,128)(2,1)}), bf16[8,64,512]{2,1,0:T(8,128)(2,1)S(1)}, u32[]{:S(2)}, u32[]{:S(2)}) async-start(bf16[8,64,512]{2,1,0:T(8,128)(2,1)} %pad_maximum_fusion), calls=%async_computation | async-start | bytes 1048576 | tf_op jit(solution)/shard_map/all_to_all | solution.py:196
  12.1 9.5 %copy-start.3 = (f32[512]{0:T(512)S(1)}, f32[512]{0:T(512)}, u32[]{:S(2)}) copy-start(f32[512]{0:T(512)} %param.7) | copy-start | bytes 6148
  14.7 1.6 %collective-permute-start.3 = (bf16[4,64,512]{2,1,0:T(8,128)(2,1)S(1)}, bf16[4,64,512]{2,1,0:T(8,128)(2,1)S(1)}, u32[]{:S(2)}, u32[]{:S(2)}) collective-permute-start(bf16[4,64,512]{2,1,0:T(8,128)(2,1)S(1)} %pad_maximum_fusion.1), channel_id=1, source_target_pairs={{0,1},{1,0},{2,3},{3,2},{4,5},{5,4},{6,7},{7,6},{8,9},{9,8},{10,11... | collective-permute-start | bytes 786440 | tf_op jit(solution)/shard_map/ppermute | solution.py:47
  17.4 6.3 %collective-permute-start.4 = (f32[16,512]{1,0:T(8,128)S(1)}, f32[16,512]{1,0:T(8,128)S(1)}, u32[]{:S(2)}, u32[]{:S(2)}) collective-permute-start(f32[16,512]{1,0:T(8,128)S(1)} %get-tuple-element.37), channel_id=1, source_target_pairs={{0,16},{8,24},{16,0},{24,8},{32,48},{40,56},{48,32},{56,40},{64,80... | collective-permute-start | bytes 98312 | tf_op jit(solution)/shard_map/ppermute | solution.py:55
  20.5 3.9 %collective-permute-start.5 = (f32[16,512]{1,0:T(8,128)S(1)}, f32[16,512]{1,0:T(8,128)S(1)}, u32[]{:S(2)}, u32[]{:S(2)}) collective-permute-start(f32[16,512]{1,0:T(8,128)S(1)} %get-tuple-element.37), channel_id=1, source_target_pairs={{0,8},{8,0},{16,24},{24,16},{32,40},{40,32},{48,56},{56,48},{64,72... | collective-permute-start | bytes 98312 | tf_op jit(solution)/shard_map/ppermute | solution.py:55
  21.1 5.1 %collective-permute-start.6 = (f32[16,512]{1,0:T(8,128)S(1)}, f32[16,512]{1,0:T(8,128)S(1)}, u32[]{:S(2)}, u32[]{:S(2)}) collective-permute-start(f32[16,512]{1,0:T(8,128)S(1)} %get-tuple-element.37), channel_id=1, source_target_pairs={{0,24},{8,16},{16,8},{24,0},{32,56},{40,48},{48,40},{56,32},{64,88... | collective-permute-start | bytes 98312 | tf_op jit(solution)/shard_map/ppermute | solution.py:55
  26.3 7.0 %collective-permute-start.7 = (f32[16,512]{1,0:T(8,128)S(1)}, f32[16,512]{1,0:T(8,128)S(1)}, u32[]{:S(2)}, u32[]{:S(2)}) collective-permute-start(f32[16,512]{1,0:T(8,128)S(1)} %multiply_add_fusion.1), channel_id=1, source_target_pairs={{0,64},{8,72},{16,80},{24,88},{32,96},{40,104},{48,112},{56,120},{... | collective-permute-start | bytes 98312 | tf_op jit(solution)/shard_map/ppermute | solution.py:55
  30.2 3.9 %collective-permute-start.8 = (f32[16,512]{1,0:T(8,128)S(1)}, f32[16,512]{1,0:T(8,128)S(1)}, u32[]{:S(2)}, u32[]{:S(2)}) collective-permute-start(f32[16,512]{1,0:T(8,128)S(1)} %multiply_add_fusion.1), channel_id=1, source_target_pairs={{0,32},{8,40},{16,48},{24,56},{32,0},{40,8},{48,16},{56,24},{64,96... | collective-permute-start | bytes 98312 | tf_op jit(solution)/shard_map/ppermute | solution.py:55
  31.3 5.1 %collective-permute-start.9 = (f32[16,512]{1,0:T(8,128)S(1)}, f32[16,512]{1,0:T(8,128)S(1)}, u32[]{:S(2)}, u32[]{:S(2)}) collective-permute-start(f32[16,512]{1,0:T(8,128)S(1)} %multiply_add_fusion.1), channel_id=1, source_target_pairs={{0,96},{8,104},{16,112},{24,120},{32,64},{40,72},{48,80},{56,88},{... | collective-permute-start | bytes 98312 | tf_op jit(solution)/shard_map/ppermute | solution.py:55

commit v4 on v3

--- a/solution.py
+++ b/solution.py
@@ -12,6 +12,7 @@
 SUBS = 8
 LANES = 128
 SCALE = 1024.0
+CHIP_ORDER = (2, 1, 3)
 VMEM = pl.BlockSpec(memory_space=pltpu.VMEM)
 PARAMS = pltpu.CompilerParams(vmem_limit_bytes=32 * 1024 * 1024)
 
@@ -70,9 +71,11 @@
     steps = chips * tokens // SUBS
     chip = lax.axis_index("tp") // 2
     for source in range(chips):
+        k = chip ^ source
+        slot = k % 2 * 2 + k // 2
         for group in range(channels // LANES):
             lanes = pl.ds(group * LANES, LANES)
-            drive_ref[group, pl.ds(source * tokens, tokens), :] = decode(code_ref[chip ^ source, :, lanes])
+            drive_ref[group, pl.ds(source * tokens, tokens), :] = decode(code_ref[slot, :, lanes])
     for group in range(channels // LANES):
         lanes = pl.ds(group * LANES, LANES)
         decay = [wide(decay_ref, mode, lanes) for mode in range(modes)]
@@ -190,10 +193,11 @@
         compiler_params=PARAMS,
     )(qkv)
     code, (low, high) = list(outs[:chips]), outs[chips:]
-    for k in (1, 3, 2):
+    for k in CHIP_ORDER:
         code[k] = across_chips(code[k], k)
     query = jnp.concatenate([low, high])
     query = lax.all_to_all(query, "tp", 0, 0).reshape(tokens, channels)
+    code = [code[0]] + [code[k] for k in CHIP_ORDER]
     near_code = jnp.stack([piece[0] for piece in code])
     far_code = across_core(jnp.stack([piece[1] for piece in code]))
 
@@ -251,17 +255,17 @@
         count = jnp.asarray(count)
         return jnp.where(count >= 0, jnp.exp(-rates * jnp.maximum(count, 0).astype(F32)), 0.0)
 
-    others = [across_blocks(block, k) for k in (2, 1, 3)]
+    others = [across_blocks(block, k) for k in CHIP_ORDER]
     others, query, local[0] = lax.optimization_barrier((others, query, local[0]))
     before = jnp.zeros_like(block)
     total = power(tokens * (3 - col)) * block
-    for k, other in zip((2, 1, 3), others):
+    for k, other in zip(CHIP_ORDER, others):
         before = before + power(tokens * (col - 1 - (col ^ k))) * other
         total = total + power(tokens * (3 - (col ^ k))) * other
-    others = [across_blocks(total, 4 * k) for k in (2, 1, 3)]
+    others = [across_blocks(total, 4 * k) for k in CHIP_ORDER]
     others, local[1] = lax.optimization_barrier((others, local[1]))
     carry = jnp.zeros_like(block)
-    for k, other in zip((2, 1, 3), others):
+    for k, other in zip(CHIP_ORDER, others):
         carry = carry + power(4 * tokens * (row - 1 - (row ^ k))) * other
     carry = before + power(tokens * col) * carry
 

time: 39.5 us -> 37 us (0.937)
  waiting for transfers between devices: 8.38 us -> 5.96 us
    ppermute x3, waiting for transfers between devices: 2.44 us -> 0.28 us  [across_chips(): lax.ppermute(value, 'tp', [(i, i ^ 2 * k) for i in range(lax.axis_size('t...]
  transfers between devices with their start and end apart: 11 -> 11, of which waited for: 7 -> 7; matrix products, arithmetic and copies ran while one was open for 3% -> 3% of each run, Pallas kernels for 16% -> 17%
where the time goes in v4:
time: 37 us; the launch traced here: 36.7 us
  starting transfers between devices  18.3 us (49%)
  Pallas kernels  9.46 us (26%)
  waiting for transfers between devices  5.96 us (16%)
  local copies, waits for them, and re-layouts  1.47 us (4%)
  other arithmetic  1.32 us (4%)
    ppermute x6, starting transfers between devices, across_blocks(): lax.ppermute(value, 'ctx', [(i, i ^ bits) for i in range(lax.axis_size('c...  9.28 us
    ppermute x6, waiting for transfers between devices, across_blocks(): lax.ppermute(value, 'ctx', [(i, i ^ bits) for i in range(lax.axis_size('c...  5.62 us
    ppermute x3, starting transfers between devices, across_chips(): lax.ppermute(value, 'tp', [(i, i ^ 2 * k) for i in range(lax.axis_size('t...  4.41 us
    all_to_all x1, starting transfers between devices, per_device(): query = lax.all_to_all(query, 'tp', 0, 0).reshape(tokens, channels)  4.31 us
    pallas_call x2, Pallas kernels, per_device(): pl.pallas_call(functools.partial(local_kernel, modes, begin), in_specs=[V...  4.04 us
    pallas_call x1, Pallas kernels, per_device(): pl.pallas_call(functools.partial(final_kernel, modes), in_specs=[VMEM] *...  2.81 us
    pallas_call x2, Pallas kernels, states(): pl.pallas_call(functools.partial(state_kernel, modes), in_specs=[VMEM] *...  2.21 us
    unnamed x8, local copies, waits for them, and re-layouts  1.42 us
  transfers between devices with their start and end apart: 11, of which 7 were waited for; matrix products, arithmetic and copies ran while one was open for 3% of the time, Pallas kernels for 17%

profile of v4, /device:TPU:0, one launch (start us, length us, event | category | flops | bytes accessed | tf_op | source)
XLA Modules:
  0.0 36.7 jit_solution(17499304224499939384)
XLA Ops:
  0.0 1.4 %copy-done = bf16[3,64,4096]{2,1,0:T(8,128)(2,1)S(1)} copy-done((bf16[3,64,4096]{2,1,0:T(8,128)(2,1)S(1)}, bf16[3,64,4096]{2,1,0:T(8,128)(2,1)}, u32[]{:S(2)}) %copy-start) | copy-done | bytes 1572888
  1.4 0.4 %shard_map.46 = (bf16[2,64,512]{2,1,0:T(8,128)(2,1)S(1)}, bf16[2,64,512]{2,1,0:T(8,128)(2,1)S(1)}, bf16[2,64,512]{2,1,0:T(8,128)(2,1)S(1)}, bf16[2,64,512]{2,1,0...) custom-call(bf16[3,64,4096]{2,1,0:T(8,128)(2,1)S(1)} %copy-done), custom_call_target="tpu_custom_call" | custom-call | tf_op jit(solution)/shard_map/pallas_call | solution.py:187
  1.8 3.4 %collective-permute-start = (bf16[2,64,512]{2,1,0:T(8,128)(2,1)S(1)}, bf16[2,64,512]{2,1,0:T(8,128)(2,1)S(1)}, u32[]{:S(2)}, u32[]{:S(2)}) collective-permute-start(bf16[2,64,512]{2,1,0:T(8,128)(2,1)S(1)} %get-tuple-element.33), channel_id=1, source_target_pairs={{0,4},{1,5},{2,6},{3,7},{4,0},{5,1},{6,2},{7,3},{8,12},{9,13},{10,... | collective-permute-start | bytes 393224 | tf_op jit(solution)/shard_map/ppermute | solution.py:52
  5.2 0.7 %collective-permute-start.1 = (bf16[2,64,512]{2,1,0:T(8,128)(2,1)S(1)}, bf16[2,64,512]{2,1,0:T(8,128)(2,1)S(1)}, u32[]{:S(2)}, u32[]{:S(2)}) collective-permute-start(bf16[2,64,512]{2,1,0:T(8,128)(2,1)S(1)} %get-tuple-element.34), channel_id=1, source_target_pairs={{0,2},{1,3},{2,0},{3,1},{4,6},{5,7},{6,4},{7,5},{8,10},{9,11},{10,... | collective-permute-start | bytes 393224 | tf_op jit(solution)/shard_map/ppermute | solution.py:52
  5.9 0.4 %collective-permute-start.2 = (bf16[2,64,512]{2,1,0:T(8,128)(2,1)S(1)}, bf16[2,64,512]{2,1,0:T(8,128)(2,1)S(1)}, u32[]{:S(2)}, u32[]{:S(2)}) collective-permute-start(bf16[2,64,512]{2,1,0:T(8,128)(2,1)S(1)} %get-tuple-element.35), channel_id=1, source_target_pairs={{0,6},{1,7},{2,4},{3,5},{4,2},{5,3},{6,0},{7,1},{8,14},{9,15},{10,... | collective-permute-start | bytes 393224 | tf_op jit(solution)/shard_map/ppermute | solution.py:52
  6.2 0.8 %pad_maximum_fusion = bf16[8,64,512]{2,1,0:T(8,128)(2,1)} fusion(bf16[4,64,512]{2,1,0:T(8,128)(2,1)S(1)} %get-tuple-element.39, bf16[4,64,512]{2,1,0:T(8,128)(2,1)S(1)} %get-tuple-element.38), kind=kLoop, calls=%fused_computation | loop fusion | flops 262144 | bytes 1048576 | tf_op jit(solution)/shard_map/concatenate | solution.py:198
  7.1 4.3 %all-to-all-start = ((bf16[8,64,512]{2,1,0:T(8,128)(2,1)}), bf16[8,64,512]{2,1,0:T(8,128)(2,1)S(1)}, u32[]{:S(2)}, u32[]{:S(2)}) async-start(bf16[8,64,512]{2,1,0:T(8,128)(2,1)} %pad_maximum_fusion), calls=%async_computation | async-start | bytes 1048576 | tf_op jit(solution)/shard_map/all_to_all | solution.py:199
  11.5 0.2 exponential_multiply_fusion
  11.7 0.0 copy-start.3
  11.7 0.0 collective-permute-done
  11.8 0.1 collective-permute-done.1
  11.9 0.2 collective-permute-done.2
  12.1 0.3 collective-permute-start.3
  12.5 1.1 %shard_map.47 = (f32[4,256,128]{2,1,0:T(8,128)S(1)}, f32[16,8,512]{2,1,0:T(8,128)S(1)}, f32[16,512]{1,0:T(8,128)S(1)}) custom-call(bf16[4,64,512]{2,1,0:T(8,128)(2,1)S(1)} %pad_maximum_fusion.2.code_ref, f32[16,512]{1,0:T(8,128)S(1)} %get-tuple-element.74.decay_ref.refs_4_.refs_8_, f32[16,8,512]{2,1,0:T(8,128)S(1)} %get-tuple-element.69.tail_ref, ...), custom_call_target="tpu_custom_call" | custom-call | flops 1000 | bytes 1000 | tf_op jit(solution)/shard_map/pallas_call | solution.py:220
  13.7 0.1 collective-permute-done.3.code_ref
  13.7 1.1 %shard_map.48 = (f32[4,256,128]{2,1,0:T(8,128)S(1)}, f32[16,8,512]{2,1,0:T(8,128)S(1)}, f32[16,512]{1,0:T(8,128)S(1)}) custom-call(bf16[4,64,512]{2,1,0:T(8,128)(2,1)S(1)} %collective-permute-done.3.code_ref, f32[16,512]{1,0:T(8,128)S(1)} %get-tuple-element.74.decay_ref.refs_4_.refs_8_, f32[16,8,512]{2,1,0:T(8,128)S(1)} %get-tuple-element.70.tail_ref, ...), custom_call_target="tpu_custom_call" | custom-call | flops 1000 | bytes 1000 | tf_op jit(solution)/shard_map/pallas_call | solution.py:220
  14.8 3.2 %collective-permute-start.4 = (f32[16,512]{1,0:T(8,128)S(1)}, f32[16,512]{1,0:T(8,128)S(1)}, u32[]{:S(2)}, u32[]{:S(2)}) collective-permute-start(f32[16,512]{1,0:T(8,128)S(1)} %get-tuple-element.37), channel_id=1, source_target_pairs={{0,16},{8,24},{16,0},{24,8},{32,48},{40,56},{48,32},{56,40},{64,80... | collective-permute-start | bytes 98312 | tf_op jit(solution)/shard_map/ppermute | solution.py:56
  18.0 0.6 %collective-permute-start.5 = (f32[16,512]{1,0:T(8,128)S(1)}, f32[16,512]{1,0:T(8,128)S(1)}, u32[]{:S(2)}, u32[]{:S(2)}) collective-permute-start(f32[16,512]{1,0:T(8,128)S(1)} %get-tuple-element.37), channel_id=1, source_target_pairs={{0,8},{8,0},{16,24},{24,16},{32,40},{40,32},{48,56},{56,48},{64,72... | collective-permute-start | bytes 98312 | tf_op jit(solution)/shard_map/ppermute | solution.py:56
  18.6 0.6 %collective-permute-start.6 = (f32[16,512]{1,0:T(8,128)S(1)}, f32[16,512]{1,0:T(8,128)S(1)}, u32[]{:S(2)}, u32[]{:S(2)}) collective-permute-start(f32[16,512]{1,0:T(8,128)S(1)} %get-tuple-element.37), channel_id=1, source_target_pairs={{0,24},{8,16},{16,8},{24,0},{32,56},{40,48},{48,40},{56,32},{64,88... | collective-permute-start | bytes 98312 | tf_op jit(solution)/shard_map/ppermute | solution.py:56
  19.1 2.0 %shard_map.49 = (f32[2,256,128]{2,1,0:T(8,128)S(1)}, f32[2,256,128]{2,1,0:T(8,128)S(1)}) custom-call(f32[4,256,128]{2,1,0:T(8,128)S(1)} %get-tuple-element.40.refs_0_, f32[4,256,128]{2,1,0:T(8,128)S(1)} %get-tuple-element.41.refs_1_, f32[16,8,512]{2,1,0:T(8,128)S(1)} %get-tuple-element.42.refs_2_, f32[16,8,512]{2,1,0:T(8,128)S(1)} %get-tuple-element.43.refs_3_, ...), custom_call_target="tpu_custom_call" | custom-call | flops 40000000 | bytes 4000000 | tf_op jit(solution)/shard_map/pallas_call | solution.py:237
  21.2 0.0 collective-permute-done.4
  21.2 0.7 %collective-permute-done.5 = f32[16,512]{1,0:T(8,128)S(1)} collective-permute-done((f32[16,512]{1,0:T(8,128)S(1)}, f32[16,512]{1,0:T(8,128)S(1)}, u32[]{:S(2)}, u32[]{:S(2)}) %collective-permute-start.5) | collective-permute-done | bytes 32800 | tf_op jit(solution)/shard_map/ppermute | solution.py:56
  21.9 1.8 %collective-permute-done.6 = f32[16,512]{1,0:T(8,128)S(1)} collective-permute-done((f32[16,512]{1,0:T(8,128)S(1)}, f32[16,512]{1,0:T(8,128)S(1)}, u32[]{:S(2)}, u32[]{:S(2)}) %collective-permute-start.6) | collective-permute-done | bytes 32800 | tf_op jit(solution)/shard_map/ppermute | solution.py:56
  23.7 4.0 %collective-permute-start.7 = (f32[16,512]{1,0:T(8,128)S(1)}, f32[16,512]{1,0:T(8,128)S(1)}, u32[]{:S(2)}, u32[]{:S(2)}) collective-permute-start(f32[16,512]{1,0:T(8,128)S(1)} %multiply_add_fusion.1), channel_id=1, source_target_pairs={{0,64},{8,72},{16,80},{24,88},{32,96},{40,104},{48,112},{56,120},{... | collective-permute-start | bytes 98312 | tf_op jit(solution)/shard_map/ppermute | solution.py:56
  27.7 1.0 %collective-permute-start.8 = (f32[16,512]{1,0:T(8,128)S(1)}, f32[16,512]{1,0:T(8,128)S(1)}, u32[]{:S(2)}, u32[]{:S(2)}) collective-permute-start(f32[16,512]{1,0:T(8,128)S(1)} %multiply_add_fusion.1), channel_id=1, source_target_pairs={{0,32},{8,40},{16,48},{24,56},{32,0},{40,8},{48,16},{56,24},{64,96... | collective-permute-start | bytes 98312 | tf_op jit(solution)/shard_map/ppermute | solution.py:56
  28.7 0.0 collective-permute-start.9
  28.7 2.0 %shard_map.50 = (f32[2,256,128]{2,1,0:T(8,128)S(1)}, f32[2,256,128]{2,1,0:T(8,128)S(1)}) custom-call(f32[4,256,128]{2,1,0:T(8,128)S(1)} %get-tuple-element.40.refs_0_, f32[4,256,128]{2,1,0:T(8,128)S(1)} %get-tuple-element.41.refs_1_, f32[16,8,512]{2,1,0:T(8,128)S(1)} %get-tuple-element.42.refs_2_, f32[16,8,512]{2,1,0:T(8,128)S(1)} %get-tuple-element.43.refs_3_, ...), custom_call_target="tpu_custom_call" | custom-call | flops 40000000 | bytes 4000000 | tf_op jit(solution)/shard_map/pallas_call | solution.py:237
  30.8 0.0 collective-permute-done.7
  30.8 0.9 %collective-permute-done.8 = f32[16,512]{1,0:T(8,128)S(1)} collective-permute-done((f32[16,512]{1,0:T(8,128)S(1)}, f32[16,512]{1,0:T(8,128)S(1)}, u32[]{:S(2)}, u32[]{:S(2)}) %collective-permute-start.8) | collective-permute-done | bytes 32800 | tf_op jit(solution)/shard_map/ppermute | solution.py:56
  31.6 2.2 %collective-permute-done.9 = f32[16,512]{1,0:T(8,128)S(1)} collective-permute-done((f32[16,512]{1,0:T(8,128)S(1)}, f32[16,512]{1,0:T(8,128)S(1)}, u32[]{:S(2)}, u32[]{:S(2)}) %collective-permute-start.9) | collective-permute-done | bytes 32800 | tf_op jit(solution)/shard_map/ppermute | solution.py:56
  33.8 0.1 multiply_add_fusion.refs_5_
  33.9 2.8 %shard_map.51 = bf16[512,512]{1,0:T(8,128)(2,1)} custom-call(f32[2,256,128]{2,1,0:T(8,128)S(1)} %get-tuple-element.46.refs_0_, f32[2,256,128]{2,1,0:T(8,128)S(1)} %get-tuple-element.47.refs_1_, f32[2,256,128]{2,1,0:T(8,128)S(1)} %get-tuple-element.53.refs_2_, f32[2,256,128]{2,1,0:T(8,128)S(1)} %get-tuple-element.54.refs_3_, bf16[512,512]{1,0:T(8,128)(2,1)S(1)} %bitcast.14, ...), custom_call_target="tpu_custom_call" | custom-call | flops 40000000 | bytes 2000000 | tf_op jit(solution)/shard_map/pallas_call | solution.py:272
  (20 shorter events, 0.2 us)
Async XLA Ops:
  0.0 1.4 %copy-start = (bf16[3,64,4096]{2,1,0:T(8,128)(2,1)S(1)}, bf16[3,64,4096]{2,1,0:T(8,128)(2,1)}, u32[]{:S(2)}) copy-start(bf16[3,64,4096]{2,1,0:T(8,128)(2,1)} %qkv_ref.1) | copy-start | bytes 4718596
  1.4 10.0 %copy-start.1 = (f32[512,16]{0,1:T(8,128)S(1)}, f32[512,16]{0,1:T(8,128)}, u32[]{:S(2)}) copy-start(f32[512,16]{0,1:T(8,128)} %param.6) | copy-start | bytes 98308
  1.4 10.0 %copy-start.2 = (f32[512,16]{0,1:T(8,128)S(1)}, f32[512,16]{0,1:T(8,128)}, u32[]{:S(2)}) copy-start(f32[512,16]{0,1:T(8,128)} %param.5) | copy-start | bytes 98308
  1.8 9.9 %collective-permute-start = (bf16[2,64,512]{2,1,0:T(8,128)(2,1)S(1)}, bf16[2,64,512]{2,1,0:T(8,128)(2,1)S(1)}, u32[]{:S(2)}, u32[]{:S(2)}) collective-permute-start(bf16[2,64,512]{2,1,0:T(8,128)(2,1)S(1)} %get-tuple-element.33), channel_id=1, source_target_pairs={{0,4},{1,5},{2,6},{3,7},{4,0},{5,1},{6,2},{7,3},{8,12},{9,13},{10,... | collective-permute-start | bytes 393224 | tf_op jit(solution)/shard_map/ppermute | solution.py:52
  5.2 6.7 %collective-permute-start.1 = (bf16[2,64,512]{2,1,0:T(8,128)(2,1)S(1)}, bf16[2,64,512]{2,1,0:T(8,128)(2,1)S(1)}, u32[]{:S(2)}, u32[]{:S(2)}) collective-permute-start(bf16[2,64,512]{2,1,0:T(8,128)(2,1)S(1)} %get-tuple-element.34), channel_id=1, source_target_pairs={{0,2},{1,3},{2,0},{3,1},{4,6},{5,7},{6,4},{7,5},{8,10},{9,11},{10,... | collective-permute-start | bytes 393224 | tf_op jit(solution)/shard_map/ppermute | solution.py:52
  5.9 6.2 %collective-permute-start.2 = (bf16[2,64,512]{2,1,0:T(8,128)(2,1)S(1)}, bf16[2,64,512]{2,1,0:T(8,128)(2,1)S(1)}, u32[]{:S(2)}, u32[]{:S(2)}) collective-permute-start(bf16[2,64,512]{2,1,0:T(8,128)(2,1)S(1)} %get-tuple-element.35), channel_id=1, source_target_pairs={{0,6},{1,7},{2,4},{3,5},{4,2},{5,3},{6,0},{7,1},{8,14},{9,15},{10,... | collective-permute-start | bytes 393224 | tf_op jit(solution)/shard_map/ppermute | solution.py:52
  7.1 16.6 %all-to-all-start = ((bf16[8,64,512]{2,1,0:T(8,128)(2,1)}), bf16[8,64,512]{2,1,0:T(8,128)(2,1)S(1)}, u32[]{:S(2)}, u32[]{:S(2)}) async-start(bf16[8,64,512]{2,1,0:T(8,128)(2,1)} %pad_maximum_fusion), calls=%async_computation | async-start | bytes 1048576 | tf_op jit(solution)/shard_map/all_to_all | solution.py:199
  11.7 7.4 %copy-start.3 = (f32[512]{0:T(512)S(1)}, f32[512]{0:T(512)}, u32[]{:S(2)}) copy-start(f32[512]{0:T(512)} %param.7) | copy-start | bytes 6148
  12.1 1.6 %collective-permute-start.3 = (bf16[4,64,512]{2,1,0:T(8,128)(2,1)S(1)}, bf16[4,64,512]{2,1,0:T(8,128)(2,1)S(1)}, u32[]{:S(2)}, u32[]{:S(2)}) collective-permute-start(bf16[4,64,512]{2,1,0:T(8,128)(2,1)S(1)} %pad_maximum_fusion.1), channel_id=1, source_target_pairs={{0,1},{1,0},{2,3},{3,2},{4,5},{5,4},{6,7},{7,6},{8,9},{9,8},{10,11... | collective-permute-start | bytes 786440 | tf_op jit(solution)/shard_map/ppermute | solution.py:48
  14.8 6.3 %collective-permute-start.4 = (f32[16,512]{1,0:T(8,128)S(1)}, f32[16,512]{1,0:T(8,128)S(1)}, u32[]{:S(2)}, u32[]{:S(2)}) collective-permute-start(f32[16,512]{1,0:T(8,128)S(1)} %get-tuple-element.37), channel_id=1, source_target_pairs={{0,16},{8,24},{16,0},{24,8},{32,48},{40,56},{48,32},{56,40},{64,80... | collective-permute-start | bytes 98312 | tf_op jit(solution)/shard_map/ppermute | solution.py:56
  18.0 3.9 %collective-permute-start.5 = (f32[16,512]{1,0:T(8,128)S(1)}, f32[16,512]{1,0:T(8,128)S(1)}, u32[]{:S(2)}, u32[]{:S(2)}) collective-permute-start(f32[16,512]{1,0:T(8,128)S(1)} %get-tuple-element.37), channel_id=1, source_target_pairs={{0,8},{8,0},{16,24},{24,16},{32,40},{40,32},{48,56},{56,48},{64,72... | collective-permute-start | bytes 98312 | tf_op jit(solution)/shard_map/ppermute | solution.py:56
  18.6 5.1 %collective-permute-start.6 = (f32[16,512]{1,0:T(8,128)S(1)}, f32[16,512]{1,0:T(8,128)S(1)}, u32[]{:S(2)}, u32[]{:S(2)}) collective-permute-start(f32[16,512]{1,0:T(8,128)S(1)} %get-tuple-element.37), channel_id=1, source_target_pairs={{0,24},{8,16},{16,8},{24,0},{32,56},{40,48},{48,40},{56,32},{64,88... | collective-permute-start | bytes 98312 | tf_op jit(solution)/shard_map/ppermute | solution.py:56
  23.7 7.0 %collective-permute-start.7 = (f32[16,512]{1,0:T(8,128)S(1)}, f32[16,512]{1,0:T(8,128)S(1)}, u32[]{:S(2)}, u32[]{:S(2)}) collective-permute-start(f32[16,512]{1,0:T(8,128)S(1)} %multiply_add_fusion.1), channel_id=1, source_target_pairs={{0,64},{8,72},{16,80},{24,88},{32,96},{40,104},{48,112},{56,120},{... | collective-permute-start | bytes 98312 | tf_op jit(solution)/shard_map/ppermute | solution.py:56
  27.7 3.9 %collective-permute-start.8 = (f32[16,512]{1,0:T(8,128)S(1)}, f32[16,512]{1,0:T(8,128)S(1)}, u32[]{:S(2)}, u32[]{:S(2)}) collective-permute-start(f32[16,512]{1,0:T(8,128)S(1)} %multiply_add_fusion.1), channel_id=1, source_target_pairs={{0,32},{8,40},{16,48},{24,56},{32,0},{40,8},{48,16},{56,24},{64,96... | collective-permute-start | bytes 98312 | tf_op jit(solution)/shard_map/ppermute | solution.py:56
  28.7 5.1 %collective-permute-start.9 = (f32[16,512]{1,0:T(8,128)S(1)}, f32[16,512]{1,0:T(8,128)S(1)}, u32[]{:S(2)}, u32[]{:S(2)}) collective-permute-start(f32[16,512]{1,0:T(8,128)S(1)} %multiply_add_fusion.1), channel_id=1, source_target_pairs={{0,96},{8,104},{16,112},{24,120},{32,64},{40,72},{48,80},{56,88},{... | collective-permute-start | bytes 98312 | tf_op jit(solution)/shard_map/ppermute | solution.py:56

commit v5 on v4

--- a/solution.py
+++ b/solution.py
@@ -75,17 +75,20 @@
         slot = k % 2 * 2 + k // 2
         for group in range(channels // LANES):
             lanes = pl.ds(group * LANES, LANES)
-            drive_ref[group, pl.ds(source * tokens, tokens), :] = decode(code_ref[slot, :, lanes])
+            drive = decode(code_ref[slot, :, lanes])
+            for sub in range(SUBS * source // chips, SUBS * (source + 1) // chips):
+                at = sub * steps - source * tokens
+                drive_ref[group, pl.ds(sub, steps, stride=SUBS), :] = drive[at : at + steps]
     for group in range(channels // LANES):
         lanes = pl.ds(group * LANES, LANES)
         decay = [wide(decay_ref, mode, lanes) for mode in range(modes)]
 
         def step(i, states):
-            x = drive_ref[group, pl.ds(i, SUBS, stride=steps), :]
+            x = drive_ref[group, pl.ds(pl.multiple_of(i * SUBS, SUBS), SUBS), :]
             return [states[m] * decay[m] + x for m in range(modes)]
 
         zero = jnp.zeros((SUBS, LANES), F32)
-        states = lax.fori_loop(0, steps, step, [zero] * modes, unroll=8)
+        states = lax.fori_loop(0, steps, step, [zero] * modes, unroll=steps)
         for mode in range(modes):
             sub_ref[mode, :, lanes] = states[mode]
             block_ref[mode : mode + 1, lanes] = earlier_ref[mode : mode + 1, lanes] + jnp.sum(
@@ -130,13 +133,13 @@
         for part, (drive_ref, out_ref) in enumerate(zip(drive_refs, out_refs)):
 
             def step(i, states):
-                at = pl.ds(i, SUBS, stride=steps)
+                at = pl.ds(pl.multiple_of(i * SUBS, SUBS), SUBS)
                 x = drive_ref[begin + group, at, :]
                 states = [states[m] * decay[m] + x for m in range(modes)]
                 out_ref[group, at, :] = total_of([states[m] * weight[m] for m in range(modes)] + [skip * x])
                 return states
 
-            lax.fori_loop(0, steps, step, [start[part] for start in starts], unroll=4)
+            lax.fori_loop(0, steps, step, [start[part] for start in starts], unroll=8)
 
 
 def final_kernel(modes, *refs):
@@ -158,14 +161,15 @@
             first = [start_ref[mode, :, lanes] * wide(carry_ref, mode, lanes) for mode in range(modes)]
 
             def step(i, states):
-                at = pl.ds(i, SUBS, stride=steps)
+                at = pl.ds(pl.multiple_of(i * SUBS, SUBS), SUBS)
                 sum_ref[core ^ part, group, at, :] = total_of([local_ref[group % (groups // 2), at, :]] + states)
                 return [states[m] * decay[m] for m in range(modes)]
 
-            lax.fori_loop(0, steps, step, first, unroll=8)
+            lax.fori_loop(0, steps, step, first, unroll=steps)
         for tile in range(2 * tokens // LANES):
             rows = pl.ds(tile * LANES, LANES)
-            mixed = jnp.concatenate([sum_ref[part, group, pl.ds(tile * LANES // 2, LANES // 2), :] for part in range(2)])
+            subs = [sum_ref[part, group, pl.ds(2 * tile + j, steps, stride=SUBS), :] for part in range(2) for j in range(2)]
+            mixed = jnp.concatenate(subs)
             gated = mixed * query_ref[rows, lanes].astype(F32)
             held_ref[group, :, rows] = gated.T.astype(BF16)
         copy_out(group).start()

time: 37 us -> 36 us (0.973)
  Pallas kernels: 9.46 us -> 6.95 us
  waiting for transfers between devices: 5.96 us -> 7.5 us
    ppermute x6, waiting for transfers between devices: 5.62 us -> 6.9 us  [across_blocks(): lax.ppermute(value, 'ctx', [(i, i ^ bits) for i in range(lax.axis_size('c...]
    pallas_call x2, Pallas kernels: 4.04 us -> 2.77 us  [per_device(): pl.pallas_call(functools.partial(local_kernel, modes, begin), in_specs=[V...]
    pallas_call x1, Pallas kernels: 2.81 us -> 2.09 us  [per_device(): pl.pallas_call(functools.partial(final_kernel, modes), in_specs=[VMEM] *...]
    pallas_call x2, Pallas kernels: 2.21 us -> 1.69 us  [states(): pl.pallas_call(functools.partial(state_kernel, modes), in_specs=[VMEM] *...]
  transfers between devices with their start and end apart: 11 -> 11, of which waited for: 7 -> 7; matrix products, arithmetic and copies ran while one was open for 3% -> 4% of each run, Pallas kernels for 17% -> 12%
where the time goes in v5:
time: 36 us; the launch traced here: 35.7 us
  starting transfers between devices  18.3 us (51%)
  waiting for transfers between devices  7.5 us (21%)
  Pallas kernels  6.95 us (19%)
  local copies, waits for them, and re-layouts  1.47 us (4%)
  other arithmetic  1.32 us (4%)
    ppermute x6, starting transfers between devices, across_blocks(): lax.ppermute(value, 'ctx', [(i, i ^ bits) for i in range(lax.axis_size('c...  9.28 us
    ppermute x6, waiting for transfers between devices, across_blocks(): lax.ppermute(value, 'ctx', [(i, i ^ bits) for i in range(lax.axis_size('c...  6.9 us
    ppermute x3, starting transfers between devices, across_chips(): lax.ppermute(value, 'tp', [(i, i ^ 2 * k) for i in range(lax.axis_size('t...  4.41 us
    all_to_all x1, starting transfers between devices, per_device(): query = lax.all_to_all(query, 'tp', 0, 0).reshape(tokens, channels)  4.31 us
    pallas_call x2, Pallas kernels, per_device(): pl.pallas_call(functools.partial(local_kernel, modes, begin), in_specs=[V...  2.77 us
    pallas_call x1, Pallas kernels, per_device(): pl.pallas_call(functools.partial(final_kernel, modes), in_specs=[VMEM] *...  2.09 us
    pallas_call x2, Pallas kernels, states(): pl.pallas_call(functools.partial(state_kernel, modes), in_specs=[VMEM] *...  1.69 us
    unnamed x8, local copies, waits for them, and re-layouts  1.42 us
  transfers between devices with their start and end apart: 11, of which 7 were waited for; matrix products, arithmetic and copies ran while one was open for 4% of the time, Pallas kernels for 12%

profile of v5, /device:TPU:0, one launch (start us, length us, event | category | flops | bytes accessed | tf_op | source)
XLA Modules:
  0.0 35.7 jit_solution(1552028383450537720)
XLA Ops:
  0.0 1.4 %copy-done = bf16[3,64,4096]{2,1,0:T(8,128)(2,1)S(1)} copy-done((bf16[3,64,4096]{2,1,0:T(8,128)(2,1)S(1)}, bf16[3,64,4096]{2,1,0:T(8,128)(2,1)}, u32[]{:S(2)}) %copy-start) | copy-done | bytes 1572888
  1.4 0.4 %shard_map.46 = (bf16[2,64,512]{2,1,0:T(8,128)(2,1)S(1)}, bf16[2,64,512]{2,1,0:T(8,128)(2,1)S(1)}, bf16[2,64,512]{2,1,0:T(8,128)(2,1)S(1)}, bf16[2,64,512]{2,1,0...) custom-call(bf16[3,64,4096]{2,1,0:T(8,128)(2,1)S(1)} %copy-done), custom_call_target="tpu_custom_call" | custom-call | tf_op jit(solution)/shard_map/pallas_call | solution.py:191
  1.8 3.4 %collective-permute-start = (bf16[2,64,512]{2,1,0:T(8,128)(2,1)S(1)}, bf16[2,64,512]{2,1,0:T(8,128)(2,1)S(1)}, u32[]{:S(2)}, u32[]{:S(2)}) collective-permute-start(bf16[2,64,512]{2,1,0:T(8,128)(2,1)S(1)} %get-tuple-element.33), channel_id=1, source_target_pairs={{0,4},{1,5},{2,6},{3,7},{4,0},{5,1},{6,2},{7,3},{8,12},{9,13},{10,... | collective-permute-start | bytes 393224 | tf_op jit(solution)/shard_map/ppermute | solution.py:52
  5.2 0.7 %collective-permute-start.1 = (bf16[2,64,512]{2,1,0:T(8,128)(2,1)S(1)}, bf16[2,64,512]{2,1,0:T(8,128)(2,1)S(1)}, u32[]{:S(2)}, u32[]{:S(2)}) collective-permute-start(bf16[2,64,512]{2,1,0:T(8,128)(2,1)S(1)} %get-tuple-element.34), channel_id=1, source_target_pairs={{0,2},{1,3},{2,0},{3,1},{4,6},{5,7},{6,4},{7,5},{8,10},{9,11},{10,... | collective-permute-start | bytes 393224 | tf_op jit(solution)/shard_map/ppermute | solution.py:52
  5.9 0.4 %collective-permute-start.2 = (bf16[2,64,512]{2,1,0:T(8,128)(2,1)S(1)}, bf16[2,64,512]{2,1,0:T(8,128)(2,1)S(1)}, u32[]{:S(2)}, u32[]{:S(2)}) collective-permute-start(bf16[2,64,512]{2,1,0:T(8,128)(2,1)S(1)} %get-tuple-element.35), channel_id=1, source_target_pairs={{0,6},{1,7},{2,4},{3,5},{4,2},{5,3},{6,0},{7,1},{8,14},{9,15},{10,... | collective-permute-start | bytes 393224 | tf_op jit(solution)/shard_map/ppermute | solution.py:52
  6.2 0.8 %pad_maximum_fusion = bf16[8,64,512]{2,1,0:T(8,128)(2,1)} fusion(bf16[4,64,512]{2,1,0:T(8,128)(2,1)S(1)} %get-tuple-element.39, bf16[4,64,512]{2,1,0:T(8,128)(2,1)S(1)} %get-tuple-element.38), kind=kLoop, calls=%fused_computation | loop fusion | flops 262144 | bytes 1048576 | tf_op jit(solution)/shard_map/concatenate | solution.py:202
  7.1 4.3 %all-to-all-start = ((bf16[8,64,512]{2,1,0:T(8,128)(2,1)}), bf16[8,64,512]{2,1,0:T(8,128)(2,1)S(1)}, u32[]{:S(2)}, u32[]{:S(2)}) async-start(bf16[8,64,512]{2,1,0:T(8,128)(2,1)} %pad_maximum_fusion), calls=%async_computation | async-start | bytes 1048576 | tf_op jit(solution)/shard_map/all_to_all | solution.py:203
  11.5 0.2 exponential_multiply_fusion
  11.7 0.0 copy-start.3
  11.7 0.0 collective-permute-done
  11.8 0.1 collective-permute-done.1
  11.9 0.2 collective-permute-done.2
  12.1 0.3 collective-permute-start.3
  12.5 0.9 %shard_map.47 = (f32[4,256,128]{2,1,0:T(8,128)S(1)}, f32[16,8,512]{2,1,0:T(8,128)S(1)}, f32[16,512]{1,0:T(8,128)S(1)}) custom-call(bf16[4,64,512]{2,1,0:T(8,128)(2,1)S(1)} %pad_maximum_fusion.2.code_ref, f32[16,512]{1,0:T(8,128)S(1)} %get-tuple-element.74.decay_ref.refs_4_.refs_8_, f32[16,8,512]{2,1,0:T(8,128)S(1)} %get-tuple-element.69.tail_ref, ...), custom_call_target="tpu_custom_call" | custom-call | flops 1000 | bytes 1000 | tf_op jit(solution)/shard_map/pallas_call | solution.py:224
  13.4 0.3 collective-permute-done.3.code_ref
  13.7 0.8 %shard_map.48 = (f32[4,256,128]{2,1,0:T(8,128)S(1)}, f32[16,8,512]{2,1,0:T(8,128)S(1)}, f32[16,512]{1,0:T(8,128)S(1)}) custom-call(bf16[4,64,512]{2,1,0:T(8,128)(2,1)S(1)} %collective-permute-done.3.code_ref, f32[16,512]{1,0:T(8,128)S(1)} %get-tuple-element.74.decay_ref.refs_4_.refs_8_, f32[16,8,512]{2,1,0:T(8,128)S(1)} %get-tuple-element.70.tail_ref, ...), custom_call_target="tpu_custom_call" | custom-call | flops 1000 | bytes 1000 | tf_op jit(solution)/shard_map/pallas_call | solution.py:224
  14.6 3.2 %collective-permute-start.4 = (f32[16,512]{1,0:T(8,128)S(1)}, f32[16,512]{1,0:T(8,128)S(1)}, u32[]{:S(2)}, u32[]{:S(2)}) collective-permute-start(f32[16,512]{1,0:T(8,128)S(1)} %get-tuple-element.37), channel_id=1, source_target_pairs={{0,16},{8,24},{16,0},{24,8},{32,48},{40,56},{48,32},{56,40},{64,80... | collective-permute-start | bytes 98312 | tf_op jit(solution)/shard_map/ppermute | solution.py:56
  17.7 0.6 %collective-permute-start.5 = (f32[16,512]{1,0:T(8,128)S(1)}, f32[16,512]{1,0:T(8,128)S(1)}, u32[]{:S(2)}, u32[]{:S(2)}) collective-permute-start(f32[16,512]{1,0:T(8,128)S(1)} %get-tuple-element.37), channel_id=1, source_target_pairs={{0,8},{8,0},{16,24},{24,16},{32,40},{40,32},{48,56},{56,48},{64,72... | collective-permute-start | bytes 98312 | tf_op jit(solution)/shard_map/ppermute | solution.py:56
  18.3 0.6 %collective-permute-start.6 = (f32[16,512]{1,0:T(8,128)S(1)}, f32[16,512]{1,0:T(8,128)S(1)}, u32[]{:S(2)}, u32[]{:S(2)}) collective-permute-start(f32[16,512]{1,0:T(8,128)S(1)} %get-tuple-element.37), channel_id=1, source_target_pairs={{0,24},{8,16},{16,8},{24,0},{32,56},{40,48},{48,40},{56,32},{64,88... | collective-permute-start | bytes 98312 | tf_op jit(solution)/shard_map/ppermute | solution.py:56
  18.9 1.4 %shard_map.49 = (f32[2,256,128]{2,1,0:T(8,128)S(1)}, f32[2,256,128]{2,1,0:T(8,128)S(1)}) custom-call(f32[4,256,128]{2,1,0:T(8,128)S(1)} %get-tuple-element.40.refs_0_, f32[4,256,128]{2,1,0:T(8,128)S(1)} %get-tuple-element.41.refs_1_, f32[16,8,512]{2,1,0:T(8,128)S(1)} %get-tuple-element.42.refs_2_, f32[16,8,512]{2,1,0:T(8,128)S(1)} %get-tuple-element.43.refs_3_, ...), custom_call_target="tpu_custom_call" | custom-call | flops 40000000 | bytes 4000000 | tf_op jit(solution)/shard_map/pallas_call | solution.py:241
  20.3 0.0 collective-permute-done.4
  20.3 1.4 %collective-permute-done.5 = f32[16,512]{1,0:T(8,128)S(1)} collective-permute-done((f32[16,512]{1,0:T(8,128)S(1)}, f32[16,512]{1,0:T(8,128)S(1)}, u32[]{:S(2)}, u32[]{:S(2)}) %collective-permute-start.5) | collective-permute-done | bytes 32800 | tf_op jit(solution)/shard_map/ppermute | solution.py:56
  21.6 1.8 %collective-permute-done.6 = f32[16,512]{1,0:T(8,128)S(1)} collective-permute-done((f32[16,512]{1,0:T(8,128)S(1)}, f32[16,512]{1,0:T(8,128)S(1)}, u32[]{:S(2)}, u32[]{:S(2)}) %collective-permute-start.6) | collective-permute-done | bytes 32800 | tf_op jit(solution)/shard_map/ppermute | solution.py:56
  23.5 4.0 %collective-permute-start.7 = (f32[16,512]{1,0:T(8,128)S(1)}, f32[16,512]{1,0:T(8,128)S(1)}, u32[]{:S(2)}, u32[]{:S(2)}) collective-permute-start(f32[16,512]{1,0:T(8,128)S(1)} %multiply_add_fusion.1), channel_id=1, source_target_pairs={{0,64},{8,72},{16,80},{24,88},{32,96},{40,104},{48,112},{56,120},{... | collective-permute-start | bytes 98312 | tf_op jit(solution)/shard_map/ppermute | solution.py:56
  27.4 1.0 %collective-permute-start.8 = (f32[16,512]{1,0:T(8,128)S(1)}, f32[16,512]{1,0:T(8,128)S(1)}, u32[]{:S(2)}, u32[]{:S(2)}) collective-permute-start(f32[16,512]{1,0:T(8,128)S(1)} %multiply_add_fusion.1), channel_id=1, source_target_pairs={{0,32},{8,40},{16,48},{24,56},{32,0},{40,8},{48,16},{56,24},{64,96... | collective-permute-start | bytes 98312 | tf_op jit(solution)/shard_map/ppermute | solution.py:56
  28.5 0.0 collective-permute-start.9
  28.5 1.4 %shard_map.50 = (f32[2,256,128]{2,1,0:T(8,128)S(1)}, f32[2,256,128]{2,1,0:T(8,128)S(1)}) custom-call(f32[4,256,128]{2,1,0:T(8,128)S(1)} %get-tuple-element.40.refs_0_, f32[4,256,128]{2,1,0:T(8,128)S(1)} %get-tuple-element.41.refs_1_, f32[16,8,512]{2,1,0:T(8,128)S(1)} %get-tuple-element.42.refs_2_, f32[16,8,512]{2,1,0:T(8,128)S(1)} %get-tuple-element.43.refs_3_, ...), custom_call_target="tpu_custom_call" | custom-call | flops 40000000 | bytes 4000000 | tf_op jit(solution)/shard_map/pallas_call | solution.py:241
  29.9 0.0 collective-permute-done.7
  29.9 1.5 %collective-permute-done.8 = f32[16,512]{1,0:T(8,128)S(1)} collective-permute-done((f32[16,512]{1,0:T(8,128)S(1)}, f32[16,512]{1,0:T(8,128)S(1)}, u32[]{:S(2)}, u32[]{:S(2)}) %collective-permute-start.8) | collective-permute-done | bytes 32800 | tf_op jit(solution)/shard_map/ppermute | solution.py:56
  31.4 2.2 %collective-permute-done.9 = f32[16,512]{1,0:T(8,128)S(1)} collective-permute-done((f32[16,512]{1,0:T(8,128)S(1)}, f32[16,512]{1,0:T(8,128)S(1)}, u32[]{:S(2)}, u32[]{:S(2)}) %collective-permute-start.9) | collective-permute-done | bytes 32800 | tf_op jit(solution)/shard_map/ppermute | solution.py:56
  33.6 0.1 multiply_add_fusion.refs_5_
  33.7 2.1 %shard_map.51 = bf16[512,512]{1,0:T(8,128)(2,1)} custom-call(f32[2,256,128]{2,1,0:T(8,128)S(1)} %get-tuple-element.46.refs_0_, f32[2,256,128]{2,1,0:T(8,128)S(1)} %get-tuple-element.47.refs_1_, f32[2,256,128]{2,1,0:T(8,128)S(1)} %get-tuple-element.53.refs_2_, f32[2,256,128]{2,1,0:T(8,128)S(1)} %get-tuple-element.54.refs_3_, bf16[512,512]{1,0:T(8,128)(2,1)S(1)} %bitcast.14, ...), custom_call_target="tpu_custom_call" | custom-call | flops 40000000 | bytes 2000000 | tf_op jit(solution)/shard_map/pallas_call | solution.py:276
  (20 shorter events, 0.2 us)
Async XLA Ops:
  0.0 1.4 %copy-start = (bf16[3,64,4096]{2,1,0:T(8,128)(2,1)S(1)}, bf16[3,64,4096]{2,1,0:T(8,128)(2,1)}, u32[]{:S(2)}) copy-start(bf16[3,64,4096]{2,1,0:T(8,128)(2,1)} %qkv_ref.1) | copy-start | bytes 4718596
  1.4 10.0 %copy-start.1 = (f32[512,16]{0,1:T(8,128)S(1)}, f32[512,16]{0,1:T(8,128)}, u32[]{:S(2)}) copy-start(f32[512,16]{0,1:T(8,128)} %param.6) | copy-start | bytes 98308
  1.4 10.0 %copy-start.2 = (f32[512,16]{0,1:T(8,128)S(1)}, f32[512,16]{0,1:T(8,128)}, u32[]{:S(2)}) copy-start(f32[512,16]{0,1:T(8,128)} %param.5) | copy-start | bytes 98308
  1.8 9.9 %collective-permute-start = (bf16[2,64,512]{2,1,0:T(8,128)(2,1)S(1)}, bf16[2,64,512]{2,1,0:T(8,128)(2,1)S(1)}, u32[]{:S(2)}, u32[]{:S(2)}) collective-permute-start(bf16[2,64,512]{2,1,0:T(8,128)(2,1)S(1)} %get-tuple-element.33), channel_id=1, source_target_pairs={{0,4},{1,5},{2,6},{3,7},{4,0},{5,1},{6,2},{7,3},{8,12},{9,13},{10,... | collective-permute-start | bytes 393224 | tf_op jit(solution)/shard_map/ppermute | solution.py:52
  5.2 6.7 %collective-permute-start.1 = (bf16[2,64,512]{2,1,0:T(8,128)(2,1)S(1)}, bf16[2,64,512]{2,1,0:T(8,128)(2,1)S(1)}, u32[]{:S(2)}, u32[]{:S(2)}) collective-permute-start(bf16[2,64,512]{2,1,0:T(8,128)(2,1)S(1)} %get-tuple-element.34), channel_id=1, source_target_pairs={{0,2},{1,3},{2,0},{3,1},{4,6},{5,7},{6,4},{7,5},{8,10},{9,11},{10,... | collective-permute-start | bytes 393224 | tf_op jit(solution)/shard_map/ppermute | solution.py:52
  5.9 6.2 %collective-permute-start.2 = (bf16[2,64,512]{2,1,0:T(8,128)(2,1)S(1)}, bf16[2,64,512]{2,1,0:T(8,128)(2,1)S(1)}, u32[]{:S(2)}, u32[]{:S(2)}) collective-permute-start(bf16[2,64,512]{2,1,0:T(8,128)(2,1)S(1)} %get-tuple-element.35), channel_id=1, source_target_pairs={{0,6},{1,7},{2,4},{3,5},{4,2},{5,3},{6,0},{7,1},{8,14},{9,15},{10,... | collective-permute-start | bytes 393224 | tf_op jit(solution)/shard_map/ppermute | solution.py:52
  7.1 16.4 %all-to-all-start = ((bf16[8,64,512]{2,1,0:T(8,128)(2,1)}), bf16[8,64,512]{2,1,0:T(8,128)(2,1)S(1)}, u32[]{:S(2)}, u32[]{:S(2)}) async-start(bf16[8,64,512]{2,1,0:T(8,128)(2,1)} %pad_maximum_fusion), calls=%async_computation | async-start | bytes 1048576 | tf_op jit(solution)/shard_map/all_to_all | solution.py:203
  11.7 7.1 %copy-start.3 = (f32[512]{0:T(512)S(1)}, f32[512]{0:T(512)}, u32[]{:S(2)}) copy-start(f32[512]{0:T(512)} %param.7) | copy-start | bytes 6148
  12.1 1.6 %collective-permute-start.3 = (bf16[4,64,512]{2,1,0:T(8,128)(2,1)S(1)}, bf16[4,64,512]{2,1,0:T(8,128)(2,1)S(1)}, u32[]{:S(2)}, u32[]{:S(2)}) collective-permute-start(bf16[4,64,512]{2,1,0:T(8,128)(2,1)S(1)} %pad_maximum_fusion.1), channel_id=1, source_target_pairs={{0,1},{1,0},{2,3},{3,2},{4,5},{5,4},{6,7},{7,6},{8,9},{9,8},{10,11... | collective-permute-start | bytes 786440 | tf_op jit(solution)/shard_map/ppermute | solution.py:48
  14.6 5.7 %collective-permute-start.4 = (f32[16,512]{1,0:T(8,128)S(1)}, f32[16,512]{1,0:T(8,128)S(1)}, u32[]{:S(2)}, u32[]{:S(2)}) collective-permute-start(f32[16,512]{1,0:T(8,128)S(1)} %get-tuple-element.37), channel_id=1, source_target_pairs={{0,16},{8,24},{16,0},{24,8},{32,48},{40,56},{48,32},{56,40},{64,80... | collective-permute-start | bytes 98312 | tf_op jit(solution)/shard_map/ppermute | solution.py:56
  17.7 3.9 %collective-permute-start.5 = (f32[16,512]{1,0:T(8,128)S(1)}, f32[16,512]{1,0:T(8,128)S(1)}, u32[]{:S(2)}, u32[]{:S(2)}) collective-permute-start(f32[16,512]{1,0:T(8,128)S(1)} %get-tuple-element.37), channel_id=1, source_target_pairs={{0,8},{8,0},{16,24},{24,16},{32,40},{40,32},{48,56},{56,48},{64,72... | collective-permute-start | bytes 98312 | tf_op jit(solution)/shard_map/ppermute | solution.py:56
  18.3 5.1 %collective-permute-start.6 = (f32[16,512]{1,0:T(8,128)S(1)}, f32[16,512]{1,0:T(8,128)S(1)}, u32[]{:S(2)}, u32[]{:S(2)}) collective-permute-start(f32[16,512]{1,0:T(8,128)S(1)} %get-tuple-element.37), channel_id=1, source_target_pairs={{0,24},{8,16},{16,8},{24,0},{32,56},{40,48},{48,40},{56,32},{64,88... | collective-permute-start | bytes 98312 | tf_op jit(solution)/shard_map/ppermute | solution.py:56
  23.5 6.4 %collective-permute-start.7 = (f32[16,512]{1,0:T(8,128)S(1)}, f32[16,512]{1,0:T(8,128)S(1)}, u32[]{:S(2)}, u32[]{:S(2)}) collective-permute-start(f32[16,512]{1,0:T(8,128)S(1)} %multiply_add_fusion.1), channel_id=1, source_target_pairs={{0,64},{8,72},{16,80},{24,88},{32,96},{40,104},{48,112},{56,120},{... | collective-permute-start | bytes 98312 | tf_op jit(solution)/shard_map/ppermute | solution.py:56
  27.4 3.9 %collective-permute-start.8 = (f32[16,512]{1,0:T(8,128)S(1)}, f32[16,512]{1,0:T(8,128)S(1)}, u32[]{:S(2)}, u32[]{:S(2)}) collective-permute-start(f32[16,512]{1,0:T(8,128)S(1)} %multiply_add_fusion.1), channel_id=1, source_target_pairs={{0,32},{8,40},{16,48},{24,56},{32,0},{40,8},{48,16},{56,24},{64,96... | collective-permute-start | bytes 98312 | tf_op jit(solution)/shard_map/ppermute | solution.py:56
  28.5 5.1 %collective-permute-start.9 = (f32[16,512]{1,0:T(8,128)S(1)}, f32[16,512]{1,0:T(8,128)S(1)}, u32[]{:S(2)}, u32[]{:S(2)}) collective-permute-start(f32[16,512]{1,0:T(8,128)S(1)} %multiply_add_fusion.1), channel_id=1, source_target_pairs={{0,96},{8,104},{16,112},{24,120},{32,64},{40,72},{48,80},{56,88},{... | collective-permute-start | bytes 98312 | tf_op jit(solution)/shard_map/ppermute | solution.py:56

commit v6 on v5

--- a/solution.py
+++ b/solution.py
@@ -12,6 +12,7 @@
 SUBS = 8
 LANES = 128
 SCALE = 1024.0
+OPEN_VMEM = 52 * 1024 * 1024
 CHIP_ORDER = (2, 1, 3)
 VMEM = pl.BlockSpec(memory_space=pltpu.VMEM)
 PARAMS = pltpu.CompilerParams(vmem_limit_bytes=32 * 1024 * 1024)
@@ -31,17 +32,33 @@
 
 
 def open_kernel(qkv_ref, *refs):
-    *code_refs, low_ref, high_ref = refs
+    *code_refs, held_ref, held_sem = refs
     _, _, width = code_refs[0].shape
     place = lax.axis_index("tp")
-    chips = len(code_refs)
-    for k, code_ref in enumerate(code_refs):
+
+    def fetch(k):
+        lanes = pl.ds(pl.multiple_of((place // 2 ^ k) * 2 * width, 2 * width), 2 * width)
+        return pltpu.make_async_copy(qkv_ref.at[pl.ds(1, 2), :, lanes], held_ref.at[k], held_sem.at[k])
+
+    order = CHIP_ORDER + (0,)
+    for k in order:
+        fetch(k).start()
+    for k in order:
+        fetch(k).wait()
         for flip in range(2):
-            lanes = pl.ds(pl.multiple_of((place ^ (2 * k + flip)) * width, width), width)
-            code_ref[flip] = encode(qkv_ref[1, :, lanes].astype(F32) * qkv_ref[2, :, lanes].astype(F32) * SCALE)
-    for half, out_ref in enumerate((low_ref, high_ref)):
-        for part in range(chips):
-            out_ref[part] = qkv_ref[0, :, pl.ds((half * chips + part) * width, width)]
+            half = pl.ds(pl.multiple_of((place % 2 ^ flip) * width, width), width)
+            scaled = held_ref[k, 0, :, half].astype(F32) * held_ref[k, 1, :, half].astype(F32) * SCALE
+            code_refs[k][flip] = encode(scaled)
+
+
+def query_kernel(qkv_ref, query_ref, moved_ref, sem):
+    parts, _, width = moved_ref.shape
+    copies = [pltpu.make_async_copy(moved_ref.at[part], query_ref.at[part], sem.at[part]) for part in range(parts)]
+    for part in range(parts):
+        moved_ref[part] = qkv_ref[0, :, pl.ds(part * width, width)]
+        copies[part].start()
+    for copy in copies:
+        copy.wait()
 
 
 def across_core(value):
@@ -188,18 +205,29 @@
     steps = half // SUBS
     core = lax.axis_index("tp") % 2
 
-    outs = pl.pallas_call(
-        open_kernel,
+    code = list(
+        pl.pallas_call(
+            open_kernel,
+            in_specs=[pl.BlockSpec(memory_space=pl.ANY)],
+            out_specs=[VMEM] * chips,
+            out_shape=[jax.ShapeDtypeStruct((2, span_tokens, channels), BF16)] * chips,
+            scratch_shapes=[
+                pltpu.VMEM((chips, 2, span_tokens, 2 * channels), BF16),
+                pltpu.SemaphoreType.DMA((chips,)),
+            ],
+            compiler_params=pltpu.CompilerParams(vmem_limit_bytes=OPEN_VMEM),
+        )(qkv)
+    )
+    query = pl.pallas_call(
+        query_kernel,
         in_specs=[VMEM],
-        out_specs=[VMEM] * (chips + 2),
-        out_shape=[jax.ShapeDtypeStruct((2, span_tokens, channels), BF16)] * chips
-        + [jax.ShapeDtypeStruct((chips, span_tokens, channels), BF16)] * 2,
+        out_specs=pl.BlockSpec(memory_space=pl.ANY),
+        out_shape=jax.ShapeDtypeStruct((devices, span_tokens, channels), BF16),
+        scratch_shapes=[pltpu.VMEM((devices, span_tokens, channels), BF16), pltpu.SemaphoreType.DMA((devices,))],
         compiler_params=PARAMS,
     )(qkv)
-    code, (low, high) = list(outs[:chips]), outs[chips:]
     for k in CHIP_ORDER:
         code[k] = across_chips(code[k], k)
-    query = jnp.concatenate([low, high])
     query = lax.all_to_all(query, "tp", 0, 0).reshape(tokens, channels)
     code = [code[0]] + [code[k] for k in CHIP_ORDER]
     near_code = jnp.stack([piece[0] for piece in code])
@@ -208,7 +236,6 @@
     rates = 1.0 / spans.T
     weight = residues.T * jnp.sqrt(rates) * (1.0 / SCALE)
     decay = jnp.exp(-rates)
-    step_decay = jnp.exp(-rates * steps)
     sub_index = jnp.arange(SUBS, dtype=jnp.int32)
 
     def first_token(side):
@@ -236,6 +263,8 @@
 
     near_drive, near_subs, block = states(near_code, tail(core), jnp.zeros((modes, channels), F32))
     far_drive, far_subs, block = states(far_code, tail(1 - core), block)
+    rates, weight, block = lax.optimization_barrier((rates, weight, block))
+    step_decay = jnp.exp(-rates * steps)
 
     local = [
         pl.pallas_call(

time: 36 us -> 35.7 us (level)
  Pallas kernels: 6.95 us -> 8.92 us
  local copies, waits for them, and re-layouts: 1.47 us -> 0.06 us
  other arithmetic: 1.32 us -> 0.53 us
    pallas_call x1 -> x2, Pallas kernels: 0.4 us -> 2.37 us  [the longest x1 1.52 us: per_device(): pl.pallas_call(open_kernel, in_specs=[pl.BlockSpec(memory_space=pl.ANY)],...]
    unnamed x8, local copies, waits for them, and re-layouts: 1.42 us -> 0.02 us
    concatenate x1 -> x0, other arithmetic: 0.84 us -> none  [per_device(): query = jnp.concatenate([low, high])]
  transfers between devices with their start and end apart: 11 -> 11, of which waited for: 7 -> 7; matrix products, arithmetic and copies ran while one was open for 4% -> 1% of each run, Pallas kernels for 12% -> 15%
where the time goes in v6:
time: 35.7 us; the launch traced here: 35.4 us
  starting transfers between devices  18.3 us (51%)
  Pallas kernels  8.92 us (25%)
  waiting for transfers between devices  7.43 us (21%)
  other arithmetic  0.53 us (1%)
    ppermute x6, starting transfers between devices, across_blocks(): lax.ppermute(value, 'ctx', [(i, i ^ bits) for i in range(lax.axis_size('c...  9.28 us
    ppermute x6, waiting for transfers between devices, across_blocks(): lax.ppermute(value, 'ctx', [(i, i ^ bits) for i in range(lax.axis_size('c...  6.74 us
    ppermute x3, starting transfers between devices, across_chips(): lax.ppermute(value, 'tp', [(i, i ^ 2 * k) for i in range(lax.axis_size('t...  4.41 us
    all_to_all x1, starting transfers between devices, per_device(): query = lax.all_to_all(query, 'tp', 0, 0).reshape(tokens, channels)  4.32 us
    pallas_call x2, Pallas kernels, per_device(): pl.pallas_call(functools.partial(local_kernel, modes, begin), in_specs=[V...  2.77 us
    pallas_call x1, Pallas kernels, per_device(): pl.pallas_call(functools.partial(final_kernel, modes), in_specs=[VMEM] *...  2.09 us
    pallas_call x2, Pallas kernels, states(): pl.pallas_call(functools.partial(state_kernel, modes), in_specs=[VMEM] *...  1.69 us
    pallas_call x1, Pallas kernels, per_device(): pl.pallas_call(open_kernel, in_specs=[pl.BlockSpec(memory_space=pl.ANY)],...  1.52 us
  transfers between devices with their start and end apart: 11, of which 7 were waited for; matrix products, arithmetic and copies ran while one was open for 1% of the time, Pallas kernels for 15%

profile of v6, /device:TPU:0, one launch (start us, length us, event | category | flops | bytes accessed | tf_op | source)
XLA Modules:
  0.0 35.4 jit_solution(2292501350396744962)
XLA Ops:
  0.0 1.5 %shard_map.46 = (bf16[2,64,512]{2,1,0:T(8,128)(2,1)S(1)}, bf16[2,64,512]{2,1,0:T(8,128)(2,1)S(1)}, bf16[2,64,512]{2,1,0:T(8,128)(2,1)S(1)}, bf16[2,64,512]{2,1,0:T(8,128)(2,1)S(1)}) custom-call(bf16[3,64,4096]{2,1,0:T(8,128)(2,1)} %qkv_ref.3), custom_call_target="tpu_custom_call" | custom-call | tf_op jit(solution)/shard_map/pallas_call | solution.py:209
  1.5 3.4 %collective-permute-start = (bf16[2,64,512]{2,1,0:T(8,128)(2,1)S(1)}, bf16[2,64,512]{2,1,0:T(8,128)(2,1)S(1)}, u32[]{:S(2)}, u32[]{:S(2)}) collective-permute-start(bf16[2,64,512]{2,1,0:T(8,128)(2,1)S(1)} %get-tuple-element.34), channel_id=1, source_target_pairs={{0,4},{1,5},{2,6},{3,7},{4,0},{5,1},{6,2},{7,3},{8,12},{9,13},{10,... | collective-permute-start | bytes 393224 | tf_op jit(solution)/shard_map/ppermute | solution.py:69
  4.9 0.7 %collective-permute-start.1 = (bf16[2,64,512]{2,1,0:T(8,128)(2,1)S(1)}, bf16[2,64,512]{2,1,0:T(8,128)(2,1)S(1)}, u32[]{:S(2)}, u32[]{:S(2)}) collective-permute-start(bf16[2,64,512]{2,1,0:T(8,128)(2,1)S(1)} %get-tuple-element.35), channel_id=1, source_target_pairs={{0,2},{1,3},{2,0},{3,1},{4,6},{5,7},{6,4},{7,5},{8,10},{9,11},{10,... | collective-permute-start | bytes 393224 | tf_op jit(solution)/shard_map/ppermute | solution.py:69
  5.6 0.4 %collective-permute-start.2 = (bf16[2,64,512]{2,1,0:T(8,128)(2,1)S(1)}, bf16[2,64,512]{2,1,0:T(8,128)(2,1)S(1)}, u32[]{:S(2)}, u32[]{:S(2)}) collective-permute-start(bf16[2,64,512]{2,1,0:T(8,128)(2,1)S(1)} %get-tuple-element.36), channel_id=1, source_target_pairs={{0,6},{1,7},{2,4},{3,5},{4,2},{5,3},{6,0},{7,1},{8,14},{9,15},{10,... | collective-permute-start | bytes 393224 | tf_op jit(solution)/shard_map/ppermute | solution.py:69
  6.0 0.9 %shard_map.49 = bf16[8,64,512]{2,1,0:T(8,128)(2,1)} custom-call(bf16[3,64,4096]{2,1,0:T(8,128)(2,1)S(1)} %copy-done), custom_call_target="tpu_custom_call" | custom-call | tf_op jit(solution)/shard_map/pallas_call | solution.py:221
  6.8 0.0 copy-start.3
  6.8 4.3 %all-to-all-start = ((bf16[8,64,512]{2,1,0:T(8,128)(2,1)}), bf16[8,64,512]{2,1,0:T(8,128)(2,1)S(1)}, u32[]{:S(2)}, u32[]{:S(2)}) async-start(bf16[8,64,512]{2,1,0:T(8,128)(2,1)} %shard_map.49), calls=%async_computation | async-start | bytes 1048576 | tf_op jit(solution)/shard_map/all_to_all | solution.py:231
  11.2 0.1 multiply_exponential_fusion
  11.4 0.0 collective-permute-done
  11.4 0.1 collective-permute-done.1
  11.6 0.2 collective-permute-done.2
  11.8 0.3 collective-permute-start.3
  12.2 0.9 %shard_map.47 = (f32[4,256,128]{2,1,0:T(8,128)S(1)}, f32[16,8,512]{2,1,0:T(8,128)S(1)}, f32[16,512]{1,0:T(8,128)S(1)}) custom-call(bf16[4,64,512]{2,1,0:T(8,128)(2,1)S(1)} %pad_maximum_fusion.1.code_ref, f32[16,512]{1,0:T(8,128)S(1)} %get-tuple-element.77.decay_ref.refs_4_.refs_8_, f32[16,8,512]{2,1,0:T(8,128)S(1)} %get-tuple-element.73.tail_ref, ...), custom_call_target="tpu_custom_call" | custom-call | flops 1000 | bytes 1000 | tf_op jit(solution)/shard_map/pallas_call | solution.py:251
  13.1 0.4 %collective-permute-done.3.code_ref = bf16[4,64,512]{2,1,0:T(8,128)(2,1)S(1)} collective-permute-done((bf16[4,64,512]{2,1,0:T(8,128)(2,1)S(1)}, bf16[4,64,512]{2,1,0:T(8,128)(2,1)S(1)}, u32[]{:S(2)}, u32[]{:S(2)}) %collective-permute-start.3) | collective-permute-done | bytes 262176 | tf_op jit(solution)/shard_map/ppermute | solution.py:65
  13.4 0.8 %shard_map.48 = (f32[4,256,128]{2,1,0:T(8,128)S(1)}, f32[16,8,512]{2,1,0:T(8,128)S(1)}, f32[16,512]{1,0:T(8,128)S(1)}) custom-call(bf16[4,64,512]{2,1,0:T(8,128)(2,1)S(1)} %collective-permute-done.3.code_ref, f32[16,512]{1,0:T(8,128)S(1)} %get-tuple-element.77.decay_ref.refs_4_.refs_8_, f32[16,8,512]{2,1,0:T(8,128)S(1)} %get-tuple-element.74.tail_ref, ...), custom_call_target="tpu_custom_call" | custom-call | flops 1000 | bytes 1000 | tf_op jit(solution)/shard_map/pallas_call | solution.py:251
  14.3 3.2 %collective-permute-start.4 = (f32[16,512]{1,0:T(8,128)S(1)}, f32[16,512]{1,0:T(8,128)S(1)}, u32[]{:S(2)}, u32[]{:S(2)}) collective-permute-start(f32[16,512]{1,0:T(8,128)S(1)} %get-tuple-element.39), channel_id=1, source_target_pairs={{0,16},{8,24},{16,0},{24,8},{32,48},{40,56},{48,32},{56,40},{64,80... | collective-permute-start | bytes 98312 | tf_op jit(solution)/shard_map/ppermute | solution.py:73
  17.4 0.6 %collective-permute-start.5 = (f32[16,512]{1,0:T(8,128)S(1)}, f32[16,512]{1,0:T(8,128)S(1)}, u32[]{:S(2)}, u32[]{:S(2)}) collective-permute-start(f32[16,512]{1,0:T(8,128)S(1)} %get-tuple-element.39), channel_id=1, source_target_pairs={{0,8},{8,0},{16,24},{24,16},{32,40},{40,32},{48,56},{56,48},{64,72... | collective-permute-start | bytes 98312 | tf_op jit(solution)/shard_map/ppermute | solution.py:73
  18.0 0.6 %collective-permute-start.6 = (f32[16,512]{1,0:T(8,128)S(1)}, f32[16,512]{1,0:T(8,128)S(1)}, u32[]{:S(2)}, u32[]{:S(2)}) collective-permute-start(f32[16,512]{1,0:T(8,128)S(1)} %get-tuple-element.39), channel_id=1, source_target_pairs={{0,24},{8,16},{16,8},{24,0},{32,56},{40,48},{48,40},{56,32},{64,88... | collective-permute-start | bytes 98312 | tf_op jit(solution)/shard_map/ppermute | solution.py:73
  18.6 1.4 %shard_map.50 = (f32[2,256,128]{2,1,0:T(8,128)S(1)}, f32[2,256,128]{2,1,0:T(8,128)S(1)}) custom-call(f32[4,256,128]{2,1,0:T(8,128)S(1)} %get-tuple-element.40.refs_0_, f32[4,256,128]{2,1,0:T(8,128)S(1)} %get-tuple-element.41.refs_1_, f32[16,8,512]{2,1,0:T(8,128)S(1)} %get-tuple-element.42.refs_2_, f32[16,8,512]{2,1,0:T(8,128)S(1)} %get-tuple-element.43.refs_3_, ...), custom_call_target="tpu_custom_call" | custom-call | flops 40000000 | bytes 4000000 | tf_op jit(solution)/shard_map/pallas_call | solution.py:270
  20.0 0.0 collective-permute-done.4
  20.0 1.4 %collective-permute-done.5 = f32[16,512]{1,0:T(8,128)S(1)} collective-permute-done((f32[16,512]{1,0:T(8,128)S(1)}, f32[16,512]{1,0:T(8,128)S(1)}, u32[]{:S(2)}, u32[]{:S(2)}) %collective-permute-start.5) | collective-permute-done | bytes 32800 | tf_op jit(solution)/shard_map/ppermute | solution.py:73
  21.4 1.8 %collective-permute-done.6 = f32[16,512]{1,0:T(8,128)S(1)} collective-permute-done((f32[16,512]{1,0:T(8,128)S(1)}, f32[16,512]{1,0:T(8,128)S(1)}, u32[]{:S(2)}, u32[]{:S(2)}) %collective-permute-start.6) | collective-permute-done | bytes 32800 | tf_op jit(solution)/shard_map/ppermute | solution.py:73
  23.2 0.0 all-to-all-done
  23.2 4.0 %collective-permute-start.7 = (f32[16,512]{1,0:T(8,128)S(1)}, f32[16,512]{1,0:T(8,128)S(1)}, u32[]{:S(2)}, u32[]{:S(2)}) collective-permute-start(f32[16,512]{1,0:T(8,128)S(1)} %multiply_add_fusion.1), channel_id=1, source_target_pairs={{0,64},{8,72},{16,80},{24,88},{32,96},{40,104},{48,112},{56,120},{... | collective-permute-start | bytes 98312 | tf_op jit(solution)/shard_map/ppermute | solution.py:73
  27.2 1.0 %collective-permute-start.8 = (f32[16,512]{1,0:T(8,128)S(1)}, f32[16,512]{1,0:T(8,128)S(1)}, u32[]{:S(2)}, u32[]{:S(2)}) collective-permute-start(f32[16,512]{1,0:T(8,128)S(1)} %multiply_add_fusion.1), channel_id=1, source_target_pairs={{0,32},{8,40},{16,48},{24,56},{32,0},{40,8},{48,16},{56,24},{64,96... | collective-permute-start | bytes 98312 | tf_op jit(solution)/shard_map/ppermute | solution.py:73
  28.2 0.0 collective-permute-start.9
  28.2 0.1 exponential_multiply_fusion
  28.3 1.4 %shard_map.51 = (f32[2,256,128]{2,1,0:T(8,128)S(1)}, f32[2,256,128]{2,1,0:T(8,128)S(1)}) custom-call(f32[4,256,128]{2,1,0:T(8,128)S(1)} %get-tuple-element.40.refs_0_, f32[4,256,128]{2,1,0:T(8,128)S(1)} %get-tuple-element.41.refs_1_, f32[16,8,512]{2,1,0:T(8,128)S(1)} %get-tuple-element.42.refs_2_, f32[16,8,512]{2,1,0:T(8,128)S(1)} %get-tuple-element.43.refs_3_, ...), custom_call_target="tpu_custom_call" | custom-call | flops 40000000 | bytes 4000000 | tf_op jit(solution)/shard_map/pallas_call | solution.py:270
  29.7 1.3 %collective-permute-done.8 = f32[16,512]{1,0:T(8,128)S(1)} collective-permute-done((f32[16,512]{1,0:T(8,128)S(1)}, f32[16,512]{1,0:T(8,128)S(1)}, u32[]{:S(2)}, u32[]{:S(2)}) %collective-permute-start.8) | collective-permute-done | bytes 32800 | tf_op jit(solution)/shard_map/ppermute | solution.py:73
  31.1 2.2 %collective-permute-done.9 = f32[16,512]{1,0:T(8,128)S(1)} collective-permute-done((f32[16,512]{1,0:T(8,128)S(1)}, f32[16,512]{1,0:T(8,128)S(1)}, u32[]{:S(2)}, u32[]{:S(2)}) %collective-permute-start.9) | collective-permute-done | bytes 32800 | tf_op jit(solution)/shard_map/ppermute | solution.py:73
  33.3 0.1 multiply_add_fusion.refs_5_
  33.4 2.1 %shard_map.52 = bf16[512,512]{1,0:T(8,128)(2,1)} custom-call(f32[2,256,128]{2,1,0:T(8,128)S(1)} %get-tuple-element.48.refs_0_, f32[2,256,128]{2,1,0:T(8,128)S(1)} %get-tuple-element.49.refs_1_, f32[2,256,128]{2,1,0:T(8,128)S(1)} %get-tuple-element.55.refs_2_, f32[2,256,128]{2,1,0:T(8,128)S(1)} %get-tuple-element.56.refs_3_, bf16[512,512]{1,0:T(8,128)(2,1)S(1)} %bitcast.14, ...), custom_call_target="tpu_custom_call" | custom-call | flops 40000000 | bytes 2000000 | tf_op jit(solution)/shard_map/pallas_call | solution.py:305
  (22 shorter events, 0.2 us)
Async XLA Ops:
  0.0 5.9 %copy-start = (bf16[3,64,4096]{2,1,0:T(8,128)(2,1)S(1)}, bf16[3,64,4096]{2,1,0:T(8,128)(2,1)}, u32[]{:S(2)}) copy-start(bf16[3,64,4096]{2,1,0:T(8,128)(2,1)} %qkv_ref.3) | copy-start | bytes 4718596
  1.5 9.9 %collective-permute-start = (bf16[2,64,512]{2,1,0:T(8,128)(2,1)S(1)}, bf16[2,64,512]{2,1,0:T(8,128)(2,1)S(1)}, u32[]{:S(2)}, u32[]{:S(2)}) collective-permute-start(bf16[2,64,512]{2,1,0:T(8,128)(2,1)S(1)} %get-tuple-element.34), channel_id=1, source_target_pairs={{0,4},{1,5},{2,6},{3,7},{4,0},{5,1},{6,2},{7,3},{8,12},{9,13},{10,... | collective-permute-start | bytes 393224 | tf_op jit(solution)/shard_map/ppermute | solution.py:69
  4.9 6.7 %collective-permute-start.1 = (bf16[2,64,512]{2,1,0:T(8,128)(2,1)S(1)}, bf16[2,64,512]{2,1,0:T(8,128)(2,1)S(1)}, u32[]{:S(2)}, u32[]{:S(2)}) collective-permute-start(bf16[2,64,512]{2,1,0:T(8,128)(2,1)S(1)} %get-tuple-element.35), channel_id=1, source_target_pairs={{0,2},{1,3},{2,0},{3,1},{4,6},{5,7},{6,4},{7,5},{8,10},{9,11},{10,... | collective-permute-start | bytes 393224 | tf_op jit(solution)/shard_map/ppermute | solution.py:69
  5.6 5.6 %copy-start.1 = (f32[512,16]{0,1:T(8,128)S(1)}, f32[512,16]{0,1:T(8,128)}, u32[]{:S(2)}) copy-start(f32[512,16]{0,1:T(8,128)} %param.6) | copy-start | bytes 98308
  5.6 5.6 %copy-start.2 = (f32[512,16]{0,1:T(8,128)S(1)}, f32[512,16]{0,1:T(8,128)}, u32[]{:S(2)}) copy-start(f32[512,16]{0,1:T(8,128)} %param.5) | copy-start | bytes 98308
  5.6 6.2 %collective-permute-start.2 = (bf16[2,64,512]{2,1,0:T(8,128)(2,1)S(1)}, bf16[2,64,512]{2,1,0:T(8,128)(2,1)S(1)}, u32[]{:S(2)}, u32[]{:S(2)}) collective-permute-start(bf16[2,64,512]{2,1,0:T(8,128)(2,1)S(1)} %get-tuple-element.36), channel_id=1, source_target_pairs={{0,6},{1,7},{2,4},{3,5},{4,2},{5,3},{6,0},{7,1},{8,14},{9,15},{10,... | collective-permute-start | bytes 393224 | tf_op jit(solution)/shard_map/ppermute | solution.py:69
  6.8 5.3 %copy-start.3 = (f32[512]{0:T(512)S(1)}, f32[512]{0:T(512)}, u32[]{:S(2)}) copy-start(f32[512]{0:T(512)} %param.7) | copy-start | bytes 6148
  6.8 16.3 %all-to-all-start = ((bf16[8,64,512]{2,1,0:T(8,128)(2,1)}), bf16[8,64,512]{2,1,0:T(8,128)(2,1)S(1)}, u32[]{:S(2)}, u32[]{:S(2)}) async-start(bf16[8,64,512]{2,1,0:T(8,128)(2,1)} %shard_map.49), calls=%async_computation | async-start | bytes 1048576 | tf_op jit(solution)/shard_map/all_to_all | solution.py:231
  11.8 1.6 %collective-permute-start.3 = (bf16[4,64,512]{2,1,0:T(8,128)(2,1)S(1)}, bf16[4,64,512]{2,1,0:T(8,128)(2,1)S(1)}, u32[]{:S(2)}, u32[]{:S(2)}) collective-permute-start(bf16[4,64,512]{2,1,0:T(8,128)(2,1)S(1)} %pad_maximum_fusion), channel_id=1, source_target_pairs={{0,1},{1,0},{2,3},{3,2},{4,5},{5,4},{6,7},{7,6},{8,9},{9,8},{10,11... | collective-permute-start | bytes 786440 | tf_op jit(solution)/shard_map/ppermute | solution.py:65
  14.3 5.7 %collective-permute-start.4 = (f32[16,512]{1,0:T(8,128)S(1)}, f32[16,512]{1,0:T(8,128)S(1)}, u32[]{:S(2)}, u32[]{:S(2)}) collective-permute-start(f32[16,512]{1,0:T(8,128)S(1)} %get-tuple-element.39), channel_id=1, source_target_pairs={{0,16},{8,24},{16,0},{24,8},{32,48},{40,56},{48,32},{56,40},{64,80... | collective-permute-start | bytes 98312 | tf_op jit(solution)/shard_map/ppermute | solution.py:73
  17.4 3.9 %collective-permute-start.5 = (f32[16,512]{1,0:T(8,128)S(1)}, f32[16,512]{1,0:T(8,128)S(1)}, u32[]{:S(2)}, u32[]{:S(2)}) collective-permute-start(f32[16,512]{1,0:T(8,128)S(1)} %get-tuple-element.39), channel_id=1, source_target_pairs={{0,8},{8,0},{16,24},{24,16},{32,40},{40,32},{48,56},{56,48},{64,72... | collective-permute-start | bytes 98312 | tf_op jit(solution)/shard_map/ppermute | solution.py:73
  18.0 5.1 %collective-permute-start.6 = (f32[16,512]{1,0:T(8,128)S(1)}, f32[16,512]{1,0:T(8,128)S(1)}, u32[]{:S(2)}, u32[]{:S(2)}) collective-permute-start(f32[16,512]{1,0:T(8,128)S(1)} %get-tuple-element.39), channel_id=1, source_target_pairs={{0,24},{8,16},{16,8},{24,0},{32,56},{40,48},{48,40},{56,32},{64,88... | collective-permute-start | bytes 98312 | tf_op jit(solution)/shard_map/ppermute | solution.py:73
  23.2 6.5 %collective-permute-start.7 = (f32[16,512]{1,0:T(8,128)S(1)}, f32[16,512]{1,0:T(8,128)S(1)}, u32[]{:S(2)}, u32[]{:S(2)}) collective-permute-start(f32[16,512]{1,0:T(8,128)S(1)} %multiply_add_fusion.1), channel_id=1, source_target_pairs={{0,64},{8,72},{16,80},{24,88},{32,96},{40,104},{48,112},{56,120},{... | collective-permute-start | bytes 98312 | tf_op jit(solution)/shard_map/ppermute | solution.py:73
  27.2 3.9 %collective-permute-start.8 = (f32[16,512]{1,0:T(8,128)S(1)}, f32[16,512]{1,0:T(8,128)S(1)}, u32[]{:S(2)}, u32[]{:S(2)}) collective-permute-start(f32[16,512]{1,0:T(8,128)S(1)} %multiply_add_fusion.1), channel_id=1, source_target_pairs={{0,32},{8,40},{16,48},{24,56},{32,0},{40,8},{48,16},{56,24},{64,96... | collective-permute-start | bytes 98312 | tf_op jit(solution)/shard_map/ppermute | solution.py:73
  28.2 5.1 %collective-permute-start.9 = (f32[16,512]{1,0:T(8,128)S(1)}, f32[16,512]{1,0:T(8,128)S(1)}, u32[]{:S(2)}, u32[]{:S(2)}) collective-permute-start(f32[16,512]{1,0:T(8,128)S(1)} %multiply_add_fusion.1), channel_id=1, source_target_pairs={{0,96},{8,104},{16,112},{24,120},{32,64},{40,72},{48,80},{56,88},{... | collective-permute-start | bytes 98312 | tf_op jit(solution)/shard_map/ppermute | solution.py:73

commit v7 on v6

--- a/solution.py
+++ b/solution.py
@@ -159,7 +159,15 @@
             lax.fori_loop(0, steps, step, [start[part] for start in starts], unroll=8)
 
 
-def final_kernel(modes, *refs):
+def final_kernel(modes, early, *refs):
+    row = lax.axis_index("ctx") // 4
+
+    @pl.when(row == 0 if early else row > 0)
+    def _():
+        finish(modes, *refs[: 9], *refs[9 if early else 10 :])
+
+
+def finish(modes, *refs):
     low_refs, high_refs = refs[0:2], refs[2:4]
     query_ref, carry_ref, near_ref, far_ref, decay_ref, out_ref, sum_ref, held_ref, out_sem = refs[4:]
     _, groups, tokens, _ = sum_ref.shape
@@ -288,33 +296,37 @@
         count = jnp.asarray(count)
         return jnp.where(count >= 0, jnp.exp(-rates * jnp.maximum(count, 0).astype(F32)), 0.0)
 
+    near_start, far_start = start(core), start(1 - core)
+
+    def final(carry, out=None):
+        early = out is None
+        return pl.pallas_call(
+            functools.partial(final_kernel, modes, early),
+            in_specs=[VMEM] * 9 + [pl.BlockSpec(memory_space=pl.ANY)] * (not early),
+            out_specs=pl.BlockSpec(memory_space=pl.ANY),
+            out_shape=jax.ShapeDtypeStruct((channels, tokens), BF16),
+            input_output_aliases={} if early else {9: 0},
+            scratch_shapes=[
+                pltpu.VMEM((2, groups, half, LANES), F32),
+                pltpu.VMEM((groups, LANES, tokens), BF16),
+                pltpu.SemaphoreType.DMA((groups,)),
+            ],
+            compiler_params=PARAMS,
+        )(*local[0], *local[1], query, carry, near_start, far_start, decay, *(() if early else (out,)))
+
     others = [across_blocks(block, k) for k in CHIP_ORDER]
-    others, query, local[0] = lax.optimization_barrier((others, query, local[0]))
+    others, query, local = lax.optimization_barrier((others, query, local))
     before = jnp.zeros_like(block)
     total = power(tokens * (3 - col)) * block
     for k, other in zip(CHIP_ORDER, others):
         before = before + power(tokens * (col - 1 - (col ^ k))) * other
         total = total + power(tokens * (3 - (col ^ k))) * other
+    total, out = lax.optimization_barrier((total, final(before)))
     others = [across_blocks(total, 4 * k) for k in CHIP_ORDER]
-    others, local[1] = lax.optimization_barrier((others, local[1]))
     carry = jnp.zeros_like(block)
     for k, other in zip(CHIP_ORDER, others):
         carry = carry + power(4 * tokens * (row - 1 - (row ^ k))) * other
-    carry = before + power(tokens * col) * carry
-
-    return pl.pallas_call(
-        functools.partial(final_kernel, modes),
-        in_specs=[VMEM] * 9,
-        out_specs=pl.BlockSpec(memory_space=pl.ANY),
-        out_shape=jax.ShapeDtypeStruct((channels, tokens), BF16),
-        scratch_shapes=[
-            pltpu.VMEM((2, groups, half, LANES), F32),
-            pltpu.VMEM((groups, LANES, tokens), BF16),
-            pltpu.SemaphoreType.DMA((groups,)),
-        ],
-        compiler_params=PARAMS,
-        cost_estimate=pl.CostEstimate(flops=40_000_000, bytes_accessed=2_000_000, transcendentals=0),
-    )(*local[0], *local[1], query, carry, start(core), start(1 - core), decay)
+    return final(before + power(tokens * col) * carry, out)
 
 
 def solution(mesh):

time: 35.7 us -> 33.7 us (0.944)
  waiting for transfers between devices: 7.43 us -> 6.14 us
  starting transfers between devices: 18.3 us -> 17.5 us
    ppermute x6, waiting for transfers between devices: 6.74 us -> 5.45 us  [across_blocks(): lax.ppermute(value, 'ctx', [(i, i ^ bits) for i in range(lax.axis_size('c...]
    ppermute x6, starting transfers between devices: 9.28 us -> 8.47 us  [across_blocks(): lax.ppermute(value, 'ctx', [(i, i ^ bits) for i in range(lax.axis_size('c...]
    pallas_call x1 -> x2, Pallas kernels: 2.09 us -> 2.17 us  [final(): pl.pallas_call(functools.partial(final_kernel, modes, early), in_specs=[V...]
  transfers between devices with their start and end apart: 11 -> 11, of which waited for: 7 -> 7; matrix products, arithmetic and copies ran while one was open for 1% -> 1% of each run, Pallas kernels for 15% -> 16%
where the time goes in v7:
time: 33.7 us; the launch traced here: 33.5 us
  starting transfers between devices  17.5 us (52%)
  Pallas kernels  9.05 us (27%)
  waiting for transfers between devices  6.14 us (18%)
  other arithmetic  0.53 us (2%)
    ppermute x6, starting transfers between devices, across_blocks(): lax.ppermute(value, 'ctx', [(i, i ^ bits) for i in range(lax.axis_size('c...  8.47 us
    ppermute x6, waiting for transfers between devices, across_blocks(): lax.ppermute(value, 'ctx', [(i, i ^ bits) for i in range(lax.axis_size('c...  5.45 us
    ppermute x3, starting transfers between devices, across_chips(): lax.ppermute(value, 'tp', [(i, i ^ 2 * k) for i in range(lax.axis_size('t...  4.41 us
    all_to_all x1, starting transfers between devices, per_device(): query = lax.all_to_all(query, 'tp', 0, 0).reshape(tokens, channels)  4.32 us
    pallas_call x2, Pallas kernels, per_device(): pl.pallas_call(functools.partial(local_kernel, modes, begin), in_specs=[V...  2.81 us
    pallas_call x2, Pallas kernels, final(): pl.pallas_call(functools.partial(final_kernel, modes, early), in_specs=[V...  2.17 us
    pallas_call x2, Pallas kernels, states(): pl.pallas_call(functools.partial(state_kernel, modes), in_specs=[VMEM] *...  1.7 us
    pallas_call x1, Pallas kernels, per_device(): pl.pallas_call(open_kernel, in_specs=[pl.BlockSpec(memory_space=pl.ANY)],...  1.52 us
  transfers between devices with their start and end apart: 11, of which 7 were waited for; matrix products, arithmetic and copies ran while one was open for 1% of the time, Pallas kernels for 16%

profile of v7, /device:TPU:0, one launch (start us, length us, event | category | flops | bytes accessed | tf_op | source)
XLA Modules:
  0.0 33.5 jit_solution(6479139840305204791)
XLA Ops:
  0.0 1.5 %shard_map.46 = (bf16[2,64,512]{2,1,0:T(8,128)(2,1)S(1)}, bf16[2,64,512]{2,1,0:T(8,128)(2,1)S(1)}, bf16[2,64,512]{2,1,0:T(8,128)(2,1)S(1)}, bf16[2,64,512]{2,1,0:T(8,128)(2,1)S(1)}) custom-call(bf16[3,64,4096]{2,1,0:T(8,128)(2,1)} %qkv_ref.3), custom_call_target="tpu_custom_call" | custom-call | tf_op jit(solution)/shard_map/pallas_call | solution.py:217
  1.5 3.4 %collective-permute-start = (bf16[2,64,512]{2,1,0:T(8,128)(2,1)S(1)}, bf16[2,64,512]{2,1,0:T(8,128)(2,1)S(1)}, u32[]{:S(2)}, u32[]{:S(2)}) collective-permute-start(bf16[2,64,512]{2,1,0:T(8,128)(2,1)S(1)} %get-tuple-element.33), channel_id=1, source_target_pairs={{0,4},{1,5},{2,6},{3,7},{4,0},{5,1},{6,2},{7,3},{8,12},{9,13},{10,... | collective-permute-start | bytes 393224 | tf_op jit(solution)/shard_map/ppermute | solution.py:69
  4.9 0.7 %collective-permute-start.1 = (bf16[2,64,512]{2,1,0:T(8,128)(2,1)S(1)}, bf16[2,64,512]{2,1,0:T(8,128)(2,1)S(1)}, u32[]{:S(2)}, u32[]{:S(2)}) collective-permute-start(bf16[2,64,512]{2,1,0:T(8,128)(2,1)S(1)} %get-tuple-element.34), channel_id=1, source_target_pairs={{0,2},{1,3},{2,0},{3,1},{4,6},{5,7},{6,4},{7,5},{8,10},{9,11},{10,... | collective-permute-start | bytes 393224 | tf_op jit(solution)/shard_map/ppermute | solution.py:69
  5.6 0.4 %collective-permute-start.2 = (bf16[2,64,512]{2,1,0:T(8,128)(2,1)S(1)}, bf16[2,64,512]{2,1,0:T(8,128)(2,1)S(1)}, u32[]{:S(2)}, u32[]{:S(2)}) collective-permute-start(bf16[2,64,512]{2,1,0:T(8,128)(2,1)S(1)} %get-tuple-element.35), channel_id=1, source_target_pairs={{0,6},{1,7},{2,4},{3,5},{4,2},{5,3},{6,0},{7,1},{8,14},{9,15},{10,... | collective-permute-start | bytes 393224 | tf_op jit(solution)/shard_map/ppermute | solution.py:69
  6.0 0.9 %shard_map.49 = bf16[8,64,512]{2,1,0:T(8,128)(2,1)} custom-call(bf16[3,64,4096]{2,1,0:T(8,128)(2,1)S(1)} %copy-done), custom_call_target="tpu_custom_call" | custom-call | tf_op jit(solution)/shard_map/pallas_call | solution.py:229
  6.8 0.0 copy-start.3
  6.8 4.3 %all-to-all-start = ((bf16[8,64,512]{2,1,0:T(8,128)(2,1)}), bf16[8,64,512]{2,1,0:T(8,128)(2,1)S(1)}, u32[]{:S(2)}, u32[]{:S(2)}) async-start(bf16[8,64,512]{2,1,0:T(8,128)(2,1)} %shard_map.49), calls=%async_computation | async-start | bytes 1048576 | tf_op jit(solution)/shard_map/all_to_all | solution.py:239
  11.2 0.1 multiply_exponential_fusion
  11.4 0.0 collective-permute-done
  11.4 0.1 collective-permute-done.1
  11.6 0.2 collective-permute-done.2
  11.8 0.3 collective-permute-start.3
  12.2 0.9 %shard_map.47 = (f32[4,256,128]{2,1,0:T(8,128)S(1)}, f32[16,8,512]{2,1,0:T(8,128)S(1)}, f32[16,512]{1,0:T(8,128)S(1)}) custom-call(bf16[4,64,512]{2,1,0:T(8,128)(2,1)S(1)} %pad_maximum_fusion.1.code_ref, f32[16,512]{1,0:T(8,128)S(1)} %get-tuple-element.77.decay_ref.refs_4_.refs_8_, f32[16,8,512]{2,1,0:T(8,128)S(1)} %get-tuple-element.73.tail_ref, ...), custom_call_target="tpu_custom_call" | custom-call | flops 1000 | bytes 1000 | tf_op jit(solution)/shard_map/pallas_call | solution.py:259
  13.1 0.4 %collective-permute-done.3.code_ref = bf16[4,64,512]{2,1,0:T(8,128)(2,1)S(1)} collective-permute-done((bf16[4,64,512]{2,1,0:T(8,128)(2,1)S(1)}, bf16[4,64,512]{2,1,0:T(8,128)(2,1)S(1)}, u32[]{:S(2)}, u32[]{:S(2)}) %collective-permute-start.3) | collective-permute-done | bytes 262176 | tf_op jit(solution)/shard_map/ppermute | solution.py:65
  13.4 0.8 %shard_map.48 = (f32[4,256,128]{2,1,0:T(8,128)S(1)}, f32[16,8,512]{2,1,0:T(8,128)S(1)}, f32[16,512]{1,0:T(8,128)S(1)}) custom-call(bf16[4,64,512]{2,1,0:T(8,128)(2,1)S(1)} %collective-permute-done.3.code_ref, f32[16,512]{1,0:T(8,128)S(1)} %get-tuple-element.77.decay_ref.refs_4_.refs_8_, f32[16,8,512]{2,1,0:T(8,128)S(1)} %get-tuple-element.74.tail_ref, ...), custom_call_target="tpu_custom_call" | custom-call | flops 1000 | bytes 1000 | tf_op jit(solution)/shard_map/pallas_call | solution.py:259
  14.3 3.2 %collective-permute-start.4 = (f32[16,512]{1,0:T(8,128)S(1)}, f32[16,512]{1,0:T(8,128)S(1)}, u32[]{:S(2)}, u32[]{:S(2)}) collective-permute-start(f32[16,512]{1,0:T(8,128)S(1)} %get-tuple-element.38), channel_id=1, source_target_pairs={{0,16},{8,24},{16,0},{24,8},{32,48},{40,56},{48,32},{56,40},{64,80... | collective-permute-start | bytes 98312 | tf_op jit(solution)/shard_map/ppermute | solution.py:73
  17.4 0.6 %collective-permute-start.5 = (f32[16,512]{1,0:T(8,128)S(1)}, f32[16,512]{1,0:T(8,128)S(1)}, u32[]{:S(2)}, u32[]{:S(2)}) collective-permute-start(f32[16,512]{1,0:T(8,128)S(1)} %get-tuple-element.38), channel_id=1, source_target_pairs={{0,8},{8,0},{16,24},{24,16},{32,40},{40,32},{48,56},{56,48},{64,72... | collective-permute-start | bytes 98312 | tf_op jit(solution)/shard_map/ppermute | solution.py:73
  18.0 0.6 %collective-permute-start.6 = (f32[16,512]{1,0:T(8,128)S(1)}, f32[16,512]{1,0:T(8,128)S(1)}, u32[]{:S(2)}, u32[]{:S(2)}) collective-permute-start(f32[16,512]{1,0:T(8,128)S(1)} %get-tuple-element.38), channel_id=1, source_target_pairs={{0,24},{8,16},{16,8},{24,0},{32,56},{40,48},{48,40},{56,32},{64,88... | collective-permute-start | bytes 98312 | tf_op jit(solution)/shard_map/ppermute | solution.py:73
  18.6 0.1 exponential_multiply_fusion
  18.8 1.4 %shard_map.51 = (f32[2,256,128]{2,1,0:T(8,128)S(1)}, f32[2,256,128]{2,1,0:T(8,128)S(1)}) custom-call(f32[4,256,128]{2,1,0:T(8,128)S(1)} %get-tuple-element.39.refs_0_, f32[4,256,128]{2,1,0:T(8,128)S(1)} %get-tuple-element.40.refs_1_, f32[16,8,512]{2,1,0:T(8,128)S(1)} %get-tuple-element.41.refs_2_, f32[16,8,512]{2,1,0:T(8,128)S(1)} %get-tuple-element.42.refs_3_, ...), custom_call_target="tpu_custom_call" | custom-call | flops 40000000 | bytes 4000000 | tf_op jit(solution)/shard_map/pallas_call | solution.py:278
  20.2 1.4 %shard_map.50 = (f32[2,256,128]{2,1,0:T(8,128)S(1)}, f32[2,256,128]{2,1,0:T(8,128)S(1)}) custom-call(f32[4,256,128]{2,1,0:T(8,128)S(1)} %get-tuple-element.39.refs_0_, f32[4,256,128]{2,1,0:T(8,128)S(1)} %get-tuple-element.40.refs_1_, f32[16,8,512]{2,1,0:T(8,128)S(1)} %get-tuple-element.41.refs_2_, f32[16,8,512]{2,1,0:T(8,128)S(1)} %get-tuple-element.42.refs_3_, ...), custom_call_target="tpu_custom_call" | custom-call | flops 40000000 | bytes 4000000 | tf_op jit(solution)/shard_map/pallas_call | solution.py:278
  21.6 0.0 collective-permute-done.5
  21.6 1.6 %collective-permute-done.6 = f32[16,512]{1,0:T(8,128)S(1)} collective-permute-done((f32[16,512]{1,0:T(8,128)S(1)}, f32[16,512]{1,0:T(8,128)S(1)}, u32[]{:S(2)}, u32[]{:S(2)}) %collective-permute-start.6) | collective-permute-done | bytes 32800 | tf_op jit(solution)/shard_map/ppermute | solution.py:73
  23.2 0.1 multiply_add_fusion.1
  23.2 2.1 %shard_map.52.refs_9_ = bf16[512,512]{1,0:T(8,128)(2,1)} custom-call(f32[2,256,128]{2,1,0:T(8,128)S(1)} %get-tuple-element.49.refs_0_, f32[2,256,128]{2,1,0:T(8,128)S(1)} %get-tuple-element.50.refs_1_, f32[2,256,128]{2,1,0:T(8,128)S(1)} %get-tuple-element.51.refs_2_, f32[2,256,128]{2,1,0:T(8,128)S(1)} %get-tuple-element.52.refs_3_, ...), custom_call_target="tpu_custom_call" | custom-call | tf_op jit(solution)/shard_map/pallas_call | solution.py:303
  25.3 1.9 %collective-permute-start.7 = (f32[16,512]{1,0:T(8,128)S(1)}, f32[16,512]{1,0:T(8,128)S(1)}, u32[]{:S(2)}, u32[]{:S(2)}) collective-permute-start(f32[16,512]{1,0:T(8,128)S(1)} %get-tuple-element.57), channel_id=1, source_target_pairs={{0,64},{8,72},{16,80},{24,88},{32,96},{40,104},{48,112},{56,120},{... | collective-permute-start | bytes 98312 | tf_op jit(solution)/shard_map/ppermute | solution.py:73
  27.2 1.0 %collective-permute-start.8 = (f32[16,512]{1,0:T(8,128)S(1)}, f32[16,512]{1,0:T(8,128)S(1)}, u32[]{:S(2)}, u32[]{:S(2)}) collective-permute-start(f32[16,512]{1,0:T(8,128)S(1)} %get-tuple-element.57), channel_id=1, source_target_pairs={{0,32},{8,40},{16,48},{24,56},{32,0},{40,8},{48,16},{56,24},{64,96... | collective-permute-start | bytes 98312 | tf_op jit(solution)/shard_map/ppermute | solution.py:73
  28.3 1.2 %collective-permute-start.9 = (f32[16,512]{1,0:T(8,128)S(1)}, f32[16,512]{1,0:T(8,128)S(1)}, u32[]{:S(2)}, u32[]{:S(2)}) collective-permute-start(f32[16,512]{1,0:T(8,128)S(1)} %get-tuple-element.57), channel_id=1, source_target_pairs={{0,96},{8,104},{16,112},{24,120},{32,64},{40,72},{48,80},{56,88},{... | collective-permute-start | bytes 98312 | tf_op jit(solution)/shard_map/ppermute | solution.py:73
  29.5 1.3 %collective-permute-done.7 = f32[16,512]{1,0:T(8,128)S(1)} collective-permute-done((f32[16,512]{1,0:T(8,128)S(1)}, f32[16,512]{1,0:T(8,128)S(1)}, u32[]{:S(2)}, u32[]{:S(2)}) %collective-permute-start.7) | collective-permute-done | bytes 32800 | tf_op jit(solution)/shard_map/ppermute | solution.py:73
  30.8 0.3 collective-permute-done.8
  31.2 2.2 %collective-permute-done.9 = f32[16,512]{1,0:T(8,128)S(1)} collective-permute-done((f32[16,512]{1,0:T(8,128)S(1)}, f32[16,512]{1,0:T(8,128)S(1)}, u32[]{:S(2)}, u32[]{:S(2)}) %collective-permute-start.9) | collective-permute-done | bytes 32800 | tf_op jit(solution)/shard_map/ppermute | solution.py:73
  33.4 0.1 shard_map.53
  (23 shorter events, 0.2 us)
Async XLA Ops:
  0.0 5.9 %copy-start = (bf16[3,64,4096]{2,1,0:T(8,128)(2,1)S(1)}, bf16[3,64,4096]{2,1,0:T(8,128)(2,1)}, u32[]{:S(2)}) copy-start(bf16[3,64,4096]{2,1,0:T(8,128)(2,1)} %qkv_ref.3) | copy-start | bytes 4718596
  1.5 9.9 %collective-permute-start = (bf16[2,64,512]{2,1,0:T(8,128)(2,1)S(1)}, bf16[2,64,512]{2,1,0:T(8,128)(2,1)S(1)}, u32[]{:S(2)}, u32[]{:S(2)}) collective-permute-start(bf16[2,64,512]{2,1,0:T(8,128)(2,1)S(1)} %get-tuple-element.33), channel_id=1, source_target_pairs={{0,4},{1,5},{2,6},{3,7},{4,0},{5,1},{6,2},{7,3},{8,12},{9,13},{10,... | collective-permute-start | bytes 393224 | tf_op jit(solution)/shard_map/ppermute | solution.py:69
  4.9 6.7 %collective-permute-start.1 = (bf16[2,64,512]{2,1,0:T(8,128)(2,1)S(1)}, bf16[2,64,512]{2,1,0:T(8,128)(2,1)S(1)}, u32[]{:S(2)}, u32[]{:S(2)}) collective-permute-start(bf16[2,64,512]{2,1,0:T(8,128)(2,1)S(1)} %get-tuple-element.34), channel_id=1, source_target_pairs={{0,2},{1,3},{2,0},{3,1},{4,6},{5,7},{6,4},{7,5},{8,10},{9,11},{10,... | collective-permute-start | bytes 393224 | tf_op jit(solution)/shard_map/ppermute | solution.py:69
  5.6 5.6 %copy-start.1 = (f32[512,16]{0,1:T(8,128)S(1)}, f32[512,16]{0,1:T(8,128)}, u32[]{:S(2)}) copy-start(f32[512,16]{0,1:T(8,128)} %param.6) | copy-start | bytes 98308
  5.6 5.6 %copy-start.2 = (f32[512,16]{0,1:T(8,128)S(1)}, f32[512,16]{0,1:T(8,128)}, u32[]{:S(2)}) copy-start(f32[512,16]{0,1:T(8,128)} %param.5) | copy-start | bytes 98308
  5.6 6.2 %collective-permute-start.2 = (bf16[2,64,512]{2,1,0:T(8,128)(2,1)S(1)}, bf16[2,64,512]{2,1,0:T(8,128)(2,1)S(1)}, u32[]{:S(2)}, u32[]{:S(2)}) collective-permute-start(bf16[2,64,512]{2,1,0:T(8,128)(2,1)S(1)} %get-tuple-element.35), channel_id=1, source_target_pairs={{0,6},{1,7},{2,4},{3,5},{4,2},{5,3},{6,0},{7,1},{8,14},{9,15},{10,... | collective-permute-start | bytes 393224 | tf_op jit(solution)/shard_map/ppermute | solution.py:69
  6.8 5.3 %copy-start.3 = (f32[512]{0:T(512)S(1)}, f32[512]{0:T(512)}, u32[]{:S(2)}) copy-start(f32[512]{0:T(512)} %param.7) | copy-start | bytes 6148
  6.8 16.3 %all-to-all-start = ((bf16[8,64,512]{2,1,0:T(8,128)(2,1)}), bf16[8,64,512]{2,1,0:T(8,128)(2,1)S(1)}, u32[]{:S(2)}, u32[]{:S(2)}) async-start(bf16[8,64,512]{2,1,0:T(8,128)(2,1)} %shard_map.49), calls=%async_computation | async-start | bytes 1048576 | tf_op jit(solution)/shard_map/all_to_all | solution.py:239
  11.8 1.6 %collective-permute-start.3 = (bf16[4,64,512]{2,1,0:T(8,128)(2,1)S(1)}, bf16[4,64,512]{2,1,0:T(8,128)(2,1)S(1)}, u32[]{:S(2)}, u32[]{:S(2)}) collective-permute-start(bf16[4,64,512]{2,1,0:T(8,128)(2,1)S(1)} %pad_maximum_fusion), channel_id=1, source_target_pairs={{0,1},{1,0},{2,3},{3,2},{4,5},{5,4},{6,7},{7,6},{8,9},{9,8},{10,11... | collective-permute-start | bytes 786440 | tf_op jit(solution)/shard_map/ppermute | solution.py:65
  14.3 7.3 %collective-permute-start.4 = (f32[16,512]{1,0:T(8,128)S(1)}, f32[16,512]{1,0:T(8,128)S(1)}, u32[]{:S(2)}, u32[]{:S(2)}) collective-permute-start(f32[16,512]{1,0:T(8,128)S(1)} %get-tuple-element.38), channel_id=1, source_target_pairs={{0,16},{8,24},{16,0},{24,8},{32,48},{40,56},{48,32},{56,40},{64,80... | collective-permute-start | bytes 98312 | tf_op jit(solution)/shard_map/ppermute | solution.py:73
  17.4 4.1 %collective-permute-start.5 = (f32[16,512]{1,0:T(8,128)S(1)}, f32[16,512]{1,0:T(8,128)S(1)}, u32[]{:S(2)}, u32[]{:S(2)}) collective-permute-start(f32[16,512]{1,0:T(8,128)S(1)} %get-tuple-element.38), channel_id=1, source_target_pairs={{0,8},{8,0},{16,24},{24,16},{32,40},{40,32},{48,56},{56,48},{64,72... | collective-permute-start | bytes 98312 | tf_op jit(solution)/shard_map/ppermute | solution.py:73
  18.0 5.1 %collective-permute-start.6 = (f32[16,512]{1,0:T(8,128)S(1)}, f32[16,512]{1,0:T(8,128)S(1)}, u32[]{:S(2)}, u32[]{:S(2)}) collective-permute-start(f32[16,512]{1,0:T(8,128)S(1)} %get-tuple-element.38), channel_id=1, source_target_pairs={{0,24},{8,16},{16,8},{24,0},{32,56},{40,48},{48,40},{56,32},{64,88... | collective-permute-start | bytes 98312 | tf_op jit(solution)/shard_map/ppermute | solution.py:73
  25.3 5.5 %collective-permute-start.7 = (f32[16,512]{1,0:T(8,128)S(1)}, f32[16,512]{1,0:T(8,128)S(1)}, u32[]{:S(2)}, u32[]{:S(2)}) collective-permute-start(f32[16,512]{1,0:T(8,128)S(1)} %get-tuple-element.57), channel_id=1, source_target_pairs={{0,64},{8,72},{16,80},{24,88},{32,96},{40,104},{48,112},{56,120},{... | collective-permute-start | bytes 98312 | tf_op jit(solution)/shard_map/ppermute | solution.py:73
  27.2 3.9 %collective-permute-start.8 = (f32[16,512]{1,0:T(8,128)S(1)}, f32[16,512]{1,0:T(8,128)S(1)}, u32[]{:S(2)}, u32[]{:S(2)}) collective-permute-start(f32[16,512]{1,0:T(8,128)S(1)} %get-tuple-element.57), channel_id=1, source_target_pairs={{0,32},{8,40},{16,48},{24,56},{32,0},{40,8},{48,16},{56,24},{64,96... | collective-permute-start | bytes 98312 | tf_op jit(solution)/shard_map/ppermute | solution.py:73
  28.3 5.1 %collective-permute-start.9 = (f32[16,512]{1,0:T(8,128)S(1)}, f32[16,512]{1,0:T(8,128)S(1)}, u32[]{:S(2)}, u32[]{:S(2)}) collective-permute-start(f32[16,512]{1,0:T(8,128)S(1)} %get-tuple-element.57), channel_id=1, source_target_pairs={{0,96},{8,104},{16,112},{24,120},{32,64},{40,72},{48,80},{56,88},{... | collective-permute-start | bytes 98312 | tf_op jit(solution)/shard_map/ppermute | solution.py:73

commit v8 on v7

--- a/solution.py
+++ b/solution.py
@@ -14,6 +14,8 @@
 SCALE = 1024.0
 OPEN_VMEM = 52 * 1024 * 1024
 CHIP_ORDER = (2, 1, 3)
+COL_ORDER = (2, 3, 1)
+ROW_ORDER = (2, 3, 1)
 VMEM = pl.BlockSpec(memory_space=pltpu.VMEM)
 PARAMS = pltpu.CompilerParams(vmem_limit_bytes=32 * 1024 * 1024)
 
@@ -314,17 +316,17 @@
             compiler_params=PARAMS,
         )(*local[0], *local[1], query, carry, near_start, far_start, decay, *(() if early else (out,)))
 
-    others = [across_blocks(block, k) for k in CHIP_ORDER]
+    others = [across_blocks(block, k) for k in COL_ORDER]
     others, query, local = lax.optimization_barrier((others, query, local))
     before = jnp.zeros_like(block)
     total = power(tokens * (3 - col)) * block
-    for k, other in zip(CHIP_ORDER, others):
+    for k, other in zip(COL_ORDER, others):
         before = before + power(tokens * (col - 1 - (col ^ k))) * other
         total = total + power(tokens * (3 - (col ^ k))) * other
     total, out = lax.optimization_barrier((total, final(before)))
-    others = [across_blocks(total, 4 * k) for k in CHIP_ORDER]
+    others = [across_blocks(total, 4 * k) for k in ROW_ORDER]
     carry = jnp.zeros_like(block)
-    for k, other in zip(CHIP_ORDER, others):
+    for k, other in zip(ROW_ORDER, others):
         carry = carry + power(4 * tokens * (row - 1 - (row ^ k))) * other
     return final(before + power(tokens * col) * carry, out)
 

time: 33.7 us -> 32.7 us (0.970)
  the two profiles are of different devices: /device:TPU:0 before, /device:TPU:40 now
where the time goes in v8:
time: 32.7 us; the launch traced here: 32.5 us
  starting transfers between devices  18.4 us (56%)
  Pallas kernels  9.05 us (28%)
  waiting for transfers between devices  4.3 us (13%)
  other arithmetic  0.53 us (2%)
    ppermute x6, starting transfers between devices, across_blocks(): lax.ppermute(value, 'ctx', [(i, i ^ bits) for i in range(lax.axis_size('c...  9.02 us
    all_to_all x1, starting transfers between devices, per_device(): query = lax.all_to_all(query, 'tp', 0, 0).reshape(tokens, channels)  4.93 us
    ppermute x3, starting transfers between devices, across_chips(): lax.ppermute(value, 'tp', [(i, i ^ 2 * k) for i in range(lax.axis_size('t...  4.17 us
    ppermute x6, waiting for transfers between devices, across_blocks(): lax.ppermute(value, 'ctx', [(i, i ^ bits) for i in range(lax.axis_size('c...  3.83 us
    pallas_call x2, Pallas kernels, per_device(): pl.pallas_call(functools.partial(local_kernel, modes, begin), in_specs=[V...  2.81 us
    pallas_call x2, Pallas kernels, final(): pl.pallas_call(functools.partial(final_kernel, modes, early), in_specs=[V...  2.17 us
    pallas_call x2, Pallas kernels, states(): pl.pallas_call(functools.partial(state_kernel, modes), in_specs=[VMEM] *...  1.7 us
    pallas_call x1, Pallas kernels, per_device(): pl.pallas_call(open_kernel, in_specs=[pl.BlockSpec(memory_space=pl.ANY)],...  1.52 us
  transfers between devices with their start and end apart: 11, of which 5 were waited for; matrix products, arithmetic and copies ran while one was open for 1% of the time, Pallas kernels for 16%

profile of v8, /device:TPU:40, one launch (start us, length us, event | category | flops | bytes accessed | tf_op | source)
XLA Modules:
  0.0 32.5 jit_solution(4285900806909606173)
XLA Ops:
  0.0 1.5 %shard_map.46 = (bf16[2,64,512]{2,1,0:T(8,128)(2,1)S(1)}, bf16[2,64,512]{2,1,0:T(8,128)(2,1)S(1)}, bf16[2,64,512]{2,1,0:T(8,128)(2,1)S(1)}, bf16[2,64,512]{2,1,0:T(8,128)(2,1)S(1)}) custom-call(bf16[3,64,4096]{2,1,0:T(8,128)(2,1)} %qkv_ref.3), custom_call_target="tpu_custom_call" | custom-call | tf_op jit(solution)/shard_map/pallas_call | solution.py:219
  1.5 2.4 %collective-permute-start = (bf16[2,64,512]{2,1,0:T(8,128)(2,1)S(1)}, bf16[2,64,512]{2,1,0:T(8,128)(2,1)S(1)}, u32[]{:S(2)}, u32[]{:S(2)}) collective-permute-start(bf16[2,64,512]{2,1,0:T(8,128)(2,1)S(1)} %get-tuple-element.33), channel_id=1, source_target_pairs={{0,4},{1,5},{2,6},{3,7},{4,0},{5,1},{6,2},{7,3},{8,12},{9,13},{10,... | collective-permute-start | bytes 393224 | tf_op jit(solution)/shard_map/ppermute | solution.py:71
  3.9 1.3 %collective-permute-start.1 = (bf16[2,64,512]{2,1,0:T(8,128)(2,1)S(1)}, bf16[2,64,512]{2,1,0:T(8,128)(2,1)S(1)}, u32[]{:S(2)}, u32[]{:S(2)}) collective-permute-start(bf16[2,64,512]{2,1,0:T(8,128)(2,1)S(1)} %get-tuple-element.34), channel_id=1, source_target_pairs={{0,2},{1,3},{2,0},{3,1},{4,6},{5,7},{6,4},{7,5},{8,10},{9,11},{10,... | collective-permute-start | bytes 393224 | tf_op jit(solution)/shard_map/ppermute | solution.py:71
  5.3 0.5 %collective-permute-start.2 = (bf16[2,64,512]{2,1,0:T(8,128)(2,1)S(1)}, bf16[2,64,512]{2,1,0:T(8,128)(2,1)S(1)}, u32[]{:S(2)}, u32[]{:S(2)}) collective-permute-start(bf16[2,64,512]{2,1,0:T(8,128)(2,1)S(1)} %get-tuple-element.35), channel_id=1, source_target_pairs={{0,6},{1,7},{2,4},{3,5},{4,2},{5,3},{6,0},{7,1},{8,14},{9,15},{10,... | collective-permute-start | bytes 393224 | tf_op jit(solution)/shard_map/ppermute | solution.py:71
  5.7 0.9 %shard_map.49 = bf16[8,64,512]{2,1,0:T(8,128)(2,1)} custom-call(bf16[3,64,4096]{2,1,0:T(8,128)(2,1)S(1)} %copy-done), custom_call_target="tpu_custom_call" | custom-call | tf_op jit(solution)/shard_map/pallas_call | solution.py:231
  6.6 0.0 copy-start.3
  6.6 4.9 %all-to-all-start = ((bf16[8,64,512]{2,1,0:T(8,128)(2,1)}), bf16[8,64,512]{2,1,0:T(8,128)(2,1)S(1)}, u32[]{:S(2)}, u32[]{:S(2)}) async-start(bf16[8,64,512]{2,1,0:T(8,128)(2,1)} %shard_map.49), calls=%async_computation | async-start | bytes 1048576 | tf_op jit(solution)/shard_map/all_to_all | solution.py:241
  11.6 0.1 multiply_exponential_fusion
  11.8 0.0 collective-permute-done
  11.8 0.0 collective-permute-done.1
  11.9 0.2 collective-permute-start.3
  12.2 0.9 %shard_map.47 = (f32[4,256,128]{2,1,0:T(8,128)S(1)}, f32[16,8,512]{2,1,0:T(8,128)S(1)}, f32[16,512]{1,0:T(8,128)S(1)}) custom-call(bf16[4,64,512]{2,1,0:T(8,128)(2,1)S(1)} %pad_maximum_fusion.1.code_ref, f32[16,512]{1,0:T(8,128)S(1)} %get-tuple-element.77.decay_ref.refs_4_.refs_8_, f32[16,8,512]{2,1,0:T(8,128)S(1)} %get-tuple-element.73.tail_ref, ...), custom_call_target="tpu_custom_call" | custom-call | flops 1000 | bytes 1000 | tf_op jit(solution)/shard_map/pallas_call | solution.py:261
  13.1 0.5 %collective-permute-done.3.code_ref = bf16[4,64,512]{2,1,0:T(8,128)(2,1)S(1)} collective-permute-done((bf16[4,64,512]{2,1,0:T(8,128)(2,1)S(1)}, bf16[4,64,512]{2,1,0:T(8,128)(2,1)S(1)}, u32[]{:S(2)}, u32[]{:S(2)}) %collective-permute-start.3) | collective-permute-done | bytes 262176 | tf_op jit(solution)/shard_map/ppermute | solution.py:67
  13.5 0.8 %shard_map.48 = (f32[4,256,128]{2,1,0:T(8,128)S(1)}, f32[16,8,512]{2,1,0:T(8,128)S(1)}, f32[16,512]{1,0:T(8,128)S(1)}) custom-call(bf16[4,64,512]{2,1,0:T(8,128)(2,1)S(1)} %collective-permute-done.3.code_ref, f32[16,512]{1,0:T(8,128)S(1)} %get-tuple-element.77.decay_ref.refs_4_.refs_8_, f32[16,8,512]{2,1,0:T(8,128)S(1)} %get-tuple-element.74.tail_ref, ...), custom_call_target="tpu_custom_call" | custom-call | flops 1000 | bytes 1000 | tf_op jit(solution)/shard_map/pallas_call | solution.py:261
  14.4 3.1 %collective-permute-start.4 = (f32[16,512]{1,0:T(8,128)S(1)}, f32[16,512]{1,0:T(8,128)S(1)}, u32[]{:S(2)}, u32[]{:S(2)}) collective-permute-start(f32[16,512]{1,0:T(8,128)S(1)} %get-tuple-element.38), channel_id=1, source_target_pairs={{0,16},{8,24},{16,0},{24,8},{32,48},{40,56},{48,32},{56,40},{64,80... | collective-permute-start | bytes 98312 | tf_op jit(solution)/shard_map/ppermute | solution.py:75
  17.5 1.1 %collective-permute-start.5 = (f32[16,512]{1,0:T(8,128)S(1)}, f32[16,512]{1,0:T(8,128)S(1)}, u32[]{:S(2)}, u32[]{:S(2)}) collective-permute-start(f32[16,512]{1,0:T(8,128)S(1)} %get-tuple-element.38), channel_id=1, source_target_pairs={{0,24},{8,16},{16,8},{24,0},{32,56},{40,48},{48,40},{56,32},{64,88... | collective-permute-start | bytes 98312 | tf_op jit(solution)/shard_map/ppermute | solution.py:75
  18.6 0.0 collective-permute-start.6
  18.6 0.1 exponential_multiply_fusion
  18.8 1.4 %shard_map.51 = (f32[2,256,128]{2,1,0:T(8,128)S(1)}, f32[2,256,128]{2,1,0:T(8,128)S(1)}) custom-call(f32[4,256,128]{2,1,0:T(8,128)S(1)} %get-tuple-element.39.refs_0_, f32[4,256,128]{2,1,0:T(8,128)S(1)} %get-tuple-element.40.refs_1_, f32[16,8,512]{2,1,0:T(8,128)S(1)} %get-tuple-element.41.refs_2_, f32[16,8,512]{2,1,0:T(8,128)S(1)} %get-tuple-element.42.refs_3_, ...), custom_call_target="tpu_custom_call" | custom-call | flops 40000000 | bytes 4000000 | tf_op jit(solution)/shard_map/pallas_call | solution.py:280
  20.2 1.4 %shard_map.50 = (f32[2,256,128]{2,1,0:T(8,128)S(1)}, f32[2,256,128]{2,1,0:T(8,128)S(1)}) custom-call(f32[4,256,128]{2,1,0:T(8,128)S(1)} %get-tuple-element.39.refs_0_, f32[4,256,128]{2,1,0:T(8,128)S(1)} %get-tuple-element.40.refs_1_, f32[16,8,512]{2,1,0:T(8,128)S(1)} %get-tuple-element.41.refs_2_, f32[16,8,512]{2,1,0:T(8,128)S(1)} %get-tuple-element.42.refs_3_, ...), custom_call_target="tpu_custom_call" | custom-call | flops 40000000 | bytes 4000000 | tf_op jit(solution)/shard_map/pallas_call | solution.py:280
  21.6 1.0 %collective-permute-done.5 = f32[16,512]{1,0:T(8,128)S(1)} collective-permute-done((f32[16,512]{1,0:T(8,128)S(1)}, f32[16,512]{1,0:T(8,128)S(1)}, u32[]{:S(2)}, u32[]{:S(2)}) %collective-permute-start.5) | collective-permute-done | bytes 32800 | tf_op jit(solution)/shard_map/ppermute | solution.py:75
  22.6 0.0 collective-permute-done.6
  22.6 0.0 all-to-all-done
  22.6 0.1 multiply_add_fusion.1
  22.7 0.1 shard_map.52.refs_9_
  22.7 3.1 %collective-permute-start.7 = (f32[16,512]{1,0:T(8,128)S(1)}, f32[16,512]{1,0:T(8,128)S(1)}, u32[]{:S(2)}, u32[]{:S(2)}) collective-permute-start(f32[16,512]{1,0:T(8,128)S(1)} %get-tuple-element.57), channel_id=1, source_target_pairs={{0,64},{8,72},{16,80},{24,88},{32,96},{40,104},{48,112},{56,120},{... | collective-permute-start | bytes 98312 | tf_op jit(solution)/shard_map/ppermute | solution.py:75
  25.8 0.6 %collective-permute-start.8 = (f32[16,512]{1,0:T(8,128)S(1)}, f32[16,512]{1,0:T(8,128)S(1)}, u32[]{:S(2)}, u32[]{:S(2)}) collective-permute-start(f32[16,512]{1,0:T(8,128)S(1)} %get-tuple-element.57), channel_id=1, source_target_pairs={{0,96},{8,104},{16,112},{24,120},{32,64},{40,72},{48,80},{56,88},{... | collective-permute-start | bytes 98312 | tf_op jit(solution)/shard_map/ppermute | solution.py:75
  26.4 1.1 %collective-permute-start.9 = (f32[16,512]{1,0:T(8,128)S(1)}, f32[16,512]{1,0:T(8,128)S(1)}, u32[]{:S(2)}, u32[]{:S(2)}) collective-permute-start(f32[16,512]{1,0:T(8,128)S(1)} %get-tuple-element.57), channel_id=1, source_target_pairs={{0,32},{8,40},{16,48},{24,56},{32,0},{40,8},{48,16},{56,24},{64,96... | collective-permute-start | bytes 98312 | tf_op jit(solution)/shard_map/ppermute | solution.py:75
  27.5 0.9 %collective-permute-done.7 = f32[16,512]{1,0:T(8,128)S(1)} collective-permute-done((f32[16,512]{1,0:T(8,128)S(1)}, f32[16,512]{1,0:T(8,128)S(1)}, u32[]{:S(2)}, u32[]{:S(2)}) %collective-permute-start.7) | collective-permute-done | bytes 32800 | tf_op jit(solution)/shard_map/ppermute | solution.py:75
  28.5 1.2 %collective-permute-done.8 = f32[16,512]{1,0:T(8,128)S(1)} collective-permute-done((f32[16,512]{1,0:T(8,128)S(1)}, f32[16,512]{1,0:T(8,128)S(1)}, u32[]{:S(2)}, u32[]{:S(2)}) %collective-permute-start.8) | collective-permute-done | bytes 32800 | tf_op jit(solution)/shard_map/ppermute | solution.py:75
  29.7 0.6 %collective-permute-done.9 = f32[16,512]{1,0:T(8,128)S(1)} collective-permute-done((f32[16,512]{1,0:T(8,128)S(1)}, f32[16,512]{1,0:T(8,128)S(1)}, u32[]{:S(2)}, u32[]{:S(2)}) %collective-permute-start.9) | collective-permute-done | bytes 32800 | tf_op jit(solution)/shard_map/ppermute | solution.py:75
  30.4 2.1 %shard_map.53 = bf16[512,512]{1,0:T(8,128)(2,1)} custom-call(f32[2,256,128]{2,1,0:T(8,128)S(1)} %get-tuple-element.49.refs_0_, f32[2,256,128]{2,1,0:T(8,128)S(1)} %get-tuple-element.50.refs_1_, f32[2,256,128]{2,1,0:T(8,128)S(1)} %get-tuple-element.51.refs_2_, f32[2,256,128]{2,1,0:T(8,128)S(1)} %get-tuple-element.52.refs_3_, ...), custom_call_target="tpu_custom_call", output_to_operand_aliasing={{}: (9, {})} | custom-call | tf_op jit(solution)/shard_map/pallas_call | solution.py:305
  (23 shorter events, 0.2 us)
Async XLA Ops:
  0.0 5.7 %copy-start = (bf16[3,64,4096]{2,1,0:T(8,128)(2,1)S(1)}, bf16[3,64,4096]{2,1,0:T(8,128)(2,1)}, u32[]{:S(2)}) copy-start(bf16[3,64,4096]{2,1,0:T(8,128)(2,1)} %qkv_ref.3) | copy-start | bytes 4718596
  1.5 10.2 %collective-permute-start = (bf16[2,64,512]{2,1,0:T(8,128)(2,1)S(1)}, bf16[2,64,512]{2,1,0:T(8,128)(2,1)S(1)}, u32[]{:S(2)}, u32[]{:S(2)}) collective-permute-start(bf16[2,64,512]{2,1,0:T(8,128)(2,1)S(1)} %get-tuple-element.33), channel_id=1, source_target_pairs={{0,4},{1,5},{2,6},{3,7},{4,0},{5,1},{6,2},{7,3},{8,12},{9,13},{10,... | collective-permute-start | bytes 393224 | tf_op jit(solution)/shard_map/ppermute | solution.py:71
  3.9 7.9 %collective-permute-start.1 = (bf16[2,64,512]{2,1,0:T(8,128)(2,1)S(1)}, bf16[2,64,512]{2,1,0:T(8,128)(2,1)S(1)}, u32[]{:S(2)}, u32[]{:S(2)}) collective-permute-start(bf16[2,64,512]{2,1,0:T(8,128)(2,1)S(1)} %get-tuple-element.34), channel_id=1, source_target_pairs={{0,2},{1,3},{2,0},{3,1},{4,6},{5,7},{6,4},{7,5},{8,10},{9,11},{10,... | collective-permute-start | bytes 393224 | tf_op jit(solution)/shard_map/ppermute | solution.py:71
  5.3 6.3 %copy-start.1 = (f32[512,16]{0,1:T(8,128)S(1)}, f32[512,16]{0,1:T(8,128)}, u32[]{:S(2)}) copy-start(f32[512,16]{0,1:T(8,128)} %param.6) | copy-start | bytes 98308
  5.3 6.3 %copy-start.2 = (f32[512,16]{0,1:T(8,128)S(1)}, f32[512,16]{0,1:T(8,128)}, u32[]{:S(2)}) copy-start(f32[512,16]{0,1:T(8,128)} %param.5) | copy-start | bytes 98308
  5.3 6.6 %collective-permute-start.2 = (bf16[2,64,512]{2,1,0:T(8,128)(2,1)S(1)}, bf16[2,64,512]{2,1,0:T(8,128)(2,1)S(1)}, u32[]{:S(2)}, u32[]{:S(2)}) collective-permute-start(bf16[2,64,512]{2,1,0:T(8,128)(2,1)S(1)} %get-tuple-element.35), channel_id=1, source_target_pairs={{0,6},{1,7},{2,4},{3,5},{4,2},{5,3},{6,0},{7,1},{8,14},{9,15},{10,... | collective-permute-start | bytes 393224 | tf_op jit(solution)/shard_map/ppermute | solution.py:71
  6.6 5.6 %copy-start.3 = (f32[512]{0:T(512)S(1)}, f32[512]{0:T(512)}, u32[]{:S(2)}) copy-start(f32[512]{0:T(512)} %param.7) | copy-start | bytes 6148
  6.6 16.0 %all-to-all-start = ((bf16[8,64,512]{2,1,0:T(8,128)(2,1)}), bf16[8,64,512]{2,1,0:T(8,128)(2,1)S(1)}, u32[]{:S(2)}, u32[]{:S(2)}) async-start(bf16[8,64,512]{2,1,0:T(8,128)(2,1)} %shard_map.49), calls=%async_computation | async-start | bytes 1048576 | tf_op jit(solution)/shard_map/all_to_all | solution.py:241
  11.9 1.6 %collective-permute-start.3 = (bf16[4,64,512]{2,1,0:T(8,128)(2,1)S(1)}, bf16[4,64,512]{2,1,0:T(8,128)(2,1)S(1)}, u32[]{:S(2)}, u32[]{:S(2)}) collective-permute-start(bf16[4,64,512]{2,1,0:T(8,128)(2,1)S(1)} %pad_maximum_fusion), channel_id=1, source_target_pairs={{0,1},{1,0},{2,3},{3,2},{4,5},{5,4},{6,7},{7,6},{8,9},{9,8},{10,11... | collective-permute-start | bytes 786440 | tf_op jit(solution)/shard_map/ppermute | solution.py:67
  14.4 7.2 %collective-permute-start.4 = (f32[16,512]{1,0:T(8,128)S(1)}, f32[16,512]{1,0:T(8,128)S(1)}, u32[]{:S(2)}, u32[]{:S(2)}) collective-permute-start(f32[16,512]{1,0:T(8,128)S(1)} %get-tuple-element.38), channel_id=1, source_target_pairs={{0,16},{8,24},{16,0},{24,8},{32,48},{40,56},{48,32},{56,40},{64,80... | collective-permute-start | bytes 98312 | tf_op jit(solution)/shard_map/ppermute | solution.py:75
  17.5 5.1 %collective-permute-start.5 = (f32[16,512]{1,0:T(8,128)S(1)}, f32[16,512]{1,0:T(8,128)S(1)}, u32[]{:S(2)}, u32[]{:S(2)}) collective-permute-start(f32[16,512]{1,0:T(8,128)S(1)} %get-tuple-element.38), channel_id=1, source_target_pairs={{0,24},{8,16},{16,8},{24,0},{32,56},{40,48},{48,40},{56,32},{64,88... | collective-permute-start | bytes 98312 | tf_op jit(solution)/shard_map/ppermute | solution.py:75
  18.6 4.0 %collective-permute-start.6 = (f32[16,512]{1,0:T(8,128)S(1)}, f32[16,512]{1,0:T(8,128)S(1)}, u32[]{:S(2)}, u32[]{:S(2)}) collective-permute-start(f32[16,512]{1,0:T(8,128)S(1)} %get-tuple-element.38), channel_id=1, source_target_pairs={{0,8},{8,0},{16,24},{24,16},{32,40},{40,32},{48,56},{56,48},{64,72... | collective-permute-start | bytes 98312 | tf_op jit(solution)/shard_map/ppermute | solution.py:75
  22.7 5.7 %collective-permute-start.7 = (f32[16,512]{1,0:T(8,128)S(1)}, f32[16,512]{1,0:T(8,128)S(1)}, u32[]{:S(2)}, u32[]{:S(2)}) collective-permute-start(f32[16,512]{1,0:T(8,128)S(1)} %get-tuple-element.57), channel_id=1, source_target_pairs={{0,64},{8,72},{16,80},{24,88},{32,96},{40,104},{48,112},{56,120},{... | collective-permute-start | bytes 98312 | tf_op jit(solution)/shard_map/ppermute | solution.py:75
  25.8 3.9 %collective-permute-start.8 = (f32[16,512]{1,0:T(8,128)S(1)}, f32[16,512]{1,0:T(8,128)S(1)}, u32[]{:S(2)}, u32[]{:S(2)}) collective-permute-start(f32[16,512]{1,0:T(8,128)S(1)} %get-tuple-element.57), channel_id=1, source_target_pairs={{0,96},{8,104},{16,112},{24,120},{32,64},{40,72},{48,80},{56,88},{... | collective-permute-start | bytes 98312 | tf_op jit(solution)/shard_map/ppermute | solution.py:75
  26.4 3.9 %collective-permute-start.9 = (f32[16,512]{1,0:T(8,128)S(1)}, f32[16,512]{1,0:T(8,128)S(1)}, u32[]{:S(2)}, u32[]{:S(2)}) collective-permute-start(f32[16,512]{1,0:T(8,128)S(1)} %get-tuple-element.57), channel_id=1, source_target_pairs={{0,32},{8,40},{16,48},{24,56},{32,0},{40,8},{48,16},{56,24},{64,96... | collective-permute-start | bytes 98312 | tf_op jit(solution)/shard_map/ppermute | solution.py:75

commit v9 on v8

--- a/solution.py
+++ b/solution.py
@@ -323,8 +323,8 @@
     for k, other in zip(COL_ORDER, others):
         before = before + power(tokens * (col - 1 - (col ^ k))) * other
         total = total + power(tokens * (3 - (col ^ k))) * other
-    total, out = lax.optimization_barrier((total, final(before)))
     others = [across_blocks(total, 4 * k) for k in ROW_ORDER]
+    others, out = lax.optimization_barrier((others, final(before)))
     carry = jnp.zeros_like(block)
     for k, other in zip(ROW_ORDER, others):
         carry = carry + power(4 * tokens * (row - 1 - (row ^ k))) * other

time: 32.7 us -> 32.1 us (0.982)
  the two profiles are of different devices: /device:TPU:40 before, /device:TPU:0 now
where the time goes in v9:
time: 32.1 us; the launch traced here: 31.8 us
  starting transfers between devices  18.3 us (57%)
  Pallas kernels  9.05 us (28%)
  waiting for transfers between devices  3.67 us (11%)
  other arithmetic  0.53 us (2%)
    ppermute x6, starting transfers between devices, across_blocks(): lax.ppermute(value, 'ctx', [(i, i ^ bits) for i in range(lax.axis_size('c...  9.28 us
    ppermute x3, starting transfers between devices, across_chips(): lax.ppermute(value, 'tp', [(i, i ^ 2 * k) for i in range(lax.axis_size('t...  4.41 us
    all_to_all x1, starting transfers between devices, per_device(): query = lax.all_to_all(query, 'tp', 0, 0).reshape(tokens, channels)  4.32 us
    ppermute x6, waiting for transfers between devices, across_blocks(): lax.ppermute(value, 'ctx', [(i, i ^ bits) for i in range(lax.axis_size('c...  2.98 us
    pallas_call x2, Pallas kernels, per_device(): pl.pallas_call(functools.partial(local_kernel, modes, begin), in_specs=[V...  2.81 us
    pallas_call x2, Pallas kernels, final(): pl.pallas_call(functools.partial(final_kernel, modes, early), in_specs=[V...  2.17 us
    pallas_call x2, Pallas kernels, states(): pl.pallas_call(functools.partial(state_kernel, modes), in_specs=[VMEM] *...  1.7 us
    pallas_call x1, Pallas kernels, per_device(): pl.pallas_call(open_kernel, in_specs=[pl.BlockSpec(memory_space=pl.ANY)],...  1.52 us
  transfers between devices with their start and end apart: 11, of which 5 were waited for; matrix products, arithmetic and copies ran while one was open for 2% of the time, Pallas kernels for 23%

profile of v9, /device:TPU:0, one launch (start us, length us, event | category | flops | bytes accessed | tf_op | source)
XLA Modules:
  0.0 31.8 jit_solution(5816104286762533164)
XLA Ops:
  0.0 1.5 %shard_map.46 = (bf16[2,64,512]{2,1,0:T(8,128)(2,1)S(1)}, bf16[2,64,512]{2,1,0:T(8,128)(2,1)S(1)}, bf16[2,64,512]{2,1,0:T(8,128)(2,1)S(1)}, bf16[2,64,512]{2,1,0:T(8,128)(2,1)S(1)}) custom-call(bf16[3,64,4096]{2,1,0:T(8,128)(2,1)} %qkv_ref.3), custom_call_target="tpu_custom_call" | custom-call | tf_op jit(solution)/shard_map/pallas_call | solution.py:219
  1.5 3.4 %collective-permute-start = (bf16[2,64,512]{2,1,0:T(8,128)(2,1)S(1)}, bf16[2,64,512]{2,1,0:T(8,128)(2,1)S(1)}, u32[]{:S(2)}, u32[]{:S(2)}) collective-permute-start(bf16[2,64,512]{2,1,0:T(8,128)(2,1)S(1)} %get-tuple-element.35), channel_id=1, source_target_pairs={{0,4},{1,5},{2,6},{3,7},{4,0},{5,1},{6,2},{7,3},{8,12},{9,13},{10,... | collective-permute-start | bytes 393224 | tf_op jit(solution)/shard_map/ppermute | solution.py:71
  4.9 0.7 %collective-permute-start.1 = (bf16[2,64,512]{2,1,0:T(8,128)(2,1)S(1)}, bf16[2,64,512]{2,1,0:T(8,128)(2,1)S(1)}, u32[]{:S(2)}, u32[]{:S(2)}) collective-permute-start(bf16[2,64,512]{2,1,0:T(8,128)(2,1)S(1)} %get-tuple-element.36), channel_id=1, source_target_pairs={{0,2},{1,3},{2,0},{3,1},{4,6},{5,7},{6,4},{7,5},{8,10},{9,11},{10,... | collective-permute-start | bytes 393224 | tf_op jit(solution)/shard_map/ppermute | solution.py:71
  5.6 0.4 %collective-permute-start.2 = (bf16[2,64,512]{2,1,0:T(8,128)(2,1)S(1)}, bf16[2,64,512]{2,1,0:T(8,128)(2,1)S(1)}, u32[]{:S(2)}, u32[]{:S(2)}) collective-permute-start(bf16[2,64,512]{2,1,0:T(8,128)(2,1)S(1)} %get-tuple-element.37), channel_id=1, source_target_pairs={{0,6},{1,7},{2,4},{3,5},{4,2},{5,3},{6,0},{7,1},{8,14},{9,15},{10,... | collective-permute-start | bytes 393224 | tf_op jit(solution)/shard_map/ppermute | solution.py:71
  6.0 0.9 %shard_map.49 = bf16[8,64,512]{2,1,0:T(8,128)(2,1)} custom-call(bf16[3,64,4096]{2,1,0:T(8,128)(2,1)S(1)} %copy-done), custom_call_target="tpu_custom_call" | custom-call | tf_op jit(solution)/shard_map/pallas_call | solution.py:231
  6.8 0.0 copy-start.3
  6.8 4.3 %all-to-all-start = ((bf16[8,64,512]{2,1,0:T(8,128)(2,1)}), bf16[8,64,512]{2,1,0:T(8,128)(2,1)S(1)}, u32[]{:S(2)}, u32[]{:S(2)}) async-start(bf16[8,64,512]{2,1,0:T(8,128)(2,1)} %shard_map.49), calls=%async_computation | async-start | bytes 1048576 | tf_op jit(solution)/shard_map/all_to_all | solution.py:241
  11.2 0.1 multiply_exponential_fusion
  11.4 0.1 collective-permute-done.1
  11.6 0.2 collective-permute-done.2
  11.8 0.3 collective-permute-start.3
  12.2 0.9 %shard_map.47 = (f32[4,256,128]{2,1,0:T(8,128)S(1)}, f32[16,8,512]{2,1,0:T(8,128)S(1)}, f32[16,512]{1,0:T(8,128)S(1)}) custom-call(bf16[4,64,512]{2,1,0:T(8,128)(2,1)S(1)} %pad_maximum_fusion.1.code_ref, f32[16,512]{1,0:T(8,128)S(1)} %get-tuple-element.81.decay_ref.refs_4_.refs_8_, f32[16,8,512]{2,1,0:T(8,128)S(1)} %get-tuple-element.77.tail_ref, ...), custom_call_target="tpu_custom_call" | custom-call | flops 1000 | bytes 1000 | tf_op jit(solution)/shard_map/pallas_call | solution.py:261
  13.1 0.4 %collective-permute-done.3.code_ref = bf16[4,64,512]{2,1,0:T(8,128)(2,1)S(1)} collective-permute-done((bf16[4,64,512]{2,1,0:T(8,128)(2,1)S(1)}, bf16[4,64,512]{2,1,0:T(8,128)(2,1)S(1)}, u32[]{:S(2)}, u32[]{:S(2)}) %collective-permute-start.3) | collective-permute-done | bytes 262176 | tf_op jit(solution)/shard_map/ppermute | solution.py:67
  13.4 0.8 %shard_map.48 = (f32[4,256,128]{2,1,0:T(8,128)S(1)}, f32[16,8,512]{2,1,0:T(8,128)S(1)}, f32[16,512]{1,0:T(8,128)S(1)}) custom-call(bf16[4,64,512]{2,1,0:T(8,128)(2,1)S(1)} %collective-permute-done.3.code_ref, f32[16,512]{1,0:T(8,128)S(1)} %get-tuple-element.81.decay_ref.refs_4_.refs_8_, f32[16,8,512]{2,1,0:T(8,128)S(1)} %get-tuple-element.78.tail_ref, ...), custom_call_target="tpu_custom_call" | custom-call | flops 1000 | bytes 1000 | tf_op jit(solution)/shard_map/pallas_call | solution.py:261
  14.3 3.2 %collective-permute-start.4 = (f32[16,512]{1,0:T(8,128)S(1)}, f32[16,512]{1,0:T(8,128)S(1)}, u32[]{:S(2)}, u32[]{:S(2)}) collective-permute-start(f32[16,512]{1,0:T(8,128)S(1)} %get-tuple-element.40), channel_id=1, source_target_pairs={{0,16},{8,24},{16,0},{24,8},{32,48},{40,56},{48,32},{56,40},{64,80... | collective-permute-start | bytes 98312 | tf_op jit(solution)/shard_map/ppermute | solution.py:75
  17.4 1.1 %collective-permute-start.5 = (f32[16,512]{1,0:T(8,128)S(1)}, f32[16,512]{1,0:T(8,128)S(1)}, u32[]{:S(2)}, u32[]{:S(2)}) collective-permute-start(f32[16,512]{1,0:T(8,128)S(1)} %get-tuple-element.40), channel_id=1, source_target_pairs={{0,24},{8,16},{16,8},{24,0},{32,56},{40,48},{48,40},{56,32},{64,88... | collective-permute-start | bytes 98312 | tf_op jit(solution)/shard_map/ppermute | solution.py:75
  18.6 0.0 collective-permute-start.6
  18.6 1.4 %shard_map.51 = (f32[2,256,128]{2,1,0:T(8,128)S(1)}, f32[2,256,128]{2,1,0:T(8,128)S(1)}) custom-call(f32[4,256,128]{2,1,0:T(8,128)S(1)} %get-tuple-element.41.refs_0_, f32[4,256,128]{2,1,0:T(8,128)S(1)} %get-tuple-element.42.refs_1_, f32[16,8,512]{2,1,0:T(8,128)S(1)} %get-tuple-element.43.refs_2_, f32[16,8,512]{2,1,0:T(8,128)S(1)} %get-tuple-element.44.refs_3_, ...), custom_call_target="tpu_custom_call" | custom-call | flops 40000000 | bytes 4000000 | tf_op jit(solution)/shard_map/pallas_call | solution.py:280
  20.0 1.4 %shard_map.50 = (f32[2,256,128]{2,1,0:T(8,128)S(1)}, f32[2,256,128]{2,1,0:T(8,128)S(1)}) custom-call(f32[4,256,128]{2,1,0:T(8,128)S(1)} %get-tuple-element.41.refs_0_, f32[4,256,128]{2,1,0:T(8,128)S(1)} %get-tuple-element.42.refs_1_, f32[16,8,512]{2,1,0:T(8,128)S(1)} %get-tuple-element.43.refs_2_, f32[16,8,512]{2,1,0:T(8,128)S(1)} %get-tuple-element.44.refs_3_, ...), custom_call_target="tpu_custom_call" | custom-call | flops 40000000 | bytes 4000000 | tf_op jit(solution)/shard_map/pallas_call | solution.py:280
  21.4 0.0 collective-permute-done.4
  21.4 1.1 %collective-permute-done.5 = f32[16,512]{1,0:T(8,128)S(1)} collective-permute-done((f32[16,512]{1,0:T(8,128)S(1)}, f32[16,512]{1,0:T(8,128)S(1)}, u32[]{:S(2)}, u32[]{:S(2)}) %collective-permute-start.5) | collective-permute-done | bytes 32800 | tf_op jit(solution)/shard_map/ppermute | solution.py:75
  22.6 0.0 collective-permute-done.6
  22.6 0.0 all-to-all-done
  22.6 0.1 multiply_add_fusion.1
  22.6 4.0 %collective-permute-start.7 = (f32[16,512]{1,0:T(8,128)S(1)}, f32[16,512]{1,0:T(8,128)S(1)}, u32[]{:S(2)}, u32[]{:S(2)}) collective-permute-start(f32[16,512]{1,0:T(8,128)S(1)} %get-tuple-element.63), channel_id=1, source_target_pairs={{0,64},{8,72},{16,80},{24,88},{32,96},{40,104},{48,112},{56,120},{... | collective-permute-start | bytes 98312 | tf_op jit(solution)/shard_map/ppermute | solution.py:75
  26.6 0.7 %collective-permute-start.8 = (f32[16,512]{1,0:T(8,128)S(1)}, f32[16,512]{1,0:T(8,128)S(1)}, u32[]{:S(2)}, u32[]{:S(2)}) collective-permute-start(f32[16,512]{1,0:T(8,128)S(1)} %get-tuple-element.63), channel_id=1, source_target_pairs={{0,96},{8,104},{16,112},{24,120},{32,64},{40,72},{48,80},{56,88},{... | collective-permute-start | bytes 98312 | tf_op jit(solution)/shard_map/ppermute | solution.py:75
  27.3 0.3 collective-permute-start.9
  27.6 0.1 exponential_multiply_fusion
  27.8 2.1 %shard_map.52.refs_9_ = bf16[512,512]{1,0:T(8,128)(2,1)} custom-call(f32[2,256,128]{2,1,0:T(8,128)S(1)} %get-tuple-element.51.refs_0_, f32[2,256,128]{2,1,0:T(8,128)S(1)} %get-tuple-element.52.refs_1_, f32[2,256,128]{2,1,0:T(8,128)S(1)} %get-tuple-element.53.refs_2_, f32[2,256,128]{2,1,0:T(8,128)S(1)} %get-tuple-element.54.refs_3_, ...), custom_call_target="tpu_custom_call" | custom-call | tf_op jit(solution)/shard_map/pallas_call | solution.py:305
  29.9 1.8 %collective-permute-done.8 = f32[16,512]{1,0:T(8,128)S(1)} collective-permute-done((f32[16,512]{1,0:T(8,128)S(1)}, f32[16,512]{1,0:T(8,128)S(1)}, u32[]{:S(2)}, u32[]{:S(2)}) %collective-permute-start.8) | collective-permute-done | bytes 32800 | tf_op jit(solution)/shard_map/ppermute | solution.py:75
  31.7 0.0 collective-permute-done.9
  31.8 0.1 shard_map.53
  (23 shorter events, 0.2 us)
Async XLA Ops:
  0.0 5.9 %copy-start = (bf16[3,64,4096]{2,1,0:T(8,128)(2,1)S(1)}, bf16[3,64,4096]{2,1,0:T(8,128)(2,1)}, u32[]{:S(2)}) copy-start(bf16[3,64,4096]{2,1,0:T(8,128)(2,1)} %qkv_ref.3) | copy-start | bytes 4718596
  1.5 9.9 %collective-permute-start = (bf16[2,64,512]{2,1,0:T(8,128)(2,1)S(1)}, bf16[2,64,512]{2,1,0:T(8,128)(2,1)S(1)}, u32[]{:S(2)}, u32[]{:S(2)}) collective-permute-start(bf16[2,64,512]{2,1,0:T(8,128)(2,1)S(1)} %get-tuple-element.35), channel_id=1, source_target_pairs={{0,4},{1,5},{2,6},{3,7},{4,0},{5,1},{6,2},{7,3},{8,12},{9,13},{10,... | collective-permute-start | bytes 393224 | tf_op jit(solution)/shard_map/ppermute | solution.py:71
  4.9 6.7 %collective-permute-start.1 = (bf16[2,64,512]{2,1,0:T(8,128)(2,1)S(1)}, bf16[2,64,512]{2,1,0:T(8,128)(2,1)S(1)}, u32[]{:S(2)}, u32[]{:S(2)}) collective-permute-start(bf16[2,64,512]{2,1,0:T(8,128)(2,1)S(1)} %get-tuple-element.36), channel_id=1, source_target_pairs={{0,2},{1,3},{2,0},{3,1},{4,6},{5,7},{6,4},{7,5},{8,10},{9,11},{10,... | collective-permute-start | bytes 393224 | tf_op jit(solution)/shard_map/ppermute | solution.py:71
  5.6 5.6 %copy-start.1 = (f32[512,16]{0,1:T(8,128)S(1)}, f32[512,16]{0,1:T(8,128)}, u32[]{:S(2)}) copy-start(f32[512,16]{0,1:T(8,128)} %param.6) | copy-start | bytes 98308
  5.6 5.6 %copy-start.2 = (f32[512,16]{0,1:T(8,128)S(1)}, f32[512,16]{0,1:T(8,128)}, u32[]{:S(2)}) copy-start(f32[512,16]{0,1:T(8,128)} %param.5) | copy-start | bytes 98308
  5.6 6.2 %collective-permute-start.2 = (bf16[2,64,512]{2,1,0:T(8,128)(2,1)S(1)}, bf16[2,64,512]{2,1,0:T(8,128)(2,1)S(1)}, u32[]{:S(2)}, u32[]{:S(2)}) collective-permute-start(bf16[2,64,512]{2,1,0:T(8,128)(2,1)S(1)} %get-tuple-element.37), channel_id=1, source_target_pairs={{0,6},{1,7},{2,4},{3,5},{4,2},{5,3},{6,0},{7,1},{8,14},{9,15},{10,... | collective-permute-start | bytes 393224 | tf_op jit(solution)/shard_map/ppermute | solution.py:71
  6.8 5.3 %copy-start.3 = (f32[512]{0:T(512)S(1)}, f32[512]{0:T(512)}, u32[]{:S(2)}) copy-start(f32[512]{0:T(512)} %param.7) | copy-start | bytes 6148
  6.8 15.7 %all-to-all-start = ((bf16[8,64,512]{2,1,0:T(8,128)(2,1)}), bf16[8,64,512]{2,1,0:T(8,128)(2,1)S(1)}, u32[]{:S(2)}, u32[]{:S(2)}) async-start(bf16[8,64,512]{2,1,0:T(8,128)(2,1)} %shard_map.49), calls=%async_computation | async-start | bytes 1048576 | tf_op jit(solution)/shard_map/all_to_all | solution.py:241
  11.8 1.6 %collective-permute-start.3 = (bf16[4,64,512]{2,1,0:T(8,128)(2,1)S(1)}, bf16[4,64,512]{2,1,0:T(8,128)(2,1)S(1)}, u32[]{:S(2)}, u32[]{:S(2)}) collective-permute-start(bf16[4,64,512]{2,1,0:T(8,128)(2,1)S(1)} %pad_maximum_fusion), channel_id=1, source_target_pairs={{0,1},{1,0},{2,3},{3,2},{4,5},{5,4},{6,7},{7,6},{8,9},{9,8},{10,11... | collective-permute-start | bytes 786440 | tf_op jit(solution)/shard_map/ppermute | solution.py:67
  14.3 7.1 %collective-permute-start.4 = (f32[16,512]{1,0:T(8,128)S(1)}, f32[16,512]{1,0:T(8,128)S(1)}, u32[]{:S(2)}, u32[]{:S(2)}) collective-permute-start(f32[16,512]{1,0:T(8,128)S(1)} %get-tuple-element.40), channel_id=1, source_target_pairs={{0,16},{8,24},{16,0},{24,8},{32,48},{40,56},{48,32},{56,40},{64,80... | collective-permute-start | bytes 98312 | tf_op jit(solution)/shard_map/ppermute | solution.py:75
  17.4 5.1 %collective-permute-start.5 = (f32[16,512]{1,0:T(8,128)S(1)}, f32[16,512]{1,0:T(8,128)S(1)}, u32[]{:S(2)}, u32[]{:S(2)}) collective-permute-start(f32[16,512]{1,0:T(8,128)S(1)} %get-tuple-element.40), channel_id=1, source_target_pairs={{0,24},{8,16},{16,8},{24,0},{32,56},{40,48},{48,40},{56,32},{64,88... | collective-permute-start | bytes 98312 | tf_op jit(solution)/shard_map/ppermute | solution.py:75
  18.6 4.0 %collective-permute-start.6 = (f32[16,512]{1,0:T(8,128)S(1)}, f32[16,512]{1,0:T(8,128)S(1)}, u32[]{:S(2)}, u32[]{:S(2)}) collective-permute-start(f32[16,512]{1,0:T(8,128)S(1)} %get-tuple-element.40), channel_id=1, source_target_pairs={{0,8},{8,0},{16,24},{24,16},{32,40},{40,32},{48,56},{56,48},{64,72... | collective-permute-start | bytes 98312 | tf_op jit(solution)/shard_map/ppermute | solution.py:75
  22.6 7.2 %collective-permute-start.7 = (f32[16,512]{1,0:T(8,128)S(1)}, f32[16,512]{1,0:T(8,128)S(1)}, u32[]{:S(2)}, u32[]{:S(2)}) collective-permute-start(f32[16,512]{1,0:T(8,128)S(1)} %get-tuple-element.63), channel_id=1, source_target_pairs={{0,64},{8,72},{16,80},{24,88},{32,96},{40,104},{48,112},{56,120},{... | collective-permute-start | bytes 98312 | tf_op jit(solution)/shard_map/ppermute | solution.py:75
  26.6 5.1 %collective-permute-start.8 = (f32[16,512]{1,0:T(8,128)S(1)}, f32[16,512]{1,0:T(8,128)S(1)}, u32[]{:S(2)}, u32[]{:S(2)}) collective-permute-start(f32[16,512]{1,0:T(8,128)S(1)} %get-tuple-element.63), channel_id=1, source_target_pairs={{0,96},{8,104},{16,112},{24,120},{32,64},{40,72},{48,80},{56,88},{... | collective-permute-start | bytes 98312 | tf_op jit(solution)/shard_map/ppermute | solution.py:75
  27.3 4.4 %collective-permute-start.9 = (f32[16,512]{1,0:T(8,128)S(1)}, f32[16,512]{1,0:T(8,128)S(1)}, u32[]{:S(2)}, u32[]{:S(2)}) collective-permute-start(f32[16,512]{1,0:T(8,128)S(1)} %get-tuple-element.63), channel_id=1, source_target_pairs={{0,32},{8,40},{16,48},{24,56},{32,0},{40,8},{48,16},{56,24},{64,96... | collective-permute-start | bytes 98312 | tf_op jit(solution)/shard_map/ppermute | solution.py:75

commit v10 on v9

--- a/solution.py
+++ b/solution.py
@@ -172,7 +172,7 @@
 def finish(modes, *refs):
     low_refs, high_refs = refs[0:2], refs[2:4]
     query_ref, carry_ref, near_ref, far_ref, decay_ref, out_ref, sum_ref, held_ref, out_sem = refs[4:]
-    _, groups, tokens, _ = sum_ref.shape
+    groups, tokens = sum_ref.shape[1], low_refs[0].shape[1]
     steps = tokens // SUBS
     core = lax.axis_index("tp") % 2
 
@@ -263,7 +263,7 @@
             in_specs=[VMEM] * 4,
             out_specs=[VMEM] * 3,
             out_shape=[
-                jax.ShapeDtypeStruct((groups, half, LANES), F32),
+                jax.ShapeDtypeStruct((groups, half + SUBS, LANES), F32),
                 jax.ShapeDtypeStruct((modes, SUBS, channels), F32),
                 jax.ShapeDtypeStruct((modes, channels), F32),
             ],
@@ -309,7 +309,7 @@
             out_shape=jax.ShapeDtypeStruct((channels, tokens), BF16),
             input_output_aliases={} if early else {9: 0},
             scratch_shapes=[
-                pltpu.VMEM((2, groups, half, LANES), F32),
+                pltpu.VMEM((2, groups, half + SUBS, LANES), F32),
                 pltpu.VMEM((groups, LANES, tokens), BF16),
                 pltpu.SemaphoreType.DMA((groups,)),
             ],

time: 32.1 us -> 32.1 us (level)
  no operation moved by 1% of the time
where the time goes in v10:
time: 32.1 us; the launch traced here: 31.8 us
  starting transfers between devices  18.3 us (57%)
  Pallas kernels  9.03 us (28%)
  waiting for transfers between devices  3.68 us (11%)
  other arithmetic  0.53 us (2%)
    ppermute x6, starting transfers between devices, across_blocks(): lax.ppermute(value, 'ctx', [(i, i ^ bits) for i in range(lax.axis_size('c...  9.28 us
    ppermute x3, starting transfers between devices, across_chips(): lax.ppermute(value, 'tp', [(i, i ^ 2 * k) for i in range(lax.axis_size('t...  4.41 us
    all_to_all x1, starting transfers between devices, per_device(): query = lax.all_to_all(query, 'tp', 0, 0).reshape(tokens, channels)  4.32 us
    ppermute x6, waiting for transfers between devices, across_blocks(): lax.ppermute(value, 'ctx', [(i, i ^ bits) for i in range(lax.axis_size('c...  2.99 us
    pallas_call x2, Pallas kernels, per_device(): pl.pallas_call(functools.partial(local_kernel, modes, begin), in_specs=[V...  2.79 us
    pallas_call x2, Pallas kernels, final(): pl.pallas_call(functools.partial(final_kernel, modes, early), in_specs=[V...  2.17 us
    pallas_call x2, Pallas kernels, states(): pl.pallas_call(functools.partial(state_kernel, modes), in_specs=[VMEM] *...  1.7 us
    pallas_call x1, Pallas kernels, per_device(): pl.pallas_call(open_kernel, in_specs=[pl.BlockSpec(memory_space=pl.ANY)],...  1.52 us
  transfers between devices with their start and end apart: 11, of which 5 were waited for; matrix products, arithmetic and copies ran while one was open for 2% of the time, Pallas kernels for 23%

profile of v10, /device:TPU:0, one launch (start us, length us, event | category | flops | bytes accessed | tf_op | source)
XLA Modules:
  0.0 31.8 jit_solution(9454754132686538960)
XLA Ops:
  0.0 1.5 %shard_map.46 = (bf16[2,64,512]{2,1,0:T(8,128)(2,1)S(1)}, bf16[2,64,512]{2,1,0:T(8,128)(2,1)S(1)}, bf16[2,64,512]{2,1,0:T(8,128)(2,1)S(1)}, bf16[2,64,512]{2,1,0:T(8,128)(2,1)S(1)}) custom-call(bf16[3,64,4096]{2,1,0:T(8,128)(2,1)} %qkv_ref.3), custom_call_target="tpu_custom_call" | custom-call | tf_op jit(solution)/shard_map/pallas_call | solution.py:219
  1.5 3.4 %collective-permute-start = (bf16[2,64,512]{2,1,0:T(8,128)(2,1)S(1)}, bf16[2,64,512]{2,1,0:T(8,128)(2,1)S(1)}, u32[]{:S(2)}, u32[]{:S(2)}) collective-permute-start(bf16[2,64,512]{2,1,0:T(8,128)(2,1)S(1)} %get-tuple-element.35), channel_id=1, source_target_pairs={{0,4},{1,5},{2,6},{3,7},{4,0},{5,1},{6,2},{7,3},{8,12},{9,13},{10,... | collective-permute-start | bytes 393224 | tf_op jit(solution)/shard_map/ppermute | solution.py:71
  4.9 0.7 %collective-permute-start.1 = (bf16[2,64,512]{2,1,0:T(8,128)(2,1)S(1)}, bf16[2,64,512]{2,1,0:T(8,128)(2,1)S(1)}, u32[]{:S(2)}, u32[]{:S(2)}) collective-permute-start(bf16[2,64,512]{2,1,0:T(8,128)(2,1)S(1)} %get-tuple-element.36), channel_id=1, source_target_pairs={{0,2},{1,3},{2,0},{3,1},{4,6},{5,7},{6,4},{7,5},{8,10},{9,11},{10,... | collective-permute-start | bytes 393224 | tf_op jit(solution)/shard_map/ppermute | solution.py:71
  5.6 0.4 %collective-permute-start.2 = (bf16[2,64,512]{2,1,0:T(8,128)(2,1)S(1)}, bf16[2,64,512]{2,1,0:T(8,128)(2,1)S(1)}, u32[]{:S(2)}, u32[]{:S(2)}) collective-permute-start(bf16[2,64,512]{2,1,0:T(8,128)(2,1)S(1)} %get-tuple-element.37), channel_id=1, source_target_pairs={{0,6},{1,7},{2,4},{3,5},{4,2},{5,3},{6,0},{7,1},{8,14},{9,15},{10,... | collective-permute-start | bytes 393224 | tf_op jit(solution)/shard_map/ppermute | solution.py:71
  6.0 0.9 %shard_map.49 = bf16[8,64,512]{2,1,0:T(8,128)(2,1)} custom-call(bf16[3,64,4096]{2,1,0:T(8,128)(2,1)S(1)} %copy-done), custom_call_target="tpu_custom_call" | custom-call | tf_op jit(solution)/shard_map/pallas_call | solution.py:231
  6.8 0.0 copy-start.3
  6.8 4.3 %all-to-all-start = ((bf16[8,64,512]{2,1,0:T(8,128)(2,1)}), bf16[8,64,512]{2,1,0:T(8,128)(2,1)S(1)}, u32[]{:S(2)}, u32[]{:S(2)}) async-start(bf16[8,64,512]{2,1,0:T(8,128)(2,1)} %shard_map.49), calls=%async_computation | async-start | bytes 1048576 | tf_op jit(solution)/shard_map/all_to_all | solution.py:241
  11.2 0.1 multiply_exponential_fusion
  11.4 0.0 collective-permute-done
  11.4 0.1 collective-permute-done.1
  11.6 0.2 collective-permute-done.2
  11.8 0.3 collective-permute-start.3
  12.2 0.9 %shard_map.47 = (f32[4,264,128]{2,1,0:T(8,128)S(1)}, f32[16,8,512]{2,1,0:T(8,128)S(1)}, f32[16,512]{1,0:T(8,128)S(1)}) custom-call(bf16[4,64,512]{2,1,0:T(8,128)(2,1)S(1)} %pad_maximum_fusion.1.code_ref, f32[16,512]{1,0:T(8,128)S(1)} %get-tuple-element.81.decay_ref.refs_4_.refs_8_, f32[16,8,512]{2,1,0:T(8,128)S(1)} %get-tuple-element.77.tail_ref, ...), custom_call_target="tpu_custom_call" | custom-call | flops 1000 | bytes 1000 | tf_op jit(solution)/shard_map/pallas_call | solution.py:261
  13.1 0.4 %collective-permute-done.3.code_ref = bf16[4,64,512]{2,1,0:T(8,128)(2,1)S(1)} collective-permute-done((bf16[4,64,512]{2,1,0:T(8,128)(2,1)S(1)}, bf16[4,64,512]{2,1,0:T(8,128)(2,1)S(1)}, u32[]{:S(2)}, u32[]{:S(2)}) %collective-permute-start.3) | collective-permute-done | bytes 262176 | tf_op jit(solution)/shard_map/ppermute | solution.py:67
  13.4 0.8 %shard_map.48 = (f32[4,264,128]{2,1,0:T(8,128)S(1)}, f32[16,8,512]{2,1,0:T(8,128)S(1)}, f32[16,512]{1,0:T(8,128)S(1)}) custom-call(bf16[4,64,512]{2,1,0:T(8,128)(2,1)S(1)} %collective-permute-done.3.code_ref, f32[16,512]{1,0:T(8,128)S(1)} %get-tuple-element.81.decay_ref.refs_4_.refs_8_, f32[16,8,512]{2,1,0:T(8,128)S(1)} %get-tuple-element.78.tail_ref, ...), custom_call_target="tpu_custom_call" | custom-call | flops 1000 | bytes 1000 | tf_op jit(solution)/shard_map/pallas_call | solution.py:261
  14.3 3.2 %collective-permute-start.4 = (f32[16,512]{1,0:T(8,128)S(1)}, f32[16,512]{1,0:T(8,128)S(1)}, u32[]{:S(2)}, u32[]{:S(2)}) collective-permute-start(f32[16,512]{1,0:T(8,128)S(1)} %get-tuple-element.40), channel_id=1, source_target_pairs={{0,16},{8,24},{16,0},{24,8},{32,48},{40,56},{48,32},{56,40},{64,80... | collective-permute-start | bytes 98312 | tf_op jit(solution)/shard_map/ppermute | solution.py:75
  17.4 1.1 %collective-permute-start.5 = (f32[16,512]{1,0:T(8,128)S(1)}, f32[16,512]{1,0:T(8,128)S(1)}, u32[]{:S(2)}, u32[]{:S(2)}) collective-permute-start(f32[16,512]{1,0:T(8,128)S(1)} %get-tuple-element.40), channel_id=1, source_target_pairs={{0,24},{8,16},{16,8},{24,0},{32,56},{40,48},{48,40},{56,32},{64,88... | collective-permute-start | bytes 98312 | tf_op jit(solution)/shard_map/ppermute | solution.py:75
  18.6 0.0 collective-permute-start.6
  18.6 1.4 %shard_map.51 = (f32[2,256,128]{2,1,0:T(8,128)S(1)}, f32[2,256,128]{2,1,0:T(8,128)S(1)}) custom-call(f32[4,264,128]{2,1,0:T(8,128)S(1)} %get-tuple-element.41.refs_0_, f32[4,264,128]{2,1,0:T(8,128)S(1)} %get-tuple-element.42.refs_1_, f32[16,8,512]{2,1,0:T(8,128)S(1)} %get-tuple-element.43.refs_2_, f32[16,8,512]{2,1,0:T(8,128)S(1)} %get-tuple-element.44.refs_3_, ...), custom_call_target="tpu_custom_call" | custom-call | flops 40000000 | bytes 4000000 | tf_op jit(solution)/shard_map/pallas_call | solution.py:280
  20.0 1.4 %shard_map.50 = (f32[2,256,128]{2,1,0:T(8,128)S(1)}, f32[2,256,128]{2,1,0:T(8,128)S(1)}) custom-call(f32[4,264,128]{2,1,0:T(8,128)S(1)} %get-tuple-element.41.refs_0_, f32[4,264,128]{2,1,0:T(8,128)S(1)} %get-tuple-element.42.refs_1_, f32[16,8,512]{2,1,0:T(8,128)S(1)} %get-tuple-element.43.refs_2_, f32[16,8,512]{2,1,0:T(8,128)S(1)} %get-tuple-element.44.refs_3_, ...), custom_call_target="tpu_custom_call" | custom-call | flops 40000000 | bytes 4000000 | tf_op jit(solution)/shard_map/pallas_call | solution.py:280
  21.4 1.2 %collective-permute-done.5 = f32[16,512]{1,0:T(8,128)S(1)} collective-permute-done((f32[16,512]{1,0:T(8,128)S(1)}, f32[16,512]{1,0:T(8,128)S(1)}, u32[]{:S(2)}, u32[]{:S(2)}) %collective-permute-start.5) | collective-permute-done | bytes 32800 | tf_op jit(solution)/shard_map/ppermute | solution.py:75
  22.6 0.0 collective-permute-done.6
  22.6 0.0 all-to-all-done
  22.6 0.1 multiply_add_fusion.1
  22.6 4.0 %collective-permute-start.7 = (f32[16,512]{1,0:T(8,128)S(1)}, f32[16,512]{1,0:T(8,128)S(1)}, u32[]{:S(2)}, u32[]{:S(2)}) collective-permute-start(f32[16,512]{1,0:T(8,128)S(1)} %get-tuple-element.63), channel_id=1, source_target_pairs={{0,64},{8,72},{16,80},{24,88},{32,96},{40,104},{48,112},{56,120},{... | collective-permute-start | bytes 98312 | tf_op jit(solution)/shard_map/ppermute | solution.py:75
  26.6 0.7 %collective-permute-start.8 = (f32[16,512]{1,0:T(8,128)S(1)}, f32[16,512]{1,0:T(8,128)S(1)}, u32[]{:S(2)}, u32[]{:S(2)}) collective-permute-start(f32[16,512]{1,0:T(8,128)S(1)} %get-tuple-element.63), channel_id=1, source_target_pairs={{0,96},{8,104},{16,112},{24,120},{32,64},{40,72},{48,80},{56,88},{... | collective-permute-start | bytes 98312 | tf_op jit(solution)/shard_map/ppermute | solution.py:75
  27.3 0.3 collective-permute-start.9
  27.6 0.1 exponential_multiply_fusion
  27.8 2.1 %shard_map.52.refs_9_ = bf16[512,512]{1,0:T(8,128)(2,1)} custom-call(f32[2,256,128]{2,1,0:T(8,128)S(1)} %get-tuple-element.51.refs_0_, f32[2,256,128]{2,1,0:T(8,128)S(1)} %get-tuple-element.52.refs_1_, f32[2,256,128]{2,1,0:T(8,128)S(1)} %get-tuple-element.53.refs_2_, f32[2,256,128]{2,1,0:T(8,128)S(1)} %get-tuple-element.54.refs_3_, ...), custom_call_target="tpu_custom_call" | custom-call | tf_op jit(solution)/shard_map/pallas_call | solution.py:305
  29.9 1.8 %collective-permute-done.8 = f32[16,512]{1,0:T(8,128)S(1)} collective-permute-done((f32[16,512]{1,0:T(8,128)S(1)}, f32[16,512]{1,0:T(8,128)S(1)}, u32[]{:S(2)}, u32[]{:S(2)}) %collective-permute-start.8) | collective-permute-done | bytes 32800 | tf_op jit(solution)/shard_map/ppermute | solution.py:75
  31.7 0.0 collective-permute-done.9
  31.8 0.1 shard_map.53
  (23 shorter events, 0.2 us)
Async XLA Ops:
  0.0 5.9 %copy-start = (bf16[3,64,4096]{2,1,0:T(8,128)(2,1)S(1)}, bf16[3,64,4096]{2,1,0:T(8,128)(2,1)}, u32[]{:S(2)}) copy-start(bf16[3,64,4096]{2,1,0:T(8,128)(2,1)} %qkv_ref.3) | copy-start | bytes 4718596
  1.5 9.9 %collective-permute-start = (bf16[2,64,512]{2,1,0:T(8,128)(2,1)S(1)}, bf16[2,64,512]{2,1,0:T(8,128)(2,1)S(1)}, u32[]{:S(2)}, u32[]{:S(2)}) collective-permute-start(bf16[2,64,512]{2,1,0:T(8,128)(2,1)S(1)} %get-tuple-element.35), channel_id=1, source_target_pairs={{0,4},{1,5},{2,6},{3,7},{4,0},{5,1},{6,2},{7,3},{8,12},{9,13},{10,... | collective-permute-start | bytes 393224 | tf_op jit(solution)/shard_map/ppermute | solution.py:71
  4.9 6.7 %collective-permute-start.1 = (bf16[2,64,512]{2,1,0:T(8,128)(2,1)S(1)}, bf16[2,64,512]{2,1,0:T(8,128)(2,1)S(1)}, u32[]{:S(2)}, u32[]{:S(2)}) collective-permute-start(bf16[2,64,512]{2,1,0:T(8,128)(2,1)S(1)} %get-tuple-element.36), channel_id=1, source_target_pairs={{0,2},{1,3},{2,0},{3,1},{4,6},{5,7},{6,4},{7,5},{8,10},{9,11},{10,... | collective-permute-start | bytes 393224 | tf_op jit(solution)/shard_map/ppermute | solution.py:71
  5.6 5.6 %copy-start.1 = (f32[512,16]{0,1:T(8,128)S(1)}, f32[512,16]{0,1:T(8,128)}, u32[]{:S(2)}) copy-start(f32[512,16]{0,1:T(8,128)} %param.6) | copy-start | bytes 98308
  5.6 5.6 %copy-start.2 = (f32[512,16]{0,1:T(8,128)S(1)}, f32[512,16]{0,1:T(8,128)}, u32[]{:S(2)}) copy-start(f32[512,16]{0,1:T(8,128)} %param.5) | copy-start | bytes 98308
  5.6 6.2 %collective-permute-start.2 = (bf16[2,64,512]{2,1,0:T(8,128)(2,1)S(1)}, bf16[2,64,512]{2,1,0:T(8,128)(2,1)S(1)}, u32[]{:S(2)}, u32[]{:S(2)}) collective-permute-start(bf16[2,64,512]{2,1,0:T(8,128)(2,1)S(1)} %get-tuple-element.37), channel_id=1, source_target_pairs={{0,6},{1,7},{2,4},{3,5},{4,2},{5,3},{6,0},{7,1},{8,14},{9,15},{10,... | collective-permute-start | bytes 393224 | tf_op jit(solution)/shard_map/ppermute | solution.py:71
  6.8 5.3 %copy-start.3 = (f32[512]{0:T(512)S(1)}, f32[512]{0:T(512)}, u32[]{:S(2)}) copy-start(f32[512]{0:T(512)} %param.7) | copy-start | bytes 6148
  6.8 15.8 %all-to-all-start = ((bf16[8,64,512]{2,1,0:T(8,128)(2,1)}), bf16[8,64,512]{2,1,0:T(8,128)(2,1)S(1)}, u32[]{:S(2)}, u32[]{:S(2)}) async-start(bf16[8,64,512]{2,1,0:T(8,128)(2,1)} %shard_map.49), calls=%async_computation | async-start | bytes 1048576 | tf_op jit(solution)/shard_map/all_to_all | solution.py:241
  11.8 1.6 %collective-permute-start.3 = (bf16[4,64,512]{2,1,0:T(8,128)(2,1)S(1)}, bf16[4,64,512]{2,1,0:T(8,128)(2,1)S(1)}, u32[]{:S(2)}, u32[]{:S(2)}) collective-permute-start(bf16[4,64,512]{2,1,0:T(8,128)(2,1)S(1)} %pad_maximum_fusion), channel_id=1, source_target_pairs={{0,1},{1,0},{2,3},{3,2},{4,5},{5,4},{6,7},{7,6},{8,9},{9,8},{10,11... | collective-permute-start | bytes 786440 | tf_op jit(solution)/shard_map/ppermute | solution.py:67
  14.3 7.1 %collective-permute-start.4 = (f32[16,512]{1,0:T(8,128)S(1)}, f32[16,512]{1,0:T(8,128)S(1)}, u32[]{:S(2)}, u32[]{:S(2)}) collective-permute-start(f32[16,512]{1,0:T(8,128)S(1)} %get-tuple-element.40), channel_id=1, source_target_pairs={{0,16},{8,24},{16,0},{24,8},{32,48},{40,56},{48,32},{56,40},{64,80... | collective-permute-start | bytes 98312 | tf_op jit(solution)/shard_map/ppermute | solution.py:75
  17.4 5.1 %collective-permute-start.5 = (f32[16,512]{1,0:T(8,128)S(1)}, f32[16,512]{1,0:T(8,128)S(1)}, u32[]{:S(2)}, u32[]{:S(2)}) collective-permute-start(f32[16,512]{1,0:T(8,128)S(1)} %get-tuple-element.40), channel_id=1, source_target_pairs={{0,24},{8,16},{16,8},{24,0},{32,56},{40,48},{48,40},{56,32},{64,88... | collective-permute-start | bytes 98312 | tf_op jit(solution)/shard_map/ppermute | solution.py:75
  18.6 4.0 %collective-permute-start.6 = (f32[16,512]{1,0:T(8,128)S(1)}, f32[16,512]{1,0:T(8,128)S(1)}, u32[]{:S(2)}, u32[]{:S(2)}) collective-permute-start(f32[16,512]{1,0:T(8,128)S(1)} %get-tuple-element.40), channel_id=1, source_target_pairs={{0,8},{8,0},{16,24},{24,16},{32,40},{40,32},{48,56},{56,48},{64,72... | collective-permute-start | bytes 98312 | tf_op jit(solution)/shard_map/ppermute | solution.py:75
  22.6 7.2 %collective-permute-start.7 = (f32[16,512]{1,0:T(8,128)S(1)}, f32[16,512]{1,0:T(8,128)S(1)}, u32[]{:S(2)}, u32[]{:S(2)}) collective-permute-start(f32[16,512]{1,0:T(8,128)S(1)} %get-tuple-element.63), channel_id=1, source_target_pairs={{0,64},{8,72},{16,80},{24,88},{32,96},{40,104},{48,112},{56,120},{... | collective-permute-start | bytes 98312 | tf_op jit(solution)/shard_map/ppermute | solution.py:75
  26.6 5.1 %collective-permute-start.8 = (f32[16,512]{1,0:T(8,128)S(1)}, f32[16,512]{1,0:T(8,128)S(1)}, u32[]{:S(2)}, u32[]{:S(2)}) collective-permute-start(f32[16,512]{1,0:T(8,128)S(1)} %get-tuple-element.63), channel_id=1, source_target_pairs={{0,96},{8,104},{16,112},{24,120},{32,64},{40,72},{48,80},{56,88},{... | collective-permute-start | bytes 98312 | tf_op jit(solution)/shard_map/ppermute | solution.py:75
  27.3 4.4 %collective-permute-start.9 = (f32[16,512]{1,0:T(8,128)S(1)}, f32[16,512]{1,0:T(8,128)S(1)}, u32[]{:S(2)}, u32[]{:S(2)}) collective-permute-start(f32[16,512]{1,0:T(8,128)S(1)} %get-tuple-element.63), channel_id=1, source_target_pairs={{0,32},{8,40},{16,48},{24,56},{32,0},{40,8},{48,16},{56,24},{64,96... | collective-permute-start | bytes 98312 | tf_op jit(solution)/shard_map/ppermute | solution.py:75

commit v11 on v10

--- a/solution.py
+++ b/solution.py
@@ -14,7 +14,7 @@
 SCALE = 1024.0
 OPEN_VMEM = 52 * 1024 * 1024
 CHIP_ORDER = (2, 1, 3)
-COL_ORDER = (2, 3, 1)
+COL_ORDER = (3, 2, 1)
 ROW_ORDER = (2, 3, 1)
 VMEM = pl.BlockSpec(memory_space=pltpu.VMEM)
 PARAMS = pltpu.CompilerParams(vmem_limit_bytes=32 * 1024 * 1024)

time: 32.1 us -> 32.1 us (level)
  no operation moved by 1% of the time
where the time goes in v11:
time: 32.1 us; the launch traced here: 31.9 us
  starting transfers between devices  18.2 us (57%)
  Pallas kernels  9.03 us (28%)
  waiting for transfers between devices  3.84 us (12%)
  other arithmetic  0.53 us (2%)
    ppermute x6, starting transfers between devices, across_blocks(): lax.ppermute(value, 'ctx', [(i, i ^ bits) for i in range(lax.axis_size('c...  9.15 us
    ppermute x3, starting transfers between devices, across_chips(): lax.ppermute(value, 'tp', [(i, i ^ 2 * k) for i in range(lax.axis_size('t...  4.41 us
    all_to_all x1, starting transfers between devices, per_device(): query = lax.all_to_all(query, 'tp', 0, 0).reshape(tokens, channels)  4.32 us
    ppermute x6, waiting for transfers between devices, across_blocks(): lax.ppermute(value, 'ctx', [(i, i ^ bits) for i in range(lax.axis_size('c...  3.15 us
    pallas_call x2, Pallas kernels, per_device(): pl.pallas_call(functools.partial(local_kernel, modes, begin), in_specs=[V...  2.79 us
    pallas_call x2, Pallas kernels, final(): pl.pallas_call(functools.partial(final_kernel, modes, early), in_specs=[V...  2.17 us
    pallas_call x2, Pallas kernels, states(): pl.pallas_call(functools.partial(state_kernel, modes), in_specs=[VMEM] *...  1.7 us
    pallas_call x1, Pallas kernels, per_device(): pl.pallas_call(open_kernel, in_specs=[pl.BlockSpec(memory_space=pl.ANY)],...  1.52 us
  transfers between devices with their start and end apart: 11, of which 5 were waited for; matrix products, arithmetic and copies ran while one was open for 2% of the time, Pallas kernels for 23%

profile of v11, /device:TPU:0, one launch (start us, length us, event | category | flops | bytes accessed | tf_op | source)
XLA Modules:
  0.0 31.9 jit_solution(8070974861483133668)
XLA Ops:
  0.0 1.5 %shard_map.46 = (bf16[2,64,512]{2,1,0:T(8,128)(2,1)S(1)}, bf16[2,64,512]{2,1,0:T(8,128)(2,1)S(1)}, bf16[2,64,512]{2,1,0:T(8,128)(2,1)S(1)}, bf16[2,64,512]{2,1,0:T(8,128)(2,1)S(1)}) custom-call(bf16[3,64,4096]{2,1,0:T(8,128)(2,1)} %qkv_ref.3), custom_call_target="tpu_custom_call" | custom-call | tf_op jit(solution)/shard_map/pallas_call | solution.py:219
  1.5 3.4 %collective-permute-start = (bf16[2,64,512]{2,1,0:T(8,128)(2,1)S(1)}, bf16[2,64,512]{2,1,0:T(8,128)(2,1)S(1)}, u32[]{:S(2)}, u32[]{:S(2)}) collective-permute-start(bf16[2,64,512]{2,1,0:T(8,128)(2,1)S(1)} %get-tuple-element.35), channel_id=1, source_target_pairs={{0,4},{1,5},{2,6},{3,7},{4,0},{5,1},{6,2},{7,3},{8,12},{9,13},{10,... | collective-permute-start | bytes 393224 | tf_op jit(solution)/shard_map/ppermute | solution.py:71
  4.9 0.7 %collective-permute-start.1 = (bf16[2,64,512]{2,1,0:T(8,128)(2,1)S(1)}, bf16[2,64,512]{2,1,0:T(8,128)(2,1)S(1)}, u32[]{:S(2)}, u32[]{:S(2)}) collective-permute-start(bf16[2,64,512]{2,1,0:T(8,128)(2,1)S(1)} %get-tuple-element.36), channel_id=1, source_target_pairs={{0,2},{1,3},{2,0},{3,1},{4,6},{5,7},{6,4},{7,5},{8,10},{9,11},{10,... | collective-permute-start | bytes 393224 | tf_op jit(solution)/shard_map/ppermute | solution.py:71
  5.6 0.4 %collective-permute-start.2 = (bf16[2,64,512]{2,1,0:T(8,128)(2,1)S(1)}, bf16[2,64,512]{2,1,0:T(8,128)(2,1)S(1)}, u32[]{:S(2)}, u32[]{:S(2)}) collective-permute-start(bf16[2,64,512]{2,1,0:T(8,128)(2,1)S(1)} %get-tuple-element.37), channel_id=1, source_target_pairs={{0,6},{1,7},{2,4},{3,5},{4,2},{5,3},{6,0},{7,1},{8,14},{9,15},{10,... | collective-permute-start | bytes 393224 | tf_op jit(solution)/shard_map/ppermute | solution.py:71
  6.0 0.9 %shard_map.49 = bf16[8,64,512]{2,1,0:T(8,128)(2,1)} custom-call(bf16[3,64,4096]{2,1,0:T(8,128)(2,1)S(1)} %copy-done), custom_call_target="tpu_custom_call" | custom-call | tf_op jit(solution)/shard_map/pallas_call | solution.py:231
  6.8 0.0 copy-start.3
  6.8 4.3 %all-to-all-start = ((bf16[8,64,512]{2,1,0:T(8,128)(2,1)}), bf16[8,64,512]{2,1,0:T(8,128)(2,1)S(1)}, u32[]{:S(2)}, u32[]{:S(2)}) async-start(bf16[8,64,512]{2,1,0:T(8,128)(2,1)} %shard_map.49), calls=%async_computation | async-start | bytes 1048576 | tf_op jit(solution)/shard_map/all_to_all | solution.py:241
  11.2 0.1 multiply_exponential_fusion
  11.4 0.0 collective-permute-done
  11.4 0.1 collective-permute-done.1
  11.6 0.2 collective-permute-done.2
  11.8 0.3 collective-permute-start.3
  12.2 0.9 %shard_map.47 = (f32[4,264,128]{2,1,0:T(8,128)S(1)}, f32[16,8,512]{2,1,0:T(8,128)S(1)}, f32[16,512]{1,0:T(8,128)S(1)}) custom-call(bf16[4,64,512]{2,1,0:T(8,128)(2,1)S(1)} %pad_maximum_fusion.1.code_ref, f32[16,512]{1,0:T(8,128)S(1)} %get-tuple-element.81.decay_ref.refs_4_.refs_8_, f32[16,8,512]{2,1,0:T(8,128)S(1)} %get-tuple-element.77.tail_ref, ...), custom_call_target="tpu_custom_call" | custom-call | flops 1000 | bytes 1000 | tf_op jit(solution)/shard_map/pallas_call | solution.py:261
  13.1 0.4 %collective-permute-done.3.code_ref = bf16[4,64,512]{2,1,0:T(8,128)(2,1)S(1)} collective-permute-done((bf16[4,64,512]{2,1,0:T(8,128)(2,1)S(1)}, bf16[4,64,512]{2,1,0:T(8,128)(2,1)S(1)}, u32[]{:S(2)}, u32[]{:S(2)}) %collective-permute-start.3) | collective-permute-done | bytes 262176 | tf_op jit(solution)/shard_map/ppermute | solution.py:67
  13.4 0.8 %shard_map.48 = (f32[4,264,128]{2,1,0:T(8,128)S(1)}, f32[16,8,512]{2,1,0:T(8,128)S(1)}, f32[16,512]{1,0:T(8,128)S(1)}) custom-call(bf16[4,64,512]{2,1,0:T(8,128)(2,1)S(1)} %collective-permute-done.3.code_ref, f32[16,512]{1,0:T(8,128)S(1)} %get-tuple-element.81.decay_ref.refs_4_.refs_8_, f32[16,8,512]{2,1,0:T(8,128)S(1)} %get-tuple-element.78.tail_ref, ...), custom_call_target="tpu_custom_call" | custom-call | flops 1000 | bytes 1000 | tf_op jit(solution)/shard_map/pallas_call | solution.py:261
  14.3 2.9 %collective-permute-start.4 = (f32[16,512]{1,0:T(8,128)S(1)}, f32[16,512]{1,0:T(8,128)S(1)}, u32[]{:S(2)}, u32[]{:S(2)}) collective-permute-start(f32[16,512]{1,0:T(8,128)S(1)} %get-tuple-element.40), channel_id=1, source_target_pairs={{0,24},{8,16},{16,8},{24,0},{32,56},{40,48},{48,40},{56,32},{64,88... | collective-permute-start | bytes 98312 | tf_op jit(solution)/shard_map/ppermute | solution.py:75
  17.2 0.8 %collective-permute-start.5 = (f32[16,512]{1,0:T(8,128)S(1)}, f32[16,512]{1,0:T(8,128)S(1)}, u32[]{:S(2)}, u32[]{:S(2)}) collective-permute-start(f32[16,512]{1,0:T(8,128)S(1)} %get-tuple-element.40), channel_id=1, source_target_pairs={{0,16},{8,24},{16,0},{24,8},{32,48},{40,56},{48,32},{56,40},{64,80... | collective-permute-start | bytes 98312 | tf_op jit(solution)/shard_map/ppermute | solution.py:75
  18.0 0.5 %collective-permute-start.6 = (f32[16,512]{1,0:T(8,128)S(1)}, f32[16,512]{1,0:T(8,128)S(1)}, u32[]{:S(2)}, u32[]{:S(2)}) collective-permute-start(f32[16,512]{1,0:T(8,128)S(1)} %get-tuple-element.40), channel_id=1, source_target_pairs={{0,8},{8,0},{16,24},{24,16},{32,40},{40,32},{48,56},{56,48},{64,72... | collective-permute-start | bytes 98312 | tf_op jit(solution)/shard_map/ppermute | solution.py:75
  18.5 1.4 %shard_map.51 = (f32[2,256,128]{2,1,0:T(8,128)S(1)}, f32[2,256,128]{2,1,0:T(8,128)S(1)}) custom-call(f32[4,264,128]{2,1,0:T(8,128)S(1)} %get-tuple-element.41.refs_0_, f32[4,264,128]{2,1,0:T(8,128)S(1)} %get-tuple-element.42.refs_1_, f32[16,8,512]{2,1,0:T(8,128)S(1)} %get-tuple-element.43.refs_2_, f32[16,8,512]{2,1,0:T(8,128)S(1)} %get-tuple-element.44.refs_3_, ...), custom_call_target="tpu_custom_call" | custom-call | flops 40000000 | bytes 4000000 | tf_op jit(solution)/shard_map/pallas_call | solution.py:280
  19.9 1.4 %shard_map.50 = (f32[2,256,128]{2,1,0:T(8,128)S(1)}, f32[2,256,128]{2,1,0:T(8,128)S(1)}) custom-call(f32[4,264,128]{2,1,0:T(8,128)S(1)} %get-tuple-element.41.refs_0_, f32[4,264,128]{2,1,0:T(8,128)S(1)} %get-tuple-element.42.refs_1_, f32[16,8,512]{2,1,0:T(8,128)S(1)} %get-tuple-element.43.refs_2_, f32[16,8,512]{2,1,0:T(8,128)S(1)} %get-tuple-element.44.refs_3_, ...), custom_call_target="tpu_custom_call" | custom-call | flops 40000000 | bytes 4000000 | tf_op jit(solution)/shard_map/pallas_call | solution.py:280
  21.3 1.3 %collective-permute-done.5 = f32[16,512]{1,0:T(8,128)S(1)} collective-permute-done((f32[16,512]{1,0:T(8,128)S(1)}, f32[16,512]{1,0:T(8,128)S(1)}, u32[]{:S(2)}, u32[]{:S(2)}) %collective-permute-start.5) | collective-permute-done | bytes 32800 | tf_op jit(solution)/shard_map/ppermute | solution.py:75
  22.6 0.0 collective-permute-done.6
  22.6 0.1 multiply_add_fusion.1
  22.7 4.0 %collective-permute-start.7 = (f32[16,512]{1,0:T(8,128)S(1)}, f32[16,512]{1,0:T(8,128)S(1)}, u32[]{:S(2)}, u32[]{:S(2)}) collective-permute-start(f32[16,512]{1,0:T(8,128)S(1)} %get-tuple-element.63), channel_id=1, source_target_pairs={{0,64},{8,72},{16,80},{24,88},{32,96},{40,104},{48,112},{56,120},{... | collective-permute-start | bytes 98312 | tf_op jit(solution)/shard_map/ppermute | solution.py:75
  26.6 0.7 %collective-permute-start.8 = (f32[16,512]{1,0:T(8,128)S(1)}, f32[16,512]{1,0:T(8,128)S(1)}, u32[]{:S(2)}, u32[]{:S(2)}) collective-permute-start(f32[16,512]{1,0:T(8,128)S(1)} %get-tuple-element.63), channel_id=1, source_target_pairs={{0,96},{8,104},{16,112},{24,120},{32,64},{40,72},{48,80},{56,88},{... | collective-permute-start | bytes 98312 | tf_op jit(solution)/shard_map/ppermute | solution.py:75
  27.3 0.3 collective-permute-start.9
  27.6 0.1 exponential_multiply_fusion
  27.8 2.1 %shard_map.52.refs_9_ = bf16[512,512]{1,0:T(8,128)(2,1)} custom-call(f32[2,256,128]{2,1,0:T(8,128)S(1)} %get-tuple-element.51.refs_0_, f32[2,256,128]{2,1,0:T(8,128)S(1)} %get-tuple-element.52.refs_1_, f32[2,256,128]{2,1,0:T(8,128)S(1)} %get-tuple-element.53.refs_2_, f32[2,256,128]{2,1,0:T(8,128)S(1)} %get-tuple-element.54.refs_3_, ...), custom_call_target="tpu_custom_call" | custom-call | tf_op jit(solution)/shard_map/pallas_call | solution.py:305
  29.9 0.0 collective-permute-done.7
  29.9 1.8 %collective-permute-done.8 = f32[16,512]{1,0:T(8,128)S(1)} collective-permute-done((f32[16,512]{1,0:T(8,128)S(1)}, f32[16,512]{1,0:T(8,128)S(1)}, u32[]{:S(2)}, u32[]{:S(2)}) %collective-permute-start.8) | collective-permute-done | bytes 32800 | tf_op jit(solution)/shard_map/ppermute | solution.py:75
  31.7 0.0 collective-permute-done.9
  31.8 0.1 shard_map.53
  (23 shorter events, 0.2 us)
Async XLA Ops:
  0.0 5.9 %copy-start = (bf16[3,64,4096]{2,1,0:T(8,128)(2,1)S(1)}, bf16[3,64,4096]{2,1,0:T(8,128)(2,1)}, u32[]{:S(2)}) copy-start(bf16[3,64,4096]{2,1,0:T(8,128)(2,1)} %qkv_ref.3) | copy-start | bytes 4718596
  1.5 9.9 %collective-permute-start = (bf16[2,64,512]{2,1,0:T(8,128)(2,1)S(1)}, bf16[2,64,512]{2,1,0:T(8,128)(2,1)S(1)}, u32[]{:S(2)}, u32[]{:S(2)}) collective-permute-start(bf16[2,64,512]{2,1,0:T(8,128)(2,1)S(1)} %get-tuple-element.35), channel_id=1, source_target_pairs={{0,4},{1,5},{2,6},{3,7},{4,0},{5,1},{6,2},{7,3},{8,12},{9,13},{10,... | collective-permute-start | bytes 393224 | tf_op jit(solution)/shard_map/ppermute | solution.py:71
  4.9 6.7 %collective-permute-start.1 = (bf16[2,64,512]{2,1,0:T(8,128)(2,1)S(1)}, bf16[2,64,512]{2,1,0:T(8,128)(2,1)S(1)}, u32[]{:S(2)}, u32[]{:S(2)}) collective-permute-start(bf16[2,64,512]{2,1,0:T(8,128)(2,1)S(1)} %get-tuple-element.36), channel_id=1, source_target_pairs={{0,2},{1,3},{2,0},{3,1},{4,6},{5,7},{6,4},{7,5},{8,10},{9,11},{10,... | collective-permute-start | bytes 393224 | tf_op jit(solution)/shard_map/ppermute | solution.py:71
  5.6 5.6 %copy-start.1 = (f32[512,16]{0,1:T(8,128)S(1)}, f32[512,16]{0,1:T(8,128)}, u32[]{:S(2)}) copy-start(f32[512,16]{0,1:T(8,128)} %param.6) | copy-start | bytes 98308
  5.6 5.6 %copy-start.2 = (f32[512,16]{0,1:T(8,128)S(1)}, f32[512,16]{0,1:T(8,128)}, u32[]{:S(2)}) copy-start(f32[512,16]{0,1:T(8,128)} %param.5) | copy-start | bytes 98308
  5.6 6.2 %collective-permute-start.2 = (bf16[2,64,512]{2,1,0:T(8,128)(2,1)S(1)}, bf16[2,64,512]{2,1,0:T(8,128)(2,1)S(1)}, u32[]{:S(2)}, u32[]{:S(2)}) collective-permute-start(bf16[2,64,512]{2,1,0:T(8,128)(2,1)S(1)} %get-tuple-element.37), channel_id=1, source_target_pairs={{0,6},{1,7},{2,4},{3,5},{4,2},{5,3},{6,0},{7,1},{8,14},{9,15},{10,... | collective-permute-start | bytes 393224 | tf_op jit(solution)/shard_map/ppermute | solution.py:71
  6.8 5.3 %copy-start.3 = (f32[512]{0:T(512)S(1)}, f32[512]{0:T(512)}, u32[]{:S(2)}) copy-start(f32[512]{0:T(512)} %param.7) | copy-start | bytes 6148
  6.8 15.8 %all-to-all-start = ((bf16[8,64,512]{2,1,0:T(8,128)(2,1)}), bf16[8,64,512]{2,1,0:T(8,128)(2,1)S(1)}, u32[]{:S(2)}, u32[]{:S(2)}) async-start(bf16[8,64,512]{2,1,0:T(8,128)(2,1)} %shard_map.49), calls=%async_computation | async-start | bytes 1048576 | tf_op jit(solution)/shard_map/all_to_all | solution.py:241
  11.8 1.6 %collective-permute-start.3 = (bf16[4,64,512]{2,1,0:T(8,128)(2,1)S(1)}, bf16[4,64,512]{2,1,0:T(8,128)(2,1)S(1)}, u32[]{:S(2)}, u32[]{:S(2)}) collective-permute-start(bf16[4,64,512]{2,1,0:T(8,128)(2,1)S(1)} %pad_maximum_fusion), channel_id=1, source_target_pairs={{0,1},{1,0},{2,3},{3,2},{4,5},{5,4},{6,7},{7,6},{8,9},{9,8},{10,11... | collective-permute-start | bytes 786440 | tf_op jit(solution)/shard_map/ppermute | solution.py:67
  14.3 7.0 %collective-permute-start.4 = (f32[16,512]{1,0:T(8,128)S(1)}, f32[16,512]{1,0:T(8,128)S(1)}, u32[]{:S(2)}, u32[]{:S(2)}) collective-permute-start(f32[16,512]{1,0:T(8,128)S(1)} %get-tuple-element.40), channel_id=1, source_target_pairs={{0,24},{8,16},{16,8},{24,0},{32,56},{40,48},{48,40},{56,32},{64,88... | collective-permute-start | bytes 98312 | tf_op jit(solution)/shard_map/ppermute | solution.py:75
  17.2 5.4 %collective-permute-start.5 = (f32[16,512]{1,0:T(8,128)S(1)}, f32[16,512]{1,0:T(8,128)S(1)}, u32[]{:S(2)}, u32[]{:S(2)}) collective-permute-start(f32[16,512]{1,0:T(8,128)S(1)} %get-tuple-element.40), channel_id=1, source_target_pairs={{0,16},{8,24},{16,0},{24,8},{32,48},{40,56},{48,32},{56,40},{64,80... | collective-permute-start | bytes 98312 | tf_op jit(solution)/shard_map/ppermute | solution.py:75
  18.0 4.6 %collective-permute-start.6 = (f32[16,512]{1,0:T(8,128)S(1)}, f32[16,512]{1,0:T(8,128)S(1)}, u32[]{:S(2)}, u32[]{:S(2)}) collective-permute-start(f32[16,512]{1,0:T(8,128)S(1)} %get-tuple-element.40), channel_id=1, source_target_pairs={{0,8},{8,0},{16,24},{24,16},{32,40},{40,32},{48,56},{56,48},{64,72... | collective-permute-start | bytes 98312 | tf_op jit(solution)/shard_map/ppermute | solution.py:75
  22.7 7.2 %collective-permute-start.7 = (f32[16,512]{1,0:T(8,128)S(1)}, f32[16,512]{1,0:T(8,128)S(1)}, u32[]{:S(2)}, u32[]{:S(2)}) collective-permute-start(f32[16,512]{1,0:T(8,128)S(1)} %get-tuple-element.63), channel_id=1, source_target_pairs={{0,64},{8,72},{16,80},{24,88},{32,96},{40,104},{48,112},{56,120},{... | collective-permute-start | bytes 98312 | tf_op jit(solution)/shard_map/ppermute | solution.py:75
  26.6 5.1 %collective-permute-start.8 = (f32[16,512]{1,0:T(8,128)S(1)}, f32[16,512]{1,0:T(8,128)S(1)}, u32[]{:S(2)}, u32[]{:S(2)}) collective-permute-start(f32[16,512]{1,0:T(8,128)S(1)} %get-tuple-element.63), channel_id=1, source_target_pairs={{0,96},{8,104},{16,112},{24,120},{32,64},{40,72},{48,80},{56,88},{... | collective-permute-start | bytes 98312 | tf_op jit(solution)/shard_map/ppermute | solution.py:75
  27.3 4.4 %collective-permute-start.9 = (f32[16,512]{1,0:T(8,128)S(1)}, f32[16,512]{1,0:T(8,128)S(1)}, u32[]{:S(2)}, u32[]{:S(2)}) collective-permute-start(f32[16,512]{1,0:T(8,128)S(1)} %get-tuple-element.63), channel_id=1, source_target_pairs={{0,32},{8,40},{16,48},{24,56},{32,0},{40,8},{48,16},{56,24},{64,96... | collective-permute-start | bytes 98312 | tf_op jit(solution)/shard_map/ppermute | solution.py:75
